TPU v7x, 32 devices: a whole 2x2x4 slice. The times are simulated.
32 devices in a mesh: dp: 8 (over y, x, core), tensor: 4 (over z).
Axes of the slice: x: 2, y: 2, z: 4, core: 2. Of those that a mesh axis runs over, the one named last changes fastest.
Arguments:
- stream_in: bfloat16 [16384, 768], P(('dp', 'tensor')), may hold values from -6 to 6
- patch_size: int32 [16], P('dp'), may hold values from 8 to 10, as said below
- norm_gain: bfloat16 [2, 2, 768], replicated, may hold values from 0.25 to 1.75
- norm_bias: bfloat16 [2, 2, 768], replicated, may hold values from -2 to 2
- input_weight: bfloat16 [2, 3, 768, 768], P(None, None, None, 'tensor'), may hold values from -0.21875 to 0.21875
- input_bias: bfloat16 [2, 2, 768], P(None, None, 'tensor'), may hold values from -3 to 3
- output_weight: bfloat16 [2, 768, 768], P(None, 'tensor'), may hold values from -0.625 to 0.625
- output_bias: bfloat16 [2, 768], replicated, may hold values from -3 to 3
- up_weight: bfloat16 [2, 768, 3072], P(None, None, 'tensor'), may hold values from -0.21875 to 0.21875
- up_bias: bfloat16 [2, 3072], P(None, 'tensor'), may hold values from -3 to 3
- down_weight: bfloat16 [2, 3072, 768], P(None, 'tensor'), may hold values from -0.109375 to 0.109375
- down_bias: bfloat16 [2, 768], replicated, may hold values from -3 to 3
- cotangent: bfloat16 [16384, 768], P(('dp', 'tensor')), may hold values from -6 to 6
Outputs:
- layer_out: bfloat16 [16384, 768], P(('dp', 'tensor'))
- grad_in: float32 [16384, 768], P(('dp', 'tensor'))
- norm_gain_grad: float32 [2, 2, 768], replicated
- norm_bias_grad: float32 [2, 2, 768], replicated
- input_weight_grad: float32 [2, 3, 768, 768], P(None, None, None, 'tensor')
- input_bias_grad: float32 [2, 2, 768], P(None, None, 'tensor')
- output_weight_grad: float32 [2, 768, 768], P(None, 'tensor')
- output_bias_grad: float32 [2, 768], replicated
- up_weight_grad: float32 [2, 768, 3072], P(None, None, 'tensor')
- up_bias_grad: float32 [2, 3072], P(None, 'tensor')
- down_weight_grad: float32 [2, 3072, 768], P(None, 'tensor')
- down_bias_grad: float32 [2, 768], replicated
Inputs may be any that keep to these rules, and one draw needn't show every extreme that they name: `patch_size`: every entry is 8 or 10, and both occur in every draw.
All inputs are finite; a program needn't handle non-finite values.
Results may differ from a plain program's by a relative error of at most 0.015.
Values may be sent and summed in bfloat16 or wider, within the bound.
No kernel may reach another device: no remote copies, remote signals or barrier semaphores. Data moves between devices by JAX's collectives and lax.ppermute only.
A program may use at most 192 MiB of HBM per device.

v0:
```python
import jax
import jax.numpy as jnp
from jax import lax
from jax.sharding import PartitionSpec as P

HD = 64
ROWS = 1024
IMAGE = 240


epsilon = 1e-06
masked_score = -1e30


def normalize(values, gain_row, bias_row):
    average = jnp.mean(values, axis=-1, keepdims=True)
    centred = values - average
    variance = jnp.mean(centred * centred, axis=-1, keepdims=True)
    return centred * lax.rsqrt(variance + epsilon) * gain_row + bias_row


def gelu_exact(values):
    return jax.nn.gelu(values, approximate=False)


def masked_scores(queries, keys_in, valid_count, head_size):
    scores = jnp.einsum(
        "qhe,khe->hqk", queries, keys_in, preferred_element_type=jnp.float32
    ) * head_size ** (-0.5)
    key_index = jnp.arange(scores.shape[-1], dtype=jnp.int32)
    return jnp.where(key_index[None, None, :] < valid_count, scores, masked_score)


def attend_forward(queries, keys_in, values_in, valid_count, head_size):
    scores = masked_scores(queries, keys_in, valid_count, head_size)
    row_top = jnp.max(scores, axis=-1, keepdims=True)
    weights = jnp.exp(scores - row_top)
    row_total = jnp.sum(weights, axis=-1, keepdims=True)
    softmax_probs = (weights / row_total).astype(jnp.bfloat16)
    mixed_heads = jnp.einsum(
        "hqk,khe->qhe", softmax_probs, values_in, preferred_element_type=jnp.float32
    )
    return (mixed_heads, row_top + jnp.log(row_total))


def attend_backward(queries, keys_in, values_in, valid_count, log_total, grad_mixed, head_size):
    score_scale = head_size ** (-0.5)
    scores = masked_scores(queries, keys_in, valid_count, head_size)
    softmax_probs = jnp.exp(scores - log_total)
    grad_values = jnp.einsum(
        "hqk,qhe->khe",
        softmax_probs.astype(jnp.bfloat16),
        grad_mixed,
        preferred_element_type=jnp.float32,
    )
    grad_probs = jnp.einsum(
        "qhe,khe->hqk", grad_mixed, values_in, preferred_element_type=jnp.float32
    )
    row_delta = jnp.sum(softmax_probs * grad_probs, axis=-1, keepdims=True)
    grad_scores = (softmax_probs * (grad_probs - row_delta)).astype(jnp.bfloat16)
    grad_queries = (
        jnp.einsum("hqk,khe->qhe", grad_scores, keys_in, preferred_element_type=jnp.float32)
        * score_scale
    )
    grad_keys = (
        jnp.einsum("hqk,qhe->khe", grad_scores, queries, preferred_element_type=jnp.float32)
        * score_scale
    )
    return (grad_queries, grad_keys, grad_values)


def local(
    stream_in,
    patch_size,
    norm_gain,
    norm_bias,
    input_weight,
    input_bias,
    output_weight,
    output_bias,
    up_weight,
    up_bias,
    down_weight,
    down_bias,
    cotangent,
):
    shard_rows = stream_in.shape[0]
    micro_count = patch_size.shape[0]
    head_size = HD
    local_width = input_weight.shape[-1]
    local_heads = local_width // head_size
    layer_count = input_weight.shape[0]
    rows_all = shard_rows * lax.axis_size("tensor")
    grid_side = IMAGE // patch_size
    valid_all = grid_side * grid_side
    row_index = lax.axis_index("tensor") * shard_rows + jnp.arange(shard_rows, dtype=jnp.int32)
    row_owner = row_index // ROWS
    row_place = row_index % ROWS
    buffer_ids = jnp.arange(micro_count, dtype=jnp.int32)
    row_limit = jnp.sum(
        jnp.where(row_owner[:, None] == buffer_ids[None, :], valid_all[None, :], 0), axis=1
    )
    row_mask = (row_place < row_limit).astype(jnp.float32)[:, None]
    gains = norm_gain.astype(jnp.float32)
    shifts = norm_bias.astype(jnp.float32)

    def head_split(array):
        return array.reshape(micro_count, ROWS, local_heads, head_size)

    stream = stream_in.astype(jnp.float32)
    saved = []
    for layer_idx in range(layer_count):
        layer_input = stream
        normed = normalize(stream, gains[layer_idx, 0], shifts[layer_idx, 0]).astype(jnp.bfloat16)
        normed_all = lax.all_gather(normed, "tensor", axis=0, tiled=True)
        projected = jnp.einsum(
            "rd,sde->sre", normed_all, input_weight[layer_idx], preferred_element_type=jnp.float32
        )
        queries = (projected[0] + input_bias[layer_idx, 0].astype(jnp.float32)).astype(jnp.bfloat16)
        keys_all = projected[1].astype(jnp.bfloat16)
        values_all = (projected[2] + input_bias[layer_idx, 1].astype(jnp.float32)).astype(
            jnp.bfloat16
        )

        def forward_buffer(group):
            return attend_forward(group[0], group[1], group[2], group[3], head_size)

        mixed_heads, log_total = lax.map(
            forward_buffer,
            (head_split(queries), head_split(keys_all), head_split(values_all), valid_all),
        )
        mixed_rows = mixed_heads.reshape(rows_all, local_width).astype(jnp.bfloat16)
        weight_out = output_weight[layer_idx]
        heads_total = lax.psum_scatter(
            jnp.dot(mixed_rows, weight_out, preferred_element_type=jnp.float32).astype(
                jnp.bfloat16
            ),
            "tensor",
            scatter_dimension=0,
            tiled=True,
        ).astype(jnp.float32)
        middle = stream + (heads_total + output_bias[layer_idx].astype(jnp.float32))
        normed_two = normalize(middle, gains[layer_idx, 1], shifts[layer_idx, 1]).astype(
            jnp.bfloat16
        )
        normed_two_all = lax.all_gather(normed_two, "tensor", axis=0, tiled=True)
        hidden_pre = jnp.dot(
            normed_two_all, up_weight[layer_idx], preferred_element_type=jnp.float32
        ) + up_bias[layer_idx].astype(jnp.float32)
        activated = gelu_exact(hidden_pre).astype(jnp.bfloat16)
        weight_down = down_weight[layer_idx]
        units_total = lax.psum_scatter(
            jnp.dot(activated, weight_down, preferred_element_type=jnp.float32).astype(
                jnp.bfloat16
            ),
            "tensor",
            scatter_dimension=0,
            tiled=True,
        ).astype(jnp.float32)
        stream = middle + (units_total + down_bias[layer_idx].astype(jnp.float32))
        saved.append(
            (
                layer_input,
                middle,
                normed_all,
                queries,
                keys_all,
                values_all,
                log_total,
                mixed_rows,
                normed_two_all,
                hidden_pre,
                activated,
            )
        )
    layer_out = stream.astype(jnp.bfloat16)
    grad_stream = cotangent.astype(jnp.float32) * row_mask
    weight_list = []
    shared_list = []
    for layer_idx in reversed(range(layer_count)):
        (
            layer_input,
            middle,
            normed_all,
            queries,
            keys_all,
            values_all,
            log_total,
            mixed_rows,
            normed_two_all,
            hidden_pre,
            activated,
        ) = saved[layer_idx]
        grad_down = grad_stream.astype(jnp.bfloat16)
        down_bias_grad = jnp.sum(grad_down.astype(jnp.float32), axis=0)
        grad_down_all = lax.all_gather(grad_down, "tensor", axis=0, tiled=True)
        down_weight_grad = jnp.einsum(
            "rf,rd->fd", activated, grad_down_all, preferred_element_type=jnp.float32
        )
        grad_act = jnp.einsum(
            "rd,fd->rf", grad_down_all, down_weight[layer_idx], preferred_element_type=jnp.float32
        )
        gelu_value, gelu_pull = jax.vjp(gelu_exact, hidden_pre)
        grad_hidden = gelu_pull(grad_act)[0].astype(jnp.bfloat16)
        up_bias_grad = jnp.sum(grad_hidden.astype(jnp.float32), axis=0)
        up_weight_grad = jnp.einsum(
            "rd,rf->df", normed_two_all, grad_hidden, preferred_element_type=jnp.float32
        )
        weight_up = up_weight[layer_idx]
        grad_normed_two = lax.psum_scatter(
            jnp.einsum(
                "rf,df->rd", grad_hidden, weight_up, preferred_element_type=jnp.float32
            ).astype(jnp.bfloat16),
            "tensor",
            scatter_dimension=0,
            tiled=True,
        ).astype(jnp.float32)
        norm_value, norm_pull = jax.vjp(
            normalize, middle, gains[layer_idx, 1], shifts[layer_idx, 1]
        )
        grad_from_norm, gain_two_grad, shift_two_grad = norm_pull(grad_normed_two)
        grad_middle = grad_stream + grad_from_norm
        grad_branch = grad_middle.astype(jnp.bfloat16)
        output_bias_grad = jnp.sum(grad_branch.astype(jnp.float32), axis=0)
        grad_branch_all = lax.all_gather(grad_branch, "tensor", axis=0, tiled=True)
        output_weight_grad = jnp.einsum(
            "re,rd->ed", mixed_rows, grad_branch_all, preferred_element_type=jnp.float32
        )
        grad_mixed = jnp.einsum(
            "rd,ed->re",
            grad_branch_all,
            output_weight[layer_idx],
            preferred_element_type=jnp.float32,
        ).astype(jnp.bfloat16)

        def backward_buffer(group):
            return attend_backward(
                group[0], group[1], group[2], group[3], group[4], group[5], head_size
            )

        grad_q, grad_k, grad_v = lax.map(
            backward_buffer,
            (
                head_split(queries),
                head_split(keys_all),
                head_split(values_all),
                valid_all,
                log_total,
                head_split(grad_mixed),
            ),
        )
        grad_projected = jnp.stack(
            [
                grad_q.reshape(rows_all, local_width),
                grad_k.reshape(rows_all, local_width),
                grad_v.reshape(rows_all, local_width),
            ]
        ).astype(jnp.bfloat16)
        input_weight_grad = jnp.einsum(
            "rd,sre->sde", normed_all, grad_projected, preferred_element_type=jnp.float32
        )
        projected_sums = jnp.sum(grad_projected.astype(jnp.float32), axis=1)
        input_bias_grad = jnp.stack([projected_sums[0], projected_sums[2]])
        weight_in = input_weight[layer_idx]
        grad_normed = lax.psum_scatter(
            jnp.einsum(
                "sre,sde->rd", grad_projected, weight_in, preferred_element_type=jnp.float32
            ).astype(jnp.bfloat16),
            "tensor",
            scatter_dimension=0,
            tiled=True,
        ).astype(jnp.float32)
        norm_value, norm_pull = jax.vjp(
            normalize, layer_input, gains[layer_idx, 0], shifts[layer_idx, 0]
        )
        grad_from_input, gain_one_grad, shift_one_grad = norm_pull(grad_normed)
        grad_stream = grad_middle + grad_from_input
        gain_pair = jnp.stack([gain_one_grad, gain_two_grad])
        shift_pair = jnp.stack([shift_one_grad, shift_two_grad])
        weight_list.insert(
            0,
            (
                input_weight_grad,
                input_bias_grad,
                output_weight_grad,
                up_weight_grad,
                up_bias_grad,
                down_weight_grad,
            ),
        )
        shared_list.insert(0, (gain_pair, shift_pair, output_bias_grad, down_bias_grad))
    stacked_weights = [
        jnp.stack([layer_grads[slot_index] for layer_grads in weight_list])
        for slot_index in range(6)
    ]
    stacked_shared = [
        jnp.stack([layer_grads[slot_index] for layer_grads in shared_list])
        for slot_index in range(4)
    ]
    (
        input_weight_all,
        input_bias_all,
        output_weight_all,
        up_weight_all,
        up_bias_all,
        down_weight_all,
    ) = stacked_weights
    gain_all, shift_all, output_bias_all, down_bias_all = stacked_shared
    (
        input_weight_all,
        input_bias_all,
        output_weight_all,
        up_weight_all,
        up_bias_all,
        down_weight_all,
    ) = lax.psum(
        (
            input_weight_all,
            input_bias_all,
            output_weight_all,
            up_weight_all,
            up_bias_all,
            down_weight_all,
        ),
        "dp",
    )
    gain_all, shift_all, output_bias_all, down_bias_all = lax.psum(
        (gain_all, shift_all, output_bias_all, down_bias_all), ("dp", "tensor")
    )
    return (
        layer_out,
        grad_stream,
        gain_all,
        shift_all,
        input_weight_all,
        input_bias_all,
        output_weight_all,
        output_bias_all,
        up_weight_all,
        up_bias_all,
        down_weight_all,
        down_bias_all,
    )


def solution(mesh):
    placed = (
        P(("dp", "tensor"), None),
        P("dp"),
        P(),
        P(),
        P(None, None, None, "tensor"),
        P(None, None, "tensor"),
        P(None, "tensor", None),
        P(),
        P(None, None, "tensor"),
        P(None, "tensor"),
        P(None, "tensor", None),
        P(),
        P(("dp", "tensor"), None),
    )
    return jax.shard_map(
        local,
        mesh=mesh,
        in_specs=placed,
        out_specs=(
            P(("dp", "tensor"), None),
            P(("dp", "tensor"), None),
            P(),
            P(),
            P(None, None, None, "tensor"),
            P(None, None, "tensor"),
            P(None, "tensor", None),
            P(),
            P(None, None, "tensor"),
            P(None, "tensor"),
            P(None, "tensor", None),
            P(),
        ),
        check_vma=False,
    )
```

profile of v0, /device:TPU:9, one launch (start us, length us, event | category | flops | bytes accessed | tf_op | source)
XLA Modules:
  0.0 1538.0 jit_solution(5088134616150104771)
XLA Ops:
  16.7 60.4 %all-gather.9.cloned.1.call-done = bf16[2048,768]{1,0:T(8,128)(2,1)} async-done(((bf16[512,768]{1,0:T(8,128)(2,1)}), bf16[2048,768]{1,0:T(8,128)(2,1)}) %all-gather.9.cloned.1.call-update) | async-done | bytes 3145744 | tf_op jit(solution)/shard_map/all_gather | solution.py:115
  93.0 20.3 %while.52 = (s32[]{:T(128)}, bf16[2,1024,3,64]{1,3,2,0:T(8,128)(2,1)S(1)}, f32[2,3,1024,1]{2,1,3,0:T(4,128)S(1)}, bf16[2,1024,3,64]{1,3,2,0:T(8,128)(2,1)S(1)}, ...) while((s32[]{:T(128)}, ...), condition=%wide.region_5.6_spmd, body=%wide.region_2.5_spmd.sunk | while | flops 843053056 | bytes 39839856 | solution.py:128
  119.3 59.8 %reduce-scatter.9.cloned.1.call-done = bf16[512,768]{1,0:T(8,128)(2,1)} async-done(((bf16[2048,768]{1,0:T(8,128)(2,1)}), bf16[512,768]{1,0:T(8,128)(2,1)}) %reduce-scatter.9.cloned.1.call-update) | async-done | bytes 786448 | tf_op jit(solution)/shard_map/reduce_scatter | solution.py:134
  184.3 61.0 %all-gather.11.cloned.1.call-done = bf16[2048,768]{1,0:T(8,128)(2,1)} async-done(((bf16[512,768]{1,0:T(8,128)(2,1)}), bf16[2048,768]{1,0:T(8,128)(2,1)}) %all-gather.11.cloned.1.call-update) | async-done | bytes 3145744 | tf_op jit(solution)/shard_map/all_gather | solution.py:146
  245.3 18.9 %multiply_convert_fusion.3 = (bf16[2048,768]{1,0:T(8,128)(2,1)S(1)}, f32[2048,768]{1,0:T(8,128)}, f32[2048,768]{1,0:T(8,128)}) fusion(f32[768]{0:T(1024)S(1)} %get-tuple-element.334, bf16[2048,768]{1,0:T(8,128)(2,1)} %all-gather.11.cloned.1.call-done, bf16[2,768,768]{2,1,0:T(8,128)(2,1)} %param.29), kind=kOutput, calls=%fused_computation.143 | convolution fusion | flops 2519728128 | bytes 20057088 | tf_op jit(solution)/shard_map/dot_general | solution.py:147
  271.1 59.8 %reduce-scatter.11.cloned.1.call-done = bf16[512,768]{1,0:T(8,128)(2,1)} async-done(((bf16[2048,768]{1,0:T(8,128)(2,1)}), bf16[512,768]{1,0:T(8,128)(2,1)}) %reduce-scatter.11.cloned.1.call-update) | async-done | bytes 786448 | tf_op jit(solution)/shard_map/reduce_scatter | solution.py:152
  334.4 61.4 %all-gather.13.cloned.1.call-done = bf16[2048,768]{1,0:T(8,128)(2,1)} async-done(((bf16[512,768]{1,0:T(8,128)(2,1)}), bf16[2048,768]{1,0:T(8,128)(2,1)}) %all-gather.13.cloned.1.call-update) | async-done | bytes 3145744 | tf_op jit(solution)/shard_map/all_gather | solution.py:115
  415.5 22.0 %while.53 = (s32[]{:T(128)}, bf16[2,1024,3,64]{1,3,2,0:T(8,128)(2,1)}, f32[2,3,1024,1]{2,1,3,0:T(4,128)S(1)}, bf16[2,1024,3,64]{1,3,2,0:T(8,128)(2,1)}, s32[2]{0...) while((s32[]{:T(128)}, ...), condition=%wide.region_15.16_spmd, body=%wide.region_12.15_spmd.sunk | while | flops 843053056 | bytes 49277124 | solution.py:128
  443.5 61.0 %reduce-scatter.13.cloned.1.call-done = bf16[512,768]{1,0:T(8,128)(2,1)} async-done(((bf16[2048,768]{1,0:T(8,128)(2,1)}), bf16[512,768]{1,0:T(8,128)(2,1)}) %reduce-scatter.13.cloned.1.call-update) | async-done | bytes 786448 | tf_op jit(solution)/shard_map/reduce_scatter | solution.py:134
  510.2 59.7 %all-gather.15.cloned.1.call-done = bf16[2048,768]{1,0:T(8,128)(2,1)} async-done(((bf16[512,768]{1,0:T(8,128)(2,1)}), bf16[2048,768]{1,0:T(8,128)(2,1)}) %all-gather.15.cloned.1.call-update) | async-done | bytes 3145744 | tf_op jit(solution)/shard_map/all_gather | solution.py:146
  569.9 18.9 %multiply_convert_fusion.2 = (bf16[2048,768]{1,0:T(8,128)(2,1)}, f32[2048,768]{1,0:T(8,128)}, f32[2048,768]{1,0:T(8,128)}) fusion(f32[768]{0:T(1024)S(1)} %copy-done.120, bf16[2048,768]{1,0:T(8,128)(2,1)} %all-gather.15.cloned.1.call-done, bf16[2,768,768]{2,1,0:T(8,128)(2,1)} %param.29), kind=kOutput, calls=%fused_computation.130 | convolution fusion | flops 2519728128 | bytes 20057088 | tf_op jit(solution)/shard_map/dot_general | solution.py:147
  588.9 45.4 %all-gather.17.cloned.1.call-done = bf16[2048,768]{1,0:T(8,128)(2,1)} async-done(((bf16[512,768]{1,0:T(8,128)(2,1)}), bf16[2048,768]{1,0:T(8,128)(2,1)}) %all-gather.17.cloned.1.call-update) | async-done | bytes 3145744 | tf_op jit(solution)/shard_map/all_gather | solution.py:196
  658.2 54.0 %reduce-scatter.17.cloned.1.call-done = bf16[512,768]{1,0:T(8,128)(2,1)} async-done(((bf16[2048,768]{1,0:T(8,128)(2,1)}), bf16[512,768]{1,0:T(8,128)(2,1)}) %reduce-scatter.17.cloned.1.call-update) | async-done | bytes 786448 | tf_op jit(solution)/shard_map/reduce_scatter | solution.py:210
  714.7 60.7 %reduce-scatter.15.cloned.1.call-done = bf16[512,768]{1,0:T(8,128)(2,1)} async-done(((bf16[2048,768]{1,0:T(8,128)(2,1)}), bf16[512,768]{1,0:T(8,128)(2,1)}) %reduce-scatter.15.cloned.1.call-update) | async-done | bytes 786448 | tf_op jit(solution)/shard_map/reduce_scatter | solution.py:152
  781.4 61.6 %all-gather.19.cloned.1.call-done = bf16[2048,768]{1,0:T(8,128)(2,1)} async-done(((bf16[512,768]{1,0:T(8,128)(2,1)}), bf16[2048,768]{1,0:T(8,128)(2,1)}) %all-gather.19.cloned.1.call-update) | async-done | bytes 3145744 | tf_op jit(solution)/shard_map/all_gather | solution.py:225
  851.9 49.7 %while.54 = (s32[]{:T(128)}, bf16[2,1024,3,64]{1,3,2,0:T(8,128)(2,1)}, bf16[2,1024,3,64]{1,3,2,0:T(8,128)(2,1)}, bf16[2,1024,3,64]{1,3,2,0:T(8,128)(2,1)}, bf16[...) while((s32[]{:T(128)}, ...), condition=%wide.region_26.27_spmd, body=%wide.region_24.26_spmd.sunk | while | flops 2060843008 | bytes 131044568 | solution.py:241
  913.5 61.0 %reduce-scatter.19.cloned.1.call-done = bf16[512,768]{1,0:T(8,128)(2,1)} async-done(((bf16[2048,768]{1,0:T(8,128)(2,1)}), bf16[512,768]{1,0:T(8,128)(2,1)}) %reduce-scatter.19.cloned.1.call-update) | async-done | bytes 786448 | tf_op jit(solution)/shard_map/reduce_scatter | solution.py:265
  982.4 61.4 %all-gather.21.cloned.1.call-done = bf16[2048,768]{1,0:T(8,128)(2,1)} async-done(((bf16[512,768]{1,0:T(8,128)(2,1)}), bf16[2048,768]{1,0:T(8,128)(2,1)}) %all-gather.21.cloned.1.call-update) | async-done | bytes 3145744 | tf_op jit(solution)/shard_map/all_gather | solution.py:196
  1060.8 61.0 %reduce-scatter.21.cloned.1.call-done = bf16[512,768]{1,0:T(8,128)(2,1)} async-done(((bf16[2048,768]{1,0:T(8,128)(2,1)}), bf16[512,768]{1,0:T(8,128)(2,1)}) %reduce-scatter.21.cloned.1.call-update) | async-done | bytes 786448 | tf_op jit(solution)/shard_map/reduce_scatter | solution.py:210
  1129.5 61.6 %all-gather.23.cloned.1.call-done = bf16[2048,768]{1,0:T(8,128)(2,1)} async-done(((bf16[512,768]{1,0:T(8,128)(2,1)}), bf16[2048,768]{1,0:T(8,128)(2,1)}) %all-gather.23.cloned.1.call-update) | async-done | bytes 3145744 | tf_op jit(solution)/shard_map/all_gather | solution.py:225
  1200.0 50.1 %while.55 = (s32[]{:T(128)}, bf16[2,1024,3,64]{1,3,2,0:T(8,128)(2,1)}, bf16[2,1024,3,64]{1,3,2,0:T(8,128)(2,1)}, bf16[2,1024,3,64]{1,3,2,0:T(8,128)(2,1)}, bf16[...) while((s32[]{:T(128)}, ...), condition=%wide.region_35.36_spmd, body=%wide.region_33.35_spmd.sunk | while | flops 2060843008 | bytes 131044568 | solution.py:241
  1300.2 21.5 %all-reduce.1 = (f32[2,2,192]{2,1,0:T(2,128)}, f32[2,768]{1,0:T(2,128)}) all-reduce(f32[2,2,192]{2,1,0:T(2,128)S(1)} %pad_maximum_fusion.9, f32[2,768]{1,0:T(2,128)S(1)} %pad_maximum_fusion.7), channel_id=1, replica_groups=mesh['dp'=8,'tensor'=4] {'dp'}, use_global_device_ids=true, to_apply=%region_52.53 | all-reduce | flops 2304 | bytes 18432 | tf_op jit(solution)/shard_map/psum | solution.py:316
  1326.9 44.6 %all-reduce = (f32[2,2,768]{2,1,0:T(2,128)}, f32[2,2,768]{2,1,0:T(2,128)}, f32[2,768]{1,0:T(2,128)}, f32[2,768]{1,0:T(2,128)}) all-reduce(f32[2,2,768]{2,1,0:T(2,128)S(1)} %pad_maximum_fusion.4, f32[2,2,768]{2,1,0:T(2,128)S(1)} %pad_maximum_fusion.5, ...), channel_id=1, replica_groups=mesh['dp'=8,'tensor'=4] {'dp','tensor'}, use_global_device_ids=true, to_apply=%region_43.44 | all-reduce | flops 9216 | bytes 73728 | tf_op jit(solution)/shard_map/psum | solution.py:327
  1374.9 145.2 %all-reduce.5.cloned.1.call-done = (f32[2,3,768,192]{2,3,1,0:T(8,128)}, f32[2,192,768]{2,1,0:T(8,128)}, f32[2,768,768]{2,1,0:T(8,128)}, f32[2,768,768]{2,1,0:T(8,128)}) async-done(((f32[2,3,768,192]{2,3,1,0:T(8,128)}, f32[2,192,768]{2,1,0:T(8,128)}, f32[2,768,768]{2,1,0:T(8,128)}, f32[2,768,768]{2,1,0:T(8,128)}), (f32[2,3,768,192]{2,3,1,0:T(8,128)}, f32[2,192,768]{2,1,0:T(8,128)}, f32[2,768,768]{2,1,0:T(8,128)}, ...) | async-done | bytes 14155792 | tf_op jit(solution)/shard_map/psum | solution.py:316
  (572 shorter events, 381.7 us)
Async XLA Ops:
  7.2 69.8 %all-gather.9.cloned.1.call-start = ((), (), s32[]{:S(2)}) async-start(), calls=%async_computation.8 | async-start | bytes 3932160 | tf_op jit(solution)/shard_map/all_gather | solution.py:115
  12.3 170.0 %copy-start.64 = (f32[768]{0:T(1024)}, f32[768]{0:T(1024)S(1)}, u32[]{:S(2)}) copy-start(f32[768]{0:T(1024)S(1)} %get-tuple-element.464) | copy-start | bytes 9220
  14.7 164.4 %reduce-scatter.9.cloned.1.call-start = ((), (), s32[]{:S(2)}) async-start(), calls=%async_computation.9 | async-start | bytes 3932160 | tf_op jit(solution)/shard_map/reduce_scatter | solution.py:134
  118.1 127.3 %all-gather.11.cloned.1.call-start = ((), (), s32[]{:S(2)}) async-start(), calls=%async_computation.10 | async-start | bytes 3932160 | tf_op jit(solution)/shard_map/all_gather | solution.py:146
  119.3 211.6 %copy-start.61 = (f32[768]{0:T(1024)}, f32[768]{0:T(1024)S(1)}, u32[]{:S(2)}) copy-start(f32[768]{0:T(1024)S(1)} %get-tuple-element.336) | copy-start | bytes 9220
  180.7 83.5 %copy-start.71 = (f32[512]{0:T(512)}, f32[512]{0:T(512)S(1)}, u32[]{:S(2)}) copy-start(f32[512]{0:T(512)S(1)} %broadcast_multiply_fusion.2) | copy-start | bytes 6148
  182.3 82.0 %copy-start.96 = (f32[512]{0:T(512)}, f32[512]{0:T(512)S(1)}, u32[]{:S(2)}) copy-start(f32[512]{0:T(512)S(1)} %multiply_reduce_fusion.4) | copy-start | bytes 6148
  183.7 147.3 %reduce-scatter.11.cloned.1.call-start = ((), (), s32[]{:S(2)}) async-start(), calls=%async_computation.11 | async-start | bytes 3932160 | tf_op jit(solution)/shard_map/reduce_scatter | solution.py:152
  269.9 126.0 %all-gather.13.cloned.1.call-start = ((), (), s32[]{:S(2)}) async-start(), calls=%async_computation.12 | async-start | bytes 3932160 | tf_op jit(solution)/shard_map/all_gather | solution.py:115
  332.5 171.9 %copy-start.5 = (f32[512,768]{1,0:T(8,128)}, f32[512,768]{1,0:T(8,128)S(1)}, u32[]{:S(2)}) copy-start(f32[512,768]{1,0:T(8,128)S(1)} %get-tuple-element.435) | copy-start | bytes 4718596
  334.2 170.3 %reduce-scatter.13.cloned.1.call-start = ((), (), s32[]{:S(2)}) async-start(), calls=%async_computation.13 | async-start | bytes 3932160 | tf_op jit(solution)/shard_map/reduce_scatter | solution.py:134
  443.4 126.5 %all-gather.15.cloned.1.call-start = ((), (), s32[]{:S(2)}) async-start(), calls=%async_computation.14 | async-start | bytes 3932160 | tf_op jit(solution)/shard_map/all_gather | solution.py:146
  508.3 126.0 %all-gather.17.cloned.1.call-start = ((), (), s32[]{:S(2)}) async-start(), calls=%async_computation.16 | async-start | bytes 3932160 | tf_op jit(solution)/shard_map/all_gather | solution.py:196
  508.4 270.0 %copy-start.88 = (f32[512]{0:T(512)}, f32[512]{0:T(512)S(1)}, u32[]{:S(2)}) copy-start(f32[512]{0:T(512)S(1)} %fusion.199) | copy-start | bytes 6148
  510.2 202.1 %reduce-scatter.17.cloned.1.call-start = ((), (), s32[]{:S(2)}) async-start(), calls=%async_computation.17 | async-start | bytes 3932160 | tf_op jit(solution)/shard_map/reduce_scatter | solution.py:210
  651.2 124.1 %reduce-scatter.15.cloned.1.call-start = ((), (), s32[]{:S(2)}) async-start(), calls=%async_computation.15 | async-start | bytes 3932160 | tf_op jit(solution)/shard_map/reduce_scatter | solution.py:152
  657.8 117.6 %copy-start.111 = (f32[768]{0:T(1024)S(1)}, f32[768]{0:T(1024)}, u32[]{:S(2)}) copy-start(f32[768]{0:T(1024)} %get-tuple-element.331) | copy-start | bytes 9220
  657.8 185.2 %all-gather.19.cloned.1.call-start = ((), (), s32[]{:S(2)}) async-start(), calls=%async_computation.18 | async-start | bytes 3932160 | tf_op jit(solution)/shard_map/all_gather | solution.py:225
  781.4 193.1 %reduce-scatter.19.cloned.1.call-start = ((), (), s32[]{:S(2)}) async-start(), calls=%async_computation.19 | async-start | bytes 3932160 | tf_op jit(solution)/shard_map/reduce_scatter | solution.py:265
  913.4 130.4 %all-gather.21.cloned.1.call-start = ((), (), s32[]{:S(2)}) async-start(), calls=%async_computation.20 | async-start | bytes 3932160 | tf_op jit(solution)/shard_map/all_gather | solution.py:196
  982.1 139.7 %reduce-scatter.21.cloned.1.call-start = ((), (), s32[]{:S(2)}) async-start(), calls=%async_computation.21 | async-start | bytes 3932160 | tf_op jit(solution)/shard_map/reduce_scatter | solution.py:210
  1060.8 130.4 %all-gather.23.cloned.1.call-start = ((), (), s32[]{:S(2)}) async-start(), calls=%async_computation.22 | async-start | bytes 3932160 | tf_op jit(solution)/shard_map/all_gather | solution.py:225
  1129.5 193.5 %reduce-scatter.23.cloned.1.call-start = ((), (), s32[]{:S(2)}) async-start(), calls=%async_computation.23 | async-start | bytes 3932160 | tf_op jit(solution)/shard_map/reduce_scatter | solution.py:265
  1261.9 258.2 %all-reduce.5.cloned.1.call-start = ((), (), s32[]{:S(2)}) async-start(), calls=%async_computation.24 | async-start | bytes 28311552 | tf_op jit(solution)/shard_map/psum | solution.py:316
  (146 other events, 3206.5 us)
Sparse Core Ops, SparseCore 0:
  14.8 62.2 all-gather.8
  118.2 60.9 reduce-scatter.8
  183.8 61.5 all-gather.10
  270.0 60.9 reduce-scatter.10
  334.3 61.4 all-gather.12
  443.5 60.9 reduce-scatter.12
  508.4 61.4 all-gather.14
  572.1 62.1 all-gather.16
  651.3 60.9 reduce-scatter.16
  715.0 60.2 reduce-scatter.14
  781.5 61.4 all-gather.18
  913.5 60.9 reduce-scatter.18
  982.3 61.4 all-gather.20
  1060.9 60.9 reduce-scatter.20
  1129.6 61.4 all-gather.22
  1262.0 60.9 reduce-scatter.22
  1328.0 192.0 all-reduce.4
where the time goes:
time: 1540 us
  waiting for transfers between devices  1040 us (68%)
  matrix products  216 us (14%)
  other arithmetic  108 us (7%)
  local copies, waits for them, and re-layouts  93.4 us (6%)
  blocking collectives  66.1 us (4%)
  between operations  16 us (1%)
    psum x1, waiting for transfers between devices, local(): lax.psum((input_weight_all, input_bias_all, output_weight_all, up_weight_...  145 us
    all_gather x2, waiting for transfers between devices, local(): grad_branch_all = lax.all_gather(grad_branch, 'tensor', axis=0, tiled=True)  123 us
    all_gather x2, waiting for transfers between devices, local(): normed_all = lax.all_gather(normed, 'tensor', axis=0, tiled=True)  122 us
    reduce_scatter x2, waiting for transfers between devices, local(): lax.psum_scatter(jnp.dot(mixed_rows, weight_out, preferred_element_type=j...  121 us
    all_gather x2, waiting for transfers between devices, local(): normed_two_all = lax.all_gather(normed_two, 'tensor', axis=0, tiled=True)  121 us
    reduce_scatter x2, waiting for transfers between devices, local(): lax.psum_scatter(jnp.dot(activated, weight_down, preferred_element_type=j...  120 us
    reduce_scatter x2, waiting for transfers between devices, local(): lax.psum_scatter(jnp.einsum('rf,df->rd', grad_hidden, weight_up, preferre...  115 us
    all_gather x2, waiting for transfers between devices, local(): grad_down_all = lax.all_gather(grad_down, 'tensor', axis=0, tiled=True)  107 us
  transfers between devices with their start and end apart: 17, of which 17 were waited for; matrix products, arithmetic and copies ran while one was open for 5% of the time, Pallas kernels for 0%

commit v1 on v0

v1 whole, which is shorter than its diff:
```python
import functools

import jax
import jax.numpy as jnp
from jax import lax
from jax.experimental import pallas as pl
from jax.experimental.pallas import tpu as pltpu
from jax.sharding import Mesh, PartitionSpec as P

HD = 64
ROWS = 1024
IMAGE = 240

epsilon = 1e-06
masked_score = -1e30
bf16 = jnp.bfloat16
f32 = jnp.float32


def dot(left, right, contract):
    return lax.dot_general(
        left, right, ((contract[:1], contract[1:]), ((), ())), preferred_element_type=f32
    )


def normalize(values, gain_row, bias_row):
    average = jnp.mean(values, axis=-1, keepdims=True)
    centred = values - average
    variance = jnp.mean(centred * centred, axis=-1, keepdims=True)
    return centred * lax.rsqrt(variance + epsilon) * gain_row + bias_row


def gelu_exact(values):
    return jax.nn.gelu(values, approximate=False)


def key_halves(core, own, received):
    first = jnp.where(core == 0, own, received)
    second = jnp.where(core == 0, received, own)
    return first, second


def attend_forward_kernel(info, queries, kv_own, kv_other, mixed, log_total):
    core, valid = info[0], info[1]
    width = queries.shape[0]
    half = kv_own.shape[1]
    key_place = lax.broadcasted_iota(jnp.int32, (half, 1), 0) + half
    key_bias = jnp.where(key_place < valid, 0.0, masked_score).astype(f32)
    for head in range(width // HD):
        rows = slice(head * HD, (head + 1) * HD)
        value_rows = slice(width + head * HD, width + (head + 1) * HD)
        query = queries[rows, :] * jnp.asarray(HD**-0.5, bf16)
        key_one, key_two = key_halves(core, kv_own[rows, :], kv_other[rows, :])
        value_one, value_two = key_halves(core, kv_own[value_rows, :], kv_other[value_rows, :])
        score_one = dot(key_one, query, (0, 0))
        score_two = dot(key_two, query, (0, 0)) + key_bias
        top = jnp.maximum(
            jnp.max(score_one, axis=0, keepdims=True), jnp.max(score_two, axis=0, keepdims=True)
        )
        weight_one = jnp.exp(score_one - top)
        weight_two = jnp.exp(score_two - top)
        total = jnp.sum(weight_one, axis=0, keepdims=True) + jnp.sum(
            weight_two, axis=0, keepdims=True
        )
        out = dot(value_one, weight_one.astype(bf16), (1, 0)) + dot(
            value_two, weight_two.astype(bf16), (1, 0)
        )
        mixed[rows, :] = (out / total).astype(bf16)
        log_total[0, head : head + 1, :] = top + jnp.log(total)


def attend_backward_kernel(
    info, queries, kv_own, kv_other, mixed, log_total, grad_mixed, grad_q, grad_own, grad_other
):
    core, valid = info[0], info[1]
    width = queries.shape[0]
    half = kv_own.shape[1]
    scale = HD**-0.5
    key_place = lax.broadcasted_iota(jnp.int32, (half, 1), 0) + half
    key_bias = jnp.where(key_place < valid, 0.0, masked_score).astype(f32)
    for head in range(width // HD):
        rows = slice(head * HD, (head + 1) * HD)
        value_rows = slice(width + head * HD, width + (head + 1) * HD)
        query = queries[rows, :] * jnp.asarray(scale, bf16)
        grad_out = grad_mixed[rows, :]
        delta = jnp.sum(
            grad_out.astype(f32) * mixed[rows, :].astype(f32), axis=0, keepdims=True
        )
        log_row = log_total[0, head : head + 1, :]
        keys = key_halves(core, kv_own[rows, :], kv_other[rows, :])
        values = key_halves(core, kv_own[value_rows, :], kv_other[value_rows, :])
        grad_query = None
        grad_keys = []
        grad_values = []
        for part in range(2):
            score = dot(keys[part], query, (0, 0))
            if part == 1:
                score = score + key_bias
            probs = jnp.exp(score - log_row)
            grad_values.append(dot(grad_out, probs.astype(bf16), (1, 1)))
            grad_probs = dot(values[part], grad_out, (0, 0))
            grad_score = (probs * (grad_probs - delta)).astype(bf16)
            term = dot(keys[part], grad_score, (1, 0))
            grad_query = term if grad_query is None else grad_query + term
            grad_keys.append(dot(query, grad_score, (1, 1)))
        grad_q[rows, :] = (grad_query * scale).astype(bf16)
        own, other = key_halves(core, *grad_keys)
        grad_own[rows, :] = own
        grad_other[rows, :] = other.astype(bf16)
        own, other = key_halves(core, *grad_values)
        grad_own[value_rows, :] = own
        grad_other[value_rows, :] = other.astype(bf16)


def attention_specs(groups, width, half):
    return dict(
        q=pl.BlockSpec((width, half), lambda g, info: (g, 0)),
        kv=pl.BlockSpec((2 * width, half), lambda g, info: (g, 0)),
        log=pl.BlockSpec((1, 8, half), lambda g, info: (g, 0, 0)),
    )


def attend_forward(info, queries, kv_own, kv_other, groups):
    features, half = queries.shape
    width = features // groups
    specs = attention_specs(groups, width, half)
    return pl.pallas_call(
        attend_forward_kernel,
        grid_spec=pltpu.PrefetchScalarGridSpec(
            num_scalar_prefetch=1,
            grid=(groups,),
            in_specs=[specs["q"], specs["kv"], specs["kv"]],
            out_specs=[specs["q"], specs["log"]],
        ),
        out_shape=[
            jax.ShapeDtypeStruct((features, half), bf16),
            jax.ShapeDtypeStruct((groups, 8, half), f32),
        ],
        compiler_params=pltpu.CompilerParams(vmem_limit_bytes=40 << 20),
        cost_estimate=pl.CostEstimate(
            flops=16 * features * half * 2 * half,
            bytes_accessed=12 * features * half,
            transcendentals=features // HD * half * 2 * half,
        ),
        name="attend_forward",
    )(info, queries, kv_own, kv_other)


def attend_backward(info, queries, kv_own, kv_other, mixed, log_total, grad_mixed, groups):
    features, half = queries.shape
    width = features // groups
    specs = attention_specs(groups, width, half)
    return pl.pallas_call(
        attend_backward_kernel,
        grid_spec=pltpu.PrefetchScalarGridSpec(
            num_scalar_prefetch=1,
            grid=(groups,),
            in_specs=[specs["q"], specs["kv"], specs["kv"], specs["q"], specs["log"], specs["q"]],
            out_specs=[specs["q"], specs["kv"], specs["kv"]],
        ),
        out_shape=[
            jax.ShapeDtypeStruct((features, half), bf16),
            jax.ShapeDtypeStruct((2 * features, half), f32),
            jax.ShapeDtypeStruct((2 * features, half), bf16),
        ],
        compiler_params=pltpu.CompilerParams(vmem_limit_bytes=40 << 20),
        cost_estimate=pl.CostEstimate(
            flops=40 * features * half * 2 * half,
            bytes_accessed=26 * features * half,
            transcendentals=features // HD * half * 2 * half,
        ),
        name="attend_backward",
    )(info, queries, kv_own, kv_other, mixed, log_total, grad_mixed)


flip_pair = [(0, 1), (1, 0)]


def over(axis, array):
    return lax.ppermute(array, axis, flip_pair)


def z_send(array, pairs):
    return lax.ppermute(array, "z", pairs)


inner_pairs = [(1, 2), (2, 1)]
outward_pairs = [(1, 0), (2, 3)]
inward_pairs = [(0, 1), (3, 2)]
near_pairs = [(0, 1), (1, 0), (2, 3), (3, 2)]


def gather_z(block):
    near = z_send(block, near_pairs)
    cross = z_send(block, inner_pairs)
    relay_one = z_send(cross, outward_pairs)
    cross_two = z_send(near, inner_pairs)
    relay_two = z_send(cross_two, outward_pairs)
    at_end = (lax.axis_index("z") == 0) | (lax.axis_index("z") == 3)
    return [
        block,
        near,
        jnp.where(at_end, relay_one, cross_two),
        jnp.where(at_end, relay_two, cross),
    ]


def add_low(kept, received):
    return (kept.astype(f32) + received.astype(f32)).astype(bf16)


def scatter_z(near, far):
    received = z_send(far, inward_pairs)
    far = add_low(far, received[::-1])
    received = z_send(far, inner_pairs)
    near = add_low(near, received[::-1])
    received = z_send(near[1], near_pairs)
    return add_low(near[0], received)


def flip_if(bit, array, axis):
    return jnp.where(bit == 1, jnp.flip(array, axis), array)


def paired(bit, own, received, axis):
    return jnp.stack(
        [jnp.where(bit == 0, own, received), jnp.where(bit == 0, received, own)], axis=axis
    )


def local(
    stream_in,
    patch_size,
    norm_gain,
    norm_bias,
    input_weight,
    input_bias,
    output_weight,
    output_bias,
    up_weight,
    up_bias,
    down_weight,
    down_bias,
    cotangent,
):
    half, width_all = stream_in.shape
    layer_count = input_weight.shape[0]
    shard = input_weight.shape[-1]
    unit_shard = up_weight.shape[-1]
    unit_slice = unit_shard // 8
    groups = lax.axis_size("z")
    outer = lax.axis_size("o")
    core, x_bit, y_bit = lax.axis_index("c"), lax.axis_index("x"), lax.axis_index("y")
    z_place = lax.axis_index("z")
    z_low, z_high = z_place % 2, z_place // 2

    swap = []
    for c in range(2):
        for z in range(groups):
            swap.append((c * groups + z, (z % 2) * groups + (z - z % 2 + c)))

    def swap_rows(array):
        return lax.ppermute(array, ("c", "z"), swap)

    other_patch = over("c", patch_size)
    patch = jnp.where(z_low == core, patch_size, other_patch)
    patch = jnp.where(z_high == 0, patch[0], patch[1])
    grid_side = IMAGE // patch
    valid = grid_side * grid_side
    info = jnp.stack([core, valid]).astype(jnp.int32)

    stream_rows = swap_rows(stream_in)

    up_bias_all = lax.all_gather(up_bias, "z", axis=0)
    input_bias_all = lax.all_gather(input_bias, "z", axis=0)

    def z_order(array):
        pairs = array.reshape((2, 2) + array.shape[1:])
        pairs = flip_if(z_high, flip_if(z_low, pairs, 1), 0)
        return pairs.reshape(array.shape)

    up_bias_all = z_order(up_bias_all).astype(f32)
    input_bias_all = z_order(input_bias_all).astype(f32)

    def unit_order(rows):
        cut = rows.reshape(2, 2, 2, 2, 2, unit_slice)
        cut = flip_if(y_bit, flip_if(x_bit, flip_if(core, cut, 4), 3), 2)
        one = cut[0].transpose(3, 1, 2, 0, 4)
        two = cut[1].transpose(3, 2, 1, 0, 4)
        return jnp.stack([one, two]).reshape(4, unit_shard)

    def unit_order_back(pieces):
        cut = pieces.reshape(2, 2, 2, 2, 2, unit_slice)
        one = cut[0].transpose(3, 1, 2, 0, 4)
        two = cut[1].transpose(3, 2, 1, 0, 4)
        cut = jnp.stack([one, two])
        cut = flip_if(y_bit, flip_if(x_bit, flip_if(core, cut, 4), 3), 2)
        return z_order(cut.reshape(4, unit_shard))

    slice_index = (y_bit * 2 + x_bit) * 2 + core

    def gather_attention(layer_idx):
        kinds = jnp.swapaxes(input_weight[layer_idx], 1, 2)
        kept = jnp.where(
            core == 0,
            jnp.stack([kinds[1], kinds[2]]),
            jnp.stack([kinds[0], output_weight[layer_idx]]),
        )
        blocks = jnp.stack(gather_z(kept))
        received = over("c", blocks)
        kv = jnp.where(core == 0, blocks, received)
        qo = jnp.where(core == 0, received, blocks)
        return (
            kv.reshape(2 * groups * shard, width_all),
            qo[:, 0].reshape(groups * shard, width_all),
            qo[:, 1].reshape(groups * shard, width_all),
        )

    def gather_units(layer_idx):
        up = lax.dynamic_slice_in_dim(
            up_weight[layer_idx], slice_index * unit_slice, unit_slice, axis=1
        )
        down = lax.dynamic_slice_in_dim(
            down_weight[layer_idx], slice_index * unit_slice, unit_slice, axis=0
        )
        blocks = gather_z(jnp.stack([up.T, down]))
        one = jnp.concatenate(blocks[:2], axis=1)
        two = jnp.concatenate(blocks[2:], axis=1)
        one = jnp.concatenate([one, over("x", one)], axis=1)
        two = jnp.concatenate([two, over("y", two)], axis=1)
        one = jnp.concatenate([one, over("y", one)], axis=1)
        two = jnp.concatenate([two, over("x", two)], axis=1)
        pieces = [one, over("c", one), two, over("c", two)]
        return [piece[0] for piece in pieces], [piece[1] for piece in pieces]

    attention_weights = [gather_attention(0)]
    unit_weights = [gather_units(0)]
    for layer_idx in range(1, layer_count):
        attention_weights.append(gather_attention(layer_idx))
        unit_weights.append(gather_units(layer_idx))

    cotangent_rows = swap_rows(cotangent)
    gains = norm_gain.astype(f32)
    shifts = norm_bias.astype(f32)

    stream = stream_rows.astype(f32)
    saved = []
    for layer_idx in range(layer_count):
        weight_kv, weight_q, weight_o = attention_weights[layer_idx]
        up_pieces, down_pieces = unit_weights[layer_idx]
        layer_input = stream
        normed = normalize(stream, gains[layer_idx, 0], shifts[layer_idx, 0]).astype(bf16)
        value_bias = input_bias_all[:, layer_idx, 1]
        kv_bias = jnp.stack([jnp.zeros_like(value_bias), value_bias], axis=1).reshape(-1, 1)
        kv_own = (dot(weight_kv, normed, (1, 1)) + kv_bias).astype(bf16)
        kv_other = over("c", kv_own)
        query_bias = input_bias_all[:, layer_idx, 0].reshape(-1, 1)
        queries = (dot(weight_q, normed, (1, 1)) + query_bias).astype(bf16)
        mixed, log_total = attend_forward(info, queries, kv_own, kv_other, groups)
        middle = stream + (
            dot(mixed, weight_o, (0, 0)) + output_bias[layer_idx].astype(f32)
        )
        normed_two = normalize(middle, gains[layer_idx, 1], shifts[layer_idx, 1]).astype(bf16)
        unit_bias = unit_order(up_bias_all[:, layer_idx])
        hidden = []
        activated = []
        branch = None
        for piece in range(4):
            pre = dot(normed_two, up_pieces[piece], (1, 1)) + unit_bias[piece]
            act = gelu_exact(pre).astype(bf16)
            hidden.append(pre)
            activated.append(act)
            term = dot(act, down_pieces[piece], (1, 0))
            branch = term if branch is None else branch + term
        stream = middle + (branch + down_bias[layer_idx].astype(f32))
        saved.append(
            (
                layer_input,
                middle,
                normed,
                queries,
                kv_own,
                kv_other,
                log_total,
                mixed,
                normed_two,
                hidden,
                activated,
            )
        )
    layer_out = swap_rows(stream.astype(bf16))

    row_place = core * half + jnp.arange(half, dtype=jnp.int32)
    row_mask = (row_place < valid).astype(f32)[:, None]
    grad_stream = cotangent_rows.astype(f32) * row_mask

    def scatter_units(up_grads, down_grads):
        def across(piece):
            sent = jnp.stack([up_grads[piece + 1], down_grads[piece + 1]]).astype(bf16)
            received = over("c", sent).astype(f32)
            return jnp.stack(
                [up_grads[piece] + received[0], down_grads[piece] + received[1]]
            ).astype(bf16)

        def halve(array, axis):
            count = array.shape[1] // 2
            return add_low(array[:, :count], over(axis, array[:, count:]))

        one, two = across(0), across(2)
        one, two = halve(one, "y"), halve(two, "x")
        one, two = halve(one, "x"), halve(two, "y")
        cut = (2, 2, unit_slice, width_all)
        one = jnp.swapaxes(one.reshape(cut), 0, 1)
        two = jnp.swapaxes(two.reshape(cut), 0, 1)
        total = scatter_z(one, two)
        if outer > 1:
            total = lax.psum(total, "o")
        total = paired(x_bit, total, over("x", total), 1)
        total = paired(y_bit, total, over("y", total), 1)
        total = paired(core, total, over("c", total), 3)
        return total.reshape(2, unit_shard, width_all).astype(f32)

    def scatter_attention(grad_kv, grad_q, grad_o):
        kv = grad_kv.reshape(groups, 2, shard, width_all)
        qo = jnp.stack(
            [
                grad_q.reshape(groups, shard, width_all),
                grad_o.reshape(groups, shard, width_all),
            ],
            axis=1,
        )
        sent = jnp.where(core == 0, qo, kv).astype(bf16)
        kept = jnp.where(core == 0, kv, qo)
        total = add_low(kept, over("c", sent))
        total = scatter_z(total[:2], total[2:])
        if outer > 1:
            total = lax.psum(total, "o")
        one, two = total[0], total[1]
        one, two = add_low(one, over("x", one)), add_low(two, over("y", two))
        one, two = add_low(one, over("y", one)), add_low(two, over("x", two))
        total = jnp.stack([one, two])
        total = paired(core, total, over("c", total), 0).astype(f32)
        weight_in = jnp.stack([total[1, 0], total[0, 0], total[0, 1]])
        return jnp.swapaxes(weight_in, 1, 2), total[1, 1]

    layer_grads = [None] * layer_count
    small_rows = [None] * layer_count
    for layer_idx in reversed(range(layer_count)):
        (
            layer_input,
            middle,
            normed,
            queries,
            kv_own,
            kv_other,
            log_total,
            mixed,
            normed_two,
            hidden,
            activated,
        ) = saved[layer_idx]
        weight_kv, weight_q, weight_o = attention_weights[layer_idx]
        up_pieces, down_pieces = unit_weights[layer_idx]
        grad_down = grad_stream.astype(bf16)
        down_bias_grad = jnp.sum(grad_down.astype(f32), axis=0)
        up_grads = [None] * 4
        down_grads = [None] * 4
        up_bias_grads = [None] * 4
        grad_normed_two = None
        for piece in (1, 3, 0, 2):
            down_grads[piece] = dot(activated[piece], grad_down, (0, 0))
            grad_act = dot(grad_down, down_pieces[piece], (1, 1))
            gelu_pull = jax.vjp(gelu_exact, hidden[piece])[1]
            grad_hidden = gelu_pull(grad_act)[0].astype(bf16)
            up_bias_grads[piece] = jnp.sum(grad_hidden.astype(f32), axis=0)
            up_grads[piece] = dot(grad_hidden, normed_two, (0, 0))
            term = dot(grad_hidden, up_pieces[piece], (1, 0))
            grad_normed_two = term if grad_normed_two is None else grad_normed_two + term
        unit_grads = scatter_units(up_grads, down_grads)
        norm_pull = jax.vjp(normalize, middle, gains[layer_idx, 1], shifts[layer_idx, 1])[1]
        grad_from_norm, gain_two_grad, shift_two_grad = norm_pull(grad_normed_two)
        grad_middle = grad_stream + grad_from_norm
        grad_branch = grad_middle.astype(bf16)
        output_bias_grad = jnp.sum(grad_branch.astype(f32), axis=0)
        grad_o = dot(mixed, grad_branch, (1, 0))
        grad_mixed = dot(weight_o, grad_branch, (1, 1)).astype(bf16)
        grad_queries, grad_kv_own, grad_kv_other = attend_backward(
            info, queries, kv_own, kv_other, mixed, log_total, grad_mixed, groups
        )
        grad_kv = add_low(grad_kv_own, over("c", grad_kv_other))
        grad_q = dot(grad_queries, normed, (1, 0))
        grad_kv_weight = dot(grad_kv, normed, (1, 0))
        attention_grads = scatter_attention(grad_kv_weight, grad_q, grad_o)
        query_bias_grad = jnp.sum(grad_queries.astype(f32), axis=1)
        value_bias_grad = jnp.sum(
            grad_kv.reshape(groups, 2, shard, half)[:, 1].astype(f32), axis=-1
        )
        grad_normed = dot(grad_queries, weight_q, (0, 0)) + dot(grad_kv, weight_kv, (0, 0))
        norm_pull = jax.vjp(normalize, layer_input, gains[layer_idx, 0], shifts[layer_idx, 0])[1]
        grad_from_input, gain_one_grad, shift_one_grad = norm_pull(grad_normed)
        grad_stream = grad_middle + grad_from_input
        layer_grads[layer_idx] = (unit_grads, attention_grads)
        small_rows[layer_idx] = jnp.concatenate(
            [
                jnp.stack(
                    [
                        gain_one_grad,
                        gain_two_grad,
                        shift_one_grad,
                        shift_two_grad,
                        output_bias_grad,
                        down_bias_grad,
                    ]
                ),
                unit_order_back(jnp.stack(up_bias_grads)),
                z_order(query_bias_grad.reshape(groups, shard)).reshape(1, -1),
                z_order(value_bias_grad).reshape(1, -1),
            ]
        )
    grad_in = swap_rows(grad_stream)
    small = jnp.stack(small_rows)
    for axis in ("c", "x", "y"):
        small = small + over(axis, small)
    small = small + z_send(small, near_pairs)
    small = small + z_send(small, [(0, 2), (2, 0), (1, 3), (3, 1)])
    if outer > 1:
        small = lax.psum(small, "o")

    def z_part(array, size):
        return lax.dynamic_slice_in_dim(array, z_place * size, size, axis=-1)

    up_bias_all = z_part(small[:, 6:10].reshape(layer_count, -1), unit_shard)
    input_bias_grad = z_part(small[:, 10:12], shard)
    return (
        layer_out,
        grad_in,
        small[:, 0:2],
        small[:, 2:4],
        jnp.stack([grads[1][0] for grads in layer_grads]),
        input_bias_grad,
        jnp.stack([grads[1][1] for grads in layer_grads]),
        small[:, 4],
        jnp.stack([jnp.swapaxes(grads[0][0], 0, 1) for grads in layer_grads]),
        up_bias_all,
        jnp.stack([grads[0][1] for grads in layer_grads]),
        small[:, 5],
    )


def solution(mesh):
    split = mesh.shape["dp"] // 8
    fine = Mesh(
        mesh.devices.reshape(split, 2, 2, 2, mesh.shape["tensor"]), ("o", "y", "x", "c", "z")
    )
    rows = P(("o", "y", "x", "c", "z"), None)
    placed = (
        rows,
        P(("o", "y", "x", "c")),
        P(),
        P(),
        P(None, None, None, "z"),
        P(None, None, "z"),
        P(None, "z", None),
        P(),
        P(None, None, "z"),
        P(None, "z"),
        P(None, "z", None),
        P(),
        rows,
    )
    return jax.shard_map(
        local,
        mesh=fine,
        in_specs=placed,
        out_specs=(rows, rows) + placed[2:12],
        check_vma=False,
    )
```

time: 1540 us -> 827 us (0.54)
  waiting for transfers between devices: 1040 us -> 252 us
  starting transfers between devices: 1.5 us -> 162 us
  matrix products: 216 us -> 151 us
  Pallas kernels: 0 us -> 63.2 us
  blocking collectives: 66.1 us -> 23.6 us
  local copies, waits for them, and re-layouts: 93.4 us -> 60.5 us
    all_gather x8 -> x0, waiting for transfers between devices: 472 us -> none  [the longest x2 123 us: local(): grad_branch_all = lax.all_gather(grad_branch, 'tensor', axis=0, tiled=True)]
    reduce_scatter x8 -> x0, waiting for transfers between devices: 419 us -> none  [the longest x2 121 us: local(): lax.psum_scatter(jnp.dot(mixed_rows, weight_out, preferred_element_type=j...]
    ppermute x0 -> x90, waiting for transfers between devices: none -> 252 us  [the longest x34 132 us: z_send(): return lax.ppermute(array, 'z', pairs)]
    ppermute x0 -> x90, starting transfers between devices: none -> 162 us  [the longest x52 71.4 us: over(): return lax.ppermute(array, axis, flip_pair)]
    psum x1 -> x0, waiting for transfers between devices: 145 us -> none  [local(): lax.psum((input_weight_all, input_bias_all, output_weight_all, up_weight_...]
    psum x2 -> x0, blocking collectives: 66.1 us -> none  [the longest x1 44.6 us: local(): lax.psum((gain_all, shift_all, output_bias_all, down_bias_all), ('dp', 't...]
    pallas_call x0 -> x4, Pallas kernels: none -> 63.2 us  [the longest x2 38.7 us: attend_backward(): pl.pallas_call(attend_backward_kernel, grid_spec=pltpu.PrefetchScalarGrid...]
    dot_general x50 -> x66, matrix products: 208 us -> 151 us  [dot(): lax.dot_general(left, right, ((contract[:1], contract[1:]), ((), ())), pr...]
  transfers between devices with their start and end apart: 17 -> 90, of which waited for: 17 -> 31; matrix products, arithmetic and copies ran while one was open for 5% -> 30% of each run, Pallas kernels for 0% -> 5%
where the time goes in v1:
time: 827 us; the launch traced here: 817 us
  waiting for transfers between devices  252 us (30%)
  starting transfers between devices  162 us (20%)
  matrix products  151 us (18%)
  other arithmetic  99 us (12%)
  Pallas kernels  63.2 us (8%)
  local copies, waits for them, and re-layouts  60.5 us (7%)
  blocking collectives  23.6 us (3%)
    dot_general x66, matrix products, dot(): lax.dot_general(left, right, ((contract[:1], contract[1:]), ((), ())), pr...  151 us
    ppermute x34, waiting for transfers between devices, z_send(): return lax.ppermute(array, 'z', pairs)  132 us
    ppermute x52, waiting for transfers between devices, over(): return lax.ppermute(array, axis, flip_pair)  119 us
    ppermute x52, starting transfers between devices, over(): return lax.ppermute(array, axis, flip_pair)  71.4 us
    ppermute x34, starting transfers between devices, z_send(): return lax.ppermute(array, 'z', pairs)  60.2 us
    pallas_call x2, Pallas kernels, attend_backward(): pl.pallas_call(attend_backward_kernel, grid_spec=pltpu.PrefetchScalarGrid...  38.7 us
    unnamed x402, local copies, waits for them, and re-layouts  35.3 us
    ppermute x4, starting transfers between devices, swap_rows(): return lax.ppermute(array, ('c', 'z'), swap)  30.1 us
  transfers between devices with their start and end apart: 90, of which 31 were waited for; matrix products, arithmetic and copies ran while one was open for 30% of the time, Pallas kernels for 5%

profile of v1, /device:TPU:9, one launch (start us, length us, event | category | flops | bytes accessed | tf_op | source)
XLA Modules:
  0.0 816.5 jit_solution(4751713511833156580)
XLA Ops:
  25.8 14.3 %all-gather = bf16[8,2,192]{2,1,0:T(2,128)(2,1)S(1)} all-gather(bf16[2,2,192]{2,1,0:T(2,128)(2,1)S(1)} %copy-done.176), channel_id=2, replica_groups=mesh['o'=1,'y'=2,'x'=2,'c'=2,'z'=4] {'z'}, dimensions={0}, use_global_device_ids=true | all-gather | bytes 7680 | tf_op jit(solution)/shard_map/all_gather | solution.py:275
  41.6 9.3 %all-gather.2 = bf16[4,2,768]{2,1,0:T(2,128)(2,1)S(1)} all-gather(bf16[1,2,768]{2,1,0:T(2,128)(2,1)S(1)} %bitcast.636), channel_id=3, replica_groups=mesh['o'=1,'y'=2,'x'=2,'c'=2,'z'=4] {'z'}, dimensions={0}, use_global_device_ids=true | all-gather | bytes 15360 | tf_op jit(solution)/shard_map/all_gather | solution.py:274
  91.7 7.6 collective-permute-done.5
  100.8 10.8 %collective-permute-done.4 = bf16[2,192,768]{2,1,0:T(8,128)(2,1)S(1)} collective-permute-done((bf16[2,192,768]{2,1,0:T(8,128)(2,1)S(1)}, bf16[2,192,768]{2,1,0:T(8,128)(2,1)S(1)}, u32[]{:S(2)}, u32[]{:S(2)}) %collective-permute-start.4) | collective-permute-done | bytes 589856 | tf_op jit(solution)/shard_map/ppermute | solution.py:184
  115.8 14.8 %collective-permute-done.6 = bf16[2,192,768]{2,1,0:T(8,128)(2,1)S(1)} collective-permute-done((bf16[2,192,768]{2,1,0:T(8,128)(2,1)S(1)}, bf16[2,192,768]{2,1,0:T(8,128)(2,1)S(1)}, u32[]{:S(2)}, u32[]{:S(2)}) %collective-permute-start.6) | collective-permute-done | bytes 589856 | tf_op jit(solution)/shard_map/ppermute | solution.py:184
  146.3 11.1 %collective-permute-done.23 = bf16[2,192,768]{2,1,0:T(8,128)(2,1)S(1)} collective-permute-done((bf16[2,192,768]{2,1,0:T(8,128)(2,1)S(1)}, bf16[2,192,768]{2,1,0:T(8,128)(2,1)S(1)}, u32[]{:S(2)}, u32[]{:S(2)}) %collective-permute-start.23) | collective-permute-done | bytes 589856 | tf_op jit(solution)/shard_map/ppermute | solution.py:184
  158.8 7.4 collective-permute-start.39
  172.2 9.3 %collective-permute-done.35 = bf16[2,192,768]{2,1,0:T(8,128)(2,1)S(1)} collective-permute-done((bf16[2,192,768]{2,1,0:T(8,128)(2,1)S(1)}, bf16[2,192,768]{2,1,0:T(8,128)(2,1)S(1)}, u32[]{:S(2)}, u32[]{:S(2)}) %collective-permute-start.35) | collective-permute-done | bytes 589856 | tf_op jit(solution)/shard_map/ppermute | solution.py:180
  185.4 34.1 %collective-permute-done.17 = bf16[2,192,768]{2,1,0:T(8,128)(2,1)S(1)} collective-permute-done((bf16[2,192,768]{2,1,0:T(8,128)(2,1)S(1)}, bf16[2,192,768]{2,1,0:T(8,128)(2,1)S(1)}, u32[]{:S(2)}, u32[]{:S(2)}) %collective-permute-start.17) | collective-permute-done | bytes 589856 | tf_op jit(solution)/shard_map/ppermute | solution.py:180
  228.7 17.9 %collective-permute-done.18 = bf16[2,384,768]{2,1,0:T(8,128)(2,1)S(1)} collective-permute-done((bf16[2,384,768]{2,1,0:T(8,128)(2,1)S(1)}, bf16[2,384,768]{2,1,0:T(8,128)(2,1)S(1)}, u32[]{:S(2)}, u32[]{:S(2)}) %collective-permute-start.18) | collective-permute-done | bytes 1179680 | tf_op jit(solution)/shard_map/ppermute | solution.py:180
  254.1 11.9 %attend_forward.2 = (bf16[768,512]{1,0:T(8,128)(2,1)S(1)}, f32[4,8,512]{2,1,0:T(8,128)S(1)}) custom-call(s32[2]{0:T(128)S(1)} %pad_add_fusion.info, bf16[768,512]{1,0:T(8,128)(2,1)S(1)} %add_convert_fusion.25.queries, bf16[1536,512]{1,0:T(8,128)(2,1)S(1)} %fusion.kv_own, bf16[1536,512]{1,0:T(8,128)(2,1)S(1)} %collective-permute-done.8.kv_other), custom_call_target="tpu_custom_call" | custom-call | flops 6442450944 | bytes 4718592 | tf_op jit(solution)/shard_map/attend_forward/pallas_call | solution.py:127
  305.0 12.5 %attend_forward.3 = (bf16[768,512]{1,0:T(8,128)(2,1)S(1)}, f32[4,8,512]{2,1,0:T(8,128)S(1)}) custom-call(s32[2]{0:T(128)S(1)} %pad_add_fusion.info, bf16[768,512]{1,0:T(8,128)(2,1)S(1)} %add_convert_fusion.22.queries, bf16[1536,512]{1,0:T(8,128)(2,1)S(1)} %fusion.1.kv_own, bf16[1536,512]{1,0:T(8,128)(2,1)S(1)} %collective-permute-done.26.kv_other), custom_call_target="tpu_custom_call" | custom-call | flops 6442450944 | bytes 4718592 | tf_op jit(solution)/shard_map/attend_forward/pallas_call | solution.py:127
  319.5 11.1 %multiply_convert_fusion.3 = (bf16[512,768]{1,0:T(8,128)(2,1)}, f32[512,768]{1,0:T(8,128)S(1)}, f32[512,768]{1,0:T(8,128)S(1)}) fusion(f32[768]{0:T(1024)S(1)} %get-tuple-element.98, bf16[512,768]{1,0:T(8,128)(2,1)S(1)} %add_convert_fusion.21, bf16[2,768,768]{2,1,0:T(8,128)(2,1)S(1)} %pad_maximum_fusion.9), kind=kOutput, calls=%fused_computation.185 | convolution fusion | flops 629932032 | bytes 5902336 | tf_op jit(solution)/shard_map/dot_general | solution.py:21
  330.6 11.3 %multiply_convert_fusion.2 = (bf16[512,768]{1,0:T(8,128)(2,1)}, f32[512,768]{1,0:T(8,128)S(1)}, f32[512,768]{1,0:T(8,128)S(1)}) fusion(f32[768]{0:T(1024)S(1)} %get-tuple-element.97, bf16[512,768]{1,0:T(8,128)(2,1)S(1)} %add_convert_fusion.21, bf16[2,768,768]{2,1,0:T(8,128)(2,1)S(1)} %collective-permute-done.30), kind=kOutput, calls=%fused_computation.172 | convolution fusion | flops 629932032 | bytes 5902336 | tf_op jit(solution)/shard_map/dot_general | solution.py:21
  348.2 11.1 %multiply_convert_fusion.1 = (bf16[512,768]{1,0:T(8,128)(2,1)}, f32[512,768]{1,0:T(8,128)S(1)}, f32[512,768]{1,0:T(8,128)S(1)}) fusion(f32[768]{0:T(1024)S(1)} %get-tuple-element.96, bf16[512,768]{1,0:T(8,128)(2,1)S(1)} %add_convert_fusion.21, bf16[2,768,768]{2,1,0:T(8,128)(2,1)S(1)} %pad_maximum_fusion.10), kind=kOutput, calls=%fused_computation.159 | convolution fusion | flops 629932032 | bytes 5902336 | tf_op jit(solution)/shard_map/dot_general | solution.py:21
  359.3 10.7 %multiply_convert_fusion = (bf16[512,768]{1,0:T(8,128)(2,1)S(1)}, f32[512,768]{1,0:T(8,128)S(1)}, f32[512,768]{1,0:T(8,128)S(1)}) fusion(f32[768]{0:T(1024)S(1)} %get-tuple-element.95, bf16[512,768]{1,0:T(8,128)(2,1)S(1)} %add_convert_fusion.21, bf16[2,768,768]{2,1,0:T(8,128)(2,1)S(1)} %collective-permute-done.37), kind=kOutput, calls=%fused_computation.146 | convolution fusion | flops 629932032 | bytes 5902336 | tf_op jit(solution)/shard_map/dot_general | solution.py:21
  383.6 19.4 %attend_backward.2 = (bf16[768,512]{1,0:T(8,128)(2,1)S(1)}, f32[1536,512]{1,0:T(8,128)S(1)}, bf16[1536,512]{1,0:T(8,128)(2,1)}) custom-call(s32[2]{0:T(128)S(1)} %pad_add_fusion.info, bf16[768,512]{1,0:T(8,128)(2,1)S(1)} %add_convert_fusion.22.queries, bf16[1536,512]{1,0:T(8,128)(2,1)S(1)} %copy-done.16, bf16[1536,512]{1,0:T(8,128)(2,1)S(1)} %copy-done.18, ...), custom_call_target="tpu_custom_call" | custom-call | flops 16106127360 | bytes 10223616 | tf_op jit(solution)/shard_map/attend_backward/pallas_call | solution.py:153
  418.8 7.4 collective-permute-start.38
  468.6 19.4 %attend_backward.3 = (bf16[768,512]{1,0:T(8,128)(2,1)S(1)}, f32[1536,512]{1,0:T(8,128)S(1)}, bf16[1536,512]{1,0:T(8,128)(2,1)}) custom-call(s32[2]{0:T(128)S(1)} %pad_add_fusion.info, bf16[768,512]{1,0:T(8,128)(2,1)S(1)} %copy-done.20, bf16[1536,512]{1,0:T(8,128)(2,1)S(1)} %copy-done.12, bf16[1536,512]{1,0:T(8,128)(2,1)S(1)} %copy-done.14, ...), custom_call_target="tpu_custom_call" | custom-call | flops 16106127360 | bytes 10223616 | tf_op jit(solution)/shard_map/attend_backward/pallas_call | solution.py:153
  536.2 27.7 %collective-permute-done.44 = f32[2,12,768]{2,0,1:T(2,128)S(1)} collective-permute-done((f32[2,12,768]{2,0,1:T(2,128)S(1)}, f32[2,12,768]{2,0,1:T(2,128)S(1)}, u32[]{:S(2)}, u32[]{:S(2)}) %collective-permute-start.44) | collective-permute-done | bytes 73760 | tf_op jit(solution)/shard_map/ppermute | solution.py:180
  583.6 13.4 %collective-permute-start.42 = (f32[512,768]{1,0:T(8,128)}, f32[512,768]{1,0:T(8,128)}, u32[]{:S(2)}, u32[]{:S(2)}) collective-permute-start(f32[512,768]{1,0:T(8,128)} %add_add_fusion.4), channel_id=1, source_target_pairs={{0,0},{1,4},{2,2},{3,6},{4,1},{5,5},{6,3},{7,7},{8,8},{9,12},{10,1... | collective-permute-start | bytes 4718600 | tf_op jit(solution)/shard_map/ppermute | solution.py:263
  641.1 16.3 %collective-permute-done.58 = bf16[2,2,192,768]{3,2,1,0:T(8,128)(2,1)S(1)} collective-permute-done((bf16[2,2,192,768]{3,2,1,0:T(8,128)(2,1)S(1)}, bf16[2,2,192,768]{3,2,1,0:T(8,128)(2,1)S(1)}, u32[]{:S(2)}, u32[]{:S(2)}) %collective-permute-start.58) | collective-permute-done | bytes 1179680 | tf_op jit(solution)/shard_map/ppermute | solution.py:184
  672.3 32.8 %collective-permute-done.72 = bf16[2,2,96,768]{3,2,1,0:T(8,128)(2,1)S(1)} collective-permute-done((bf16[2,2,96,768]{3,2,1,0:T(8,128)(2,1)S(1)}, bf16[2,2,96,768]{3,2,1,0:T(8,128)(2,1)S(1)}, u32[]{:S(2)}, u32[]{:S(2)}) %collective-permute-start.72) | collective-permute-done | bytes 589856 | tf_op jit(solution)/shard_map/ppermute | solution.py:184
  782.6 8.1 collective-permute-start.56
  (927 shorter events, 460.5 us)
Async XLA Ops:
  7.4 49.1 %collective-permute-start.27 = (bf16[2,96,768]{2,1,0:T(8,128)(2,1)}, bf16[2,96,768]{2,1,0:T(8,128)(2,1)S(1)}, u32[]{:S(2)}, u32[]{:S(2)}) collective-permute-start(bf16[2,96,768]{2,1,0:T(8,128)(2,1)} %pad_maximum_fusion.35), channel_id=1, source_target_pairs={{0,1},{1,0},{2,3},{3,2},{4,5},{5,4},{6,7},{7,6},{8,9},{9,8},{10,11... | collective-permute-start | bytes 884744 | tf_op jit(solution)/shard_map/ppermute | solution.py:184
  7.4 52.1 %collective-permute-start.31 = (bf16[2,96,768]{2,1,0:T(8,128)(2,1)}, bf16[2,96,768]{2,1,0:T(8,128)(2,1)}, u32[]{:S(2)}, u32[]{:S(2)}) collective-permute-start(bf16[2,96,768]{2,1,0:T(8,128)(2,1)} %pad_maximum_fusion.35), channel_id=1, source_target_pairs={{1,2},{2,1},{5,6},{6,5},{9,10},{10,9},{13,14},{14,13},{17,18},{18,... | collective-permute-start | bytes 884744 | tf_op jit(solution)/shard_map/ppermute | solution.py:184
  15.0 47.8 %collective-permute-start.9 = (bf16[2,96,768]{2,1,0:T(8,128)(2,1)}, bf16[2,96,768]{2,1,0:T(8,128)(2,1)}, u32[]{:S(2)}, u32[]{:S(2)}) collective-permute-start(bf16[2,96,768]{2,1,0:T(8,128)(2,1)} %pad_maximum_fusion.34), channel_id=1, source_target_pairs={{0,1},{1,0},{2,3},{3,2},{4,5},{5,4},{6,7},{7,6},{8,9},{9,8},{10,11... | collective-permute-start | bytes 884744 | tf_op jit(solution)/shard_map/ppermute | solution.py:184
  18.3 61.1 %collective-permute-start.2 = (bf16[2,192,768]{2,1,0:T(8,128)(2,1)}, bf16[2,192,768]{2,1,0:T(8,128)(2,1)}, u32[]{:S(2)}, u32[]{:S(2)}) collective-permute-start(bf16[2,192,768]{2,1,0:T(8,128)(2,1)} %slice_select_fusion.1), channel_id=1, source_target_pairs={{0,1},{1,0},{2,3},{3,2},{4,5},{5,4},{6,7},{7,6},{8,9},{9,8},{10,11... | collective-permute-start | bytes 1769480 | tf_op jit(solution)/shard_map/ppermute | solution.py:184
  82.6 56.9 %collective-permute-start.20 = (bf16[2,192,768]{2,1,0:T(8,128)(2,1)S(1)}, bf16[2,192,768]{2,1,0:T(8,128)(2,1)S(1)}, u32[]{:S(2)}, u32[]{:S(2)}) collective-permute-start(bf16[2,192,768]{2,1,0:T(8,128)(2,1)S(1)} %copy-done.137), channel_id=1, source_target_pairs={{0,1},{1,0},{2,3},{3,2},{4,5},{5,4},{6,7},{7,6},{8,9},{9,8},{10,11... | collective-permute-start | bytes 1769480 | tf_op jit(solution)/shard_map/ppermute | solution.py:184
  86.7 57.2 %collective-permute-start.21 = (bf16[2,192,768]{2,1,0:T(8,128)(2,1)S(1)}, bf16[2,192,768]{2,1,0:T(8,128)(2,1)S(1)}, u32[]{:S(2)}, u32[]{:S(2)}) collective-permute-start(bf16[2,192,768]{2,1,0:T(8,128)(2,1)S(1)} %copy-done.137), channel_id=1, source_target_pairs={{1,2},{2,1},{5,6},{6,5},{9,10},{10,9},{13,14},{14,13},{17,18},{18,... | collective-permute-start | bytes 1769480 | tf_op jit(solution)/shard_map/ppermute | solution.py:184
  90.4 50.5 %collective-permute-start.34 = (bf16[2,96,768]{2,1,0:T(8,128)(2,1)S(1)}, bf16[2,96,768]{2,1,0:T(8,128)(2,1)S(1)}, u32[]{:S(2)}, u32[]{:S(2)}) collective-permute-start(bf16[2,96,768]{2,1,0:T(8,128)(2,1)S(1)} %copy-done.141), channel_id=1, source_target_pairs={{1,0},{2,3},{5,4},{6,7},{9,8},{10,11},{13,12},{14,15},{17,16},{18,... | collective-permute-start | bytes 884744 | tf_op jit(solution)/shard_map/ppermute | solution.py:184
  132.0 88.8 %collective-permute-start.7 = (bf16[4,2,192,768]{3,2,1,0:T(8,128)(2,1)S(1)}, bf16[4,2,192,768]{3,2,1,0:T(8,128)(2,1)S(1)}, u32[]{:S(2)}, u32[]{:S(2)}) collective-permute-start(bf16[4,2,192,768]{3,2,1,0:T(8,128)(2,1)S(1)} %pad_maximum_fusion.5), channel_id=1, source_target_pairs={{0,4},{4,0},{1,5},{5,1},{2,6},{6,2},{3,7},{7,3},{8,12},{12,8},{9,1... | collective-permute-start | bytes 7077896 | tf_op jit(solution)/shard_map/ppermute | solution.py:180
  158.8 183.1 %collective-permute-start.39 = (bf16[512,768]{1,0:T(8,128)(2,1)}, bf16[512,768]{1,0:T(8,128)(2,1)}, u32[]{:S(2)}, u32[]{:S(2)}) collective-permute-start(bf16[512,768]{1,0:T(8,128)(2,1)} %param.25), channel_id=1, source_target_pairs={{0,0},{1,4},{2,2},{3,6},{4,1},{5,5},{6,3},{7,7},{8,8},{9,12},{10,1... | collective-permute-start | bytes 2359304 | tf_op jit(solution)/shard_map/ppermute | solution.py:263
  169.7 55.6 %collective-permute-start.11 = (bf16[2,384,768]{2,1,0:T(8,128)(2,1)S(1)}, bf16[2,384,768]{2,1,0:T(8,128)(2,1)S(1)}, u32[]{:S(2)}, u32[]{:S(2)}) collective-permute-start(bf16[2,384,768]{2,1,0:T(8,128)(2,1)S(1)} %pad_maximum_fusion.19), channel_id=1, source_target_pairs={{0,16},{16,0},{1,17},{17,1},{2,18},{18,2},{3,19},{19,3},{4,20},{20... | collective-permute-start | bytes 3538952 | tf_op jit(solution)/shard_map/ppermute | solution.py:180
  170.6 48.9 %collective-permute-start.17 = (bf16[2,192,768]{2,1,0:T(8,128)(2,1)S(1)}, bf16[2,192,768]{2,1,0:T(8,128)(2,1)S(1)}, u32[]{:S(2)}, u32[]{:S(2)}) collective-permute-start(bf16[2,192,768]{2,1,0:T(8,128)(2,1)S(1)} %pad_maximum_fusion.27), channel_id=1, source_target_pairs={{0,16},{16,0},{1,17},{17,1},{2,18},{18,2},{3,19},{19,3},{4,20},{20... | collective-permute-start | bytes 1769480 | tf_op jit(solution)/shard_map/ppermute | solution.py:180
  181.5 67.8 %collective-permute-start.25 = (bf16[4,2,192,768]{3,2,1,0:T(8,128)(2,1)S(1)}, bf16[4,2,192,768]{3,2,1,0:T(8,128)(2,1)S(1)}, u32[]{:S(2)}, u32[]{:S(2)}) collective-permute-start(bf16[4,2,192,768]{3,2,1,0:T(8,128)(2,1)S(1)} %pad_maximum_fusion.8), channel_id=1, source_target_pairs={{0,4},{4,0},{1,5},{5,1},{2,6},{6,2},{3,7},{7,3},{8,12},{12,8},{9,1... | collective-permute-start | bytes 7077896 | tf_op jit(solution)/shard_map/ppermute | solution.py:180
  219.5 78.0 %collective-permute-start.29 = (bf16[2,384,768]{2,1,0:T(8,128)(2,1)}, bf16[2,384,768]{2,1,0:T(8,128)(2,1)}, u32[]{:S(2)}, u32[]{:S(2)}) collective-permute-start(bf16[2,384,768]{2,1,0:T(8,128)(2,1)} %pad_maximum_fusion.21), channel_id=1, source_target_pairs={{0,16},{16,0},{1,17},{17,1},{2,18},{18,2},{3,19},{19,3},{4,20},{20... | collective-permute-start | bytes 3538952 | tf_op jit(solution)/shard_map/ppermute | solution.py:180
  246.6 53.0 %collective-permute-start.36 = (bf16[2,384,768]{2,1,0:T(8,128)(2,1)}, bf16[2,384,768]{2,1,0:T(8,128)(2,1)}, u32[]{:S(2)}, u32[]{:S(2)}) collective-permute-start(bf16[2,384,768]{2,1,0:T(8,128)(2,1)} %pad_maximum_fusion.22), channel_id=1, source_target_pairs={{0,8},{8,0},{1,9},{9,1},{2,10},{10,2},{3,11},{11,3},{4,12},{12,4},... | collective-permute-start | bytes 3538952 | tf_op jit(solution)/shard_map/ppermute | solution.py:180
  302.0 57.2 %collective-permute-start.37 = (bf16[2,768,768]{2,1,0:T(8,128)(2,1)S(1)}, bf16[2,768,768]{2,1,0:T(8,128)(2,1)S(1)}, u32[]{:S(2)}, u32[]{:S(2)}) collective-permute-start(bf16[2,768,768]{2,1,0:T(8,128)(2,1)S(1)} %pad_maximum_fusion.10), channel_id=1, source_target_pairs={{0,4},{4,0},{1,5},{5,1},{2,6},{6,2},{3,7},{7,3},{8,12},{12,8},{9,1... | collective-permute-start | bytes 7077896 | tf_op jit(solution)/shard_map/ppermute | solution.py:180
  406.9 102.1 %collective-permute-start.78 = (bf16[2,768,768]{2,1,0:T(8,128)(2,1)}, bf16[2,768,768]{2,1,0:T(8,128)(2,1)}, u32[]{:S(2)}, u32[]{:S(2)}) collective-permute-start(bf16[2,768,768]{2,1,0:T(8,128)(2,1)} %pad_maximum_fusion.13), channel_id=1, source_target_pairs={{0,4},{4,0},{1,5},{5,1},{2,6},{6,2},{3,7},{7,3},{8,12},{12,8},{9,1... | collective-permute-start | bytes 7077896 | tf_op jit(solution)/shard_map/ppermute | solution.py:180
  410.9 105.6 %collective-permute-start.81 = (bf16[2,768,768]{2,1,0:T(8,128)(2,1)}, bf16[2,768,768]{2,1,0:T(8,128)(2,1)}, u32[]{:S(2)}, u32[]{:S(2)}) collective-permute-start(bf16[2,768,768]{2,1,0:T(8,128)(2,1)} %pad_maximum_fusion.14), channel_id=1, source_target_pairs={{0,4},{4,0},{1,5},{5,1},{2,6},{6,2},{3,7},{7,3},{8,12},{12,8},{9,1... | collective-permute-start | bytes 7077896 | tf_op jit(solution)/shard_map/ppermute | solution.py:180
  449.5 147.9 %collective-permute-start.66 = (bf16[2,768,768]{2,1,0:T(8,128)(2,1)}, bf16[2,768,768]{2,1,0:T(8,128)(2,1)}, u32[]{:S(2)}, u32[]{:S(2)}) collective-permute-start(bf16[2,768,768]{2,1,0:T(8,128)(2,1)} %pad_maximum_fusion.11), channel_id=1, source_target_pairs={{0,4},{4,0},{1,5},{5,1},{2,6},{6,2},{3,7},{7,3},{8,12},{12,8},{9,1... | collective-permute-start | bytes 7077896 | tf_op jit(solution)/shard_map/ppermute | solution.py:180
  454.6 146.7 %collective-permute-start.69 = (bf16[2,768,768]{2,1,0:T(8,128)(2,1)}, bf16[2,768,768]{2,1,0:T(8,128)(2,1)}, u32[]{:S(2)}, u32[]{:S(2)}) collective-permute-start(bf16[2,768,768]{2,1,0:T(8,128)(2,1)} %pad_maximum_fusion.12), channel_id=1, source_target_pairs={{0,4},{4,0},{1,5},{5,1},{2,6},{6,2},{3,7},{7,3},{8,12},{12,8},{9,1... | collective-permute-start | bytes 7077896 | tf_op jit(solution)/shard_map/ppermute | solution.py:180
  516.2 65.7 %collective-permute-start.79 = (bf16[2,384,768]{2,1,0:T(8,128)(2,1)}, bf16[2,384,768]{2,1,0:T(8,128)(2,1)}, u32[]{:S(2)}, u32[]{:S(2)}) collective-permute-start(bf16[2,384,768]{2,1,0:T(8,128)(2,1)} %pad_maximum_fusion.16), channel_id=1, source_target_pairs={{0,16},{16,0},{1,17},{17,1},{2,18},{18,2},{3,19},{19,3},{4,20},{20... | collective-permute-start | bytes 3538952 | tf_op jit(solution)/shard_map/ppermute | solution.py:180
  534.5 49.1 %collective-permute-start.82 = (bf16[2,384,768]{2,1,0:T(8,128)(2,1)S(1)}, bf16[2,384,768]{2,1,0:T(8,128)(2,1)S(1)}, u32[]{:S(2)}, u32[]{:S(2)}) collective-permute-start(bf16[2,384,768]{2,1,0:T(8,128)(2,1)S(1)} %pad_maximum_fusion.15), channel_id=1, source_target_pairs={{0,8},{8,0},{1,9},{9,1},{2,10},{10,2},{3,11},{11,3},{4,12},{12,4},... | collective-permute-start | bytes 3538952 | tf_op jit(solution)/shard_map/ppermute | solution.py:180
  581.9 78.1 %collective-permute-start.48 = (bf16[4,2,192,768]{3,2,1,0:T(8,128)(2,1)}, bf16[4,2,192,768]{3,2,1,0:T(8,128)(2,1)}, u32[]{:S(2)}, u32[]{:S(2)}) collective-permute-start(bf16[4,2,192,768]{3,2,1,0:T(8,128)(2,1)} %select_convert_fusion.1), channel_id=1, source_target_pairs={{0,4},{4,0},{1,5},{5,1},{2,6},{6,2},{3,7},{7,3},{8,12},{12,8},{9,1... | collective-permute-start | bytes 7077896 | tf_op jit(solution)/shard_map/ppermute | solution.py:180
  657.6 50.8 %collective-permute-start.59 = (bf16[2,2,192,768]{3,2,1,0:T(8,128)(2,1)S(1)}, bf16[2,2,192,768]{3,2,1,0:T(8,128)(2,1)S(1)}, u32[]{:S(2)}, u32[]{:S(2)}) collective-permute-start(bf16[2,2,192,768]{3,2,1,0:T(8,128)(2,1)S(1)} %add_convert_fusion.9), channel_id=1, source_target_pairs={{1,2},{2,1},{5,6},{6,5},{9,10},{10,9},{13,14},{14,13},{17,18},{18,... | collective-permute-start | bytes 3538952 | tf_op jit(solution)/shard_map/ppermute | solution.py:184
  662.8 66.5 %collective-permute-start.49 = (bf16[2,2,192,768]{3,2,1,0:T(8,128)(2,1)S(1)}, bf16[2,2,192,768]{3,2,1,0:T(8,128)(2,1)S(1)}, u32[]{:S(2)}, u32[]{:S(2)}) collective-permute-start(bf16[2,2,192,768]{3,2,1,0:T(8,128)(2,1)S(1)} %slice.573), channel_id=1, source_target_pairs={{0,1},{3,2},{4,5},{7,6},{8,9},{11,10},{12,13},{15,14},{16,17},{19,... | collective-permute-start | bytes 3538952 | tf_op jit(solution)/shard_map/ppermute | solution.py:184
  (263 other events, 4326.2 us)

commit v2 on v1

v2 whole, which is shorter than its diff:
```python
import functools

import jax
import jax.numpy as jnp
from jax import lax
from jax.experimental import pallas as pl
from jax.experimental.pallas import tpu as pltpu
from jax.sharding import Mesh, PartitionSpec as P

HD = 64
ROWS = 1024
IMAGE = 240

epsilon = 1e-06
masked_score = -1e30
bf16 = jnp.bfloat16
f32 = jnp.float32


def dot(left, right, contract):
    return lax.dot_general(
        left, right, ((contract[:1], contract[1:]), ((), ())), preferred_element_type=f32
    )


def kernel_cost(seconds):
    return pl.CostEstimate(
        flops=int(1.1535e15 * seconds), bytes_accessed=int(3.69e12 * seconds), transcendentals=0
    )


def normalize(values, gain_row, bias_row):
    average = jnp.mean(values, axis=-1, keepdims=True)
    centred = values - average
    variance = jnp.mean(centred * centred, axis=-1, keepdims=True)
    return centred * lax.rsqrt(variance + epsilon) * gain_row + bias_row


def gelu_pair(values):
    size = jnp.abs(values)
    knot = 1.0 / (1.0 + (0.3275911 * 0.5**0.5) * size)
    bell = jnp.exp(values * values * -0.5)
    series = knot * (
        0.127414796
        + knot * (-0.142248368 + knot * (0.7107068705 + knot * (-0.7265760135 + knot * 0.5307027145)))
    )
    tail = series * bell
    normal = jnp.where(values > 0, 1.0 - tail, tail)
    return values * normal, normal + values * bell * 0.3989422804014327


def key_halves(core, own, received):
    first = jnp.where(core == 0, own, received)
    second = jnp.where(core == 0, received, own)
    return first, second


def attend_forward_kernel(info, queries, kv_own, kv_other, mixed, log_total):
    core, valid = info[0], info[1]
    width = queries.shape[0]
    half = kv_own.shape[1]
    key_place = lax.broadcasted_iota(jnp.int32, (half, 1), 0) + half
    key_bias = jnp.where(key_place < valid, 0.0, masked_score).astype(f32)
    for head in range(width // HD):
        rows = slice(head * HD, (head + 1) * HD)
        value_rows = slice(width + head * HD, width + (head + 1) * HD)
        query = queries[rows, :] * jnp.asarray(HD**-0.5, bf16)
        key_one, key_two = key_halves(core, kv_own[rows, :], kv_other[rows, :])
        value_one, value_two = key_halves(core, kv_own[value_rows, :], kv_other[value_rows, :])
        score_one = dot(key_one, query, (0, 0))
        score_two = dot(key_two, query, (0, 0)) + key_bias
        top = jnp.maximum(
            jnp.max(score_one, axis=0, keepdims=True), jnp.max(score_two, axis=0, keepdims=True)
        )
        weight_one = jnp.exp(score_one - top)
        weight_two = jnp.exp(score_two - top)
        total = jnp.sum(weight_one, axis=0, keepdims=True) + jnp.sum(
            weight_two, axis=0, keepdims=True
        )
        out = dot(value_one, weight_one.astype(bf16), (1, 0)) + dot(
            value_two, weight_two.astype(bf16), (1, 0)
        )
        mixed[rows, :] = (out / total).astype(bf16)
        log_total[0, head : head + 1, :] = top + jnp.log(total)


def attend_backward_kernel(
    info, queries, kv_own, kv_other, mixed, log_total, grad_mixed, grad_q, grad_own, grad_other
):
    core, valid = info[0], info[1]
    width = queries.shape[0]
    half = kv_own.shape[1]
    scale = HD**-0.5
    key_place = lax.broadcasted_iota(jnp.int32, (half, 1), 0) + half
    key_bias = jnp.where(key_place < valid, 0.0, masked_score).astype(f32)
    for head in range(width // HD):
        rows = slice(head * HD, (head + 1) * HD)
        value_rows = slice(width + head * HD, width + (head + 1) * HD)
        query = queries[rows, :] * jnp.asarray(scale, bf16)
        grad_out = grad_mixed[rows, :]
        delta = jnp.sum(
            grad_out.astype(f32) * mixed[rows, :].astype(f32), axis=0, keepdims=True
        )
        log_row = log_total[0, head : head + 1, :]
        keys = key_halves(core, kv_own[rows, :], kv_other[rows, :])
        values = key_halves(core, kv_own[value_rows, :], kv_other[value_rows, :])
        grad_query = None
        grad_keys = []
        grad_values = []
        for part in range(2):
            score = dot(keys[part], query, (0, 0))
            if part == 1:
                score = score + key_bias
            probs = jnp.exp(score - log_row)
            grad_values.append(dot(grad_out, probs.astype(bf16), (1, 1)))
            grad_probs = dot(values[part], grad_out, (0, 0))
            grad_score = (probs * (grad_probs - delta)).astype(bf16)
            term = dot(keys[part], grad_score, (1, 0))
            grad_query = term if grad_query is None else grad_query + term
            grad_keys.append(dot(query, grad_score, (1, 1)))
        grad_q[rows, :] = (grad_query * scale).astype(bf16)
        own, other = key_halves(core, *grad_keys)
        grad_own[rows, :] = own
        grad_other[rows, :] = other.astype(bf16)
        own, other = key_halves(core, *grad_values)
        grad_own[value_rows, :] = own
        grad_other[value_rows, :] = other.astype(bf16)


def attention_specs(groups, width, half):
    return dict(
        q=pl.BlockSpec((width, half), lambda g, info: (g, 0)),
        kv=pl.BlockSpec((2 * width, half), lambda g, info: (g, 0)),
        log=pl.BlockSpec((1, 8, half), lambda g, info: (g, 0, 0)),
    )


def attend_forward(info, queries, kv_own, kv_other, groups):
    features, half = queries.shape
    width = features // groups
    specs = attention_specs(groups, width, half)
    return pl.pallas_call(
        attend_forward_kernel,
        grid_spec=pltpu.PrefetchScalarGridSpec(
            num_scalar_prefetch=1,
            grid=(groups,),
            in_specs=[specs["q"], specs["kv"], specs["kv"]],
            out_specs=[specs["q"], specs["log"]],
        ),
        out_shape=[
            jax.ShapeDtypeStruct((features, half), bf16),
            jax.ShapeDtypeStruct((groups, 8, half), f32),
        ],
        compiler_params=pltpu.CompilerParams(vmem_limit_bytes=40 << 20),
        cost_estimate=kernel_cost(14e-6),
        name="attend_forward",
    )(info, queries, kv_own, kv_other)


def attend_backward(info, queries, kv_own, kv_other, mixed, log_total, grad_mixed, groups):
    features, half = queries.shape
    width = features // groups
    specs = attention_specs(groups, width, half)
    return pl.pallas_call(
        attend_backward_kernel,
        grid_spec=pltpu.PrefetchScalarGridSpec(
            num_scalar_prefetch=1,
            grid=(groups,),
            in_specs=[specs["q"], specs["kv"], specs["kv"], specs["q"], specs["log"], specs["q"]],
            out_specs=[specs["q"], specs["kv"], specs["kv"]],
        ),
        out_shape=[
            jax.ShapeDtypeStruct((features, half), bf16),
            jax.ShapeDtypeStruct((2 * features, half), f32),
            jax.ShapeDtypeStruct((2 * features, half), bf16),
        ],
        compiler_params=pltpu.CompilerParams(vmem_limit_bytes=40 << 20),
        cost_estimate=kernel_cost(21e-6),
        name="attend_backward",
    )(info, queries, kv_own, kv_other, mixed, log_total, grad_mixed)


def stream_pieces(pieces, buffer, arrived):
    step = pl.program_id(0)
    rows = buffer.shape[1]

    def copy(index):
        source, offset = pieces[index]
        return pltpu.make_async_copy(
            source.at[pl.ds(offset, rows), :], buffer.at[index % 2], arrived.at[index % 2]
        )

    @pl.when(step == 0)
    def _():
        copy(0).start()

    for index in range(len(pieces) - 1):

        @pl.when(step == index)
        def _(index=index):
            copy(index + 1).start()

    for index in range(len(pieces)):

        @pl.when(step == index)
        def _(index=index):
            copy(index).wait()

    return lax.rem(step, 2)


def list_pieces(refs, rows):
    return [(ref, start) for ref in refs for start in range(0, ref.shape[0], rows)]


def units_forward_kernel(count, rows, normed, middle, unit_bias, down_bias, *refs):
    weights = refs[:count]
    activated, slopes, result, buffer, arrived = refs[count:]
    slot = stream_pieces(list_pieces(weights, rows), buffer, arrived)
    width = normed.shape[1]
    pre = dot(normed[...], buffer[slot, :, :width], (1, 1)) + unit_bias[0]
    act, slope = gelu_pair(pre)
    act = act.astype(bf16)
    activated[...] = act
    slopes[...] = slope.astype(bf16)

    @pl.when(pl.program_id(0) == 0)
    def _():
        result[...] = middle[...] + down_bias[...]

    result[...] += dot(act, buffer[slot, :, width:], (1, 0))


def units_forward(normed, middle, unit_bias, down_bias, weights):
    tokens, width = normed.shape
    rows = unit_bias.shape[1]
    steps = unit_bias.shape[0]
    units = rows * steps
    whole = pl.BlockSpec((tokens, width), lambda i: (0, 0))
    block = pl.BlockSpec((tokens, rows), lambda i: (0, i))
    return pl.pallas_call(
        functools.partial(units_forward_kernel, len(weights), rows),
        grid=(steps,),
        in_specs=[
            whole,
            whole,
            pl.BlockSpec((1, 1, rows), lambda i: (i, 0, 0)),
            pl.BlockSpec((1, width), lambda i: (0, 0)),
        ]
        + [pl.BlockSpec(memory_space=pl.ANY)] * len(weights),
        out_specs=[block, block, whole],
        out_shape=[
            jax.ShapeDtypeStruct((tokens, units), bf16),
            jax.ShapeDtypeStruct((tokens, units), bf16),
            jax.ShapeDtypeStruct((tokens, width), f32),
        ],
        scratch_shapes=[
            pltpu.VMEM((2, rows, 2 * width), bf16),
            pltpu.SemaphoreType.DMA((2,)),
        ],
        compiler_params=pltpu.CompilerParams(vmem_limit_bytes=40 << 20),
        cost_estimate=kernel_cost(17e-6),
        name="units_forward",
    )(normed, middle, unit_bias[:, None, :], down_bias, *weights)


def stream_blocks(place, source, buffer, arrived):
    step = pl.program_id(0)
    rows = buffer.shape[1]

    def copy(index):
        offset = pl.multiple_of(place[index] * rows, rows)
        slot = lax.rem(index, 2)
        return pltpu.make_async_copy(
            source.at[pl.ds(offset, rows), :], buffer.at[slot], arrived.at[slot]
        )

    @pl.when(step == 0)
    def _():
        copy(0).start()

    @pl.when(step + 1 < pl.num_programs(0))
    def _():
        copy(step + 1).start()

    copy(step).wait()
    return lax.rem(step, 2)


def units_backward_kernel(count, rows, place, grad_down, normed, activated, slopes, *refs):
    weights = refs[:count]
    sent, kept, grad_normed, bias_grad, buffer, arrived = refs[count:]
    step = pl.program_id(0)
    if count == 1:
        slot = stream_blocks(place, weights[0], buffer, arrived)
    else:
        slot = stream_pieces(list_pieces(weights, rows), buffer, arrived)
    width = normed.shape[1]
    grad_act = dot(grad_down[...], buffer[slot, :, width:], (1, 1))
    grad_hidden = grad_act * slopes[...].astype(f32)
    bias_grad[0] = jnp.sum(grad_hidden, axis=0, keepdims=True)
    grad_hidden = grad_hidden.astype(bf16)

    @pl.when(step == 0)
    def _():
        grad_normed[...] = jnp.zeros_like(grad_normed)

    grad_normed[...] += dot(grad_hidden, buffer[slot, :, :width], (1, 0))
    up = dot(grad_hidden, normed[...], (0, 0)).astype(bf16)
    down = dot(activated[...], grad_down[...], (0, 0)).astype(bf16)

    def store(target):
        target[:, :width] = up
        target[:, width:] = down

    half = pl.num_programs(0) // 2
    pl.when(step < half)(lambda: store(sent))
    pl.when(step >= half)(lambda: store(kept))


def units_backward(place, grad_down, normed, activated, slopes, weights, rows):
    tokens, width = normed.shape
    units = activated.shape[1]
    steps = units // rows
    half = steps // 2
    whole = pl.BlockSpec((tokens, width), lambda i, place: (0, 0))
    block = pl.BlockSpec((tokens, rows), lambda i, place: (0, place[i]))
    return pl.pallas_call(
        functools.partial(units_backward_kernel, len(weights), rows),
        grid_spec=pltpu.PrefetchScalarGridSpec(
            num_scalar_prefetch=1,
            grid=(steps,),
            in_specs=[whole, whole, block, block]
            + [pl.BlockSpec(memory_space=pl.ANY)] * len(weights),
            out_specs=[
                pl.BlockSpec((rows, 2 * width), lambda i, place: (jnp.minimum(i, half - 1), 0)),
                pl.BlockSpec((rows, 2 * width), lambda i, place: (jnp.maximum(i - half, 0), 0)),
                whole,
                pl.BlockSpec((1, 1, rows), lambda i, place: (place[i], 0, 0)),
            ],
            scratch_shapes=[
                pltpu.VMEM((2, rows, 2 * width), bf16),
                pltpu.SemaphoreType.DMA((2,)),
            ],
        ),
        out_shape=[jax.ShapeDtypeStruct((units // 2, 2 * width), bf16)] * 2
        + [
            jax.ShapeDtypeStruct((tokens, width), f32),
            jax.ShapeDtypeStruct((steps, 1, rows), f32),
        ],
        compiler_params=pltpu.CompilerParams(vmem_limit_bytes=40 << 20),
        cost_estimate=kernel_cost(20e-6),
        name="units_backward",
    )(place, grad_down, normed, activated, slopes, *weights)


def norm_backward_kernel(last, values, grad, kept, gain, *refs):
    if last:
        earlier, others, result, packed, sums = refs[:3], refs[3], *refs[4:]
    else:
        result, low, sums = refs
    step = pl.program_id(0)
    block = values[...]
    average = jnp.mean(block, axis=-1, keepdims=True)
    centred = block - average
    scale = lax.rsqrt(jnp.mean(centred * centred, axis=-1, keepdims=True) + epsilon)
    unit = centred * scale
    down = grad[...]
    inner = down * gain[...]
    total = kept[...] + scale * (
        inner
        - jnp.mean(inner, axis=-1, keepdims=True)
        - unit * jnp.mean(inner * unit, axis=-1, keepdims=True)
    )
    result[...] = total

    @pl.when(step == 0)
    def _():
        sums[...] = jnp.zeros_like(sums)

    sums[0:1, :] += jnp.sum(down * unit, axis=0, keepdims=True)
    sums[1:2, :] += jnp.sum(down, axis=0, keepdims=True)
    if not last:
        rounded = total.astype(bf16)
        low[...] = rounded
        sums[2:3, :] += jnp.sum(rounded.astype(f32), axis=0, keepdims=True)
    else:

        @pl.when(step == pl.num_programs(0) - 1)
        def _():
            rows = jnp.concatenate(
                [ref[0:3, :] for ref in earlier] + [sums[0:2, :], others[...]]
            )
            high = rows.astype(bf16)
            packed[0 : rows.shape[0], :] = high
            packed[rows.shape[0] :, :] = (rows - high.astype(f32)).astype(bf16)


def norm_backward(values, grad, kept, gain, *rows):
    tokens, width = values.shape
    steps = 4
    block = pl.BlockSpec((tokens // steps, width), lambda i: (i, 0))

    def whole(count):
        return pl.BlockSpec((count, width), lambda i: (0, 0))

    last = bool(rows)
    if last:
        count = 2 * (11 + rows[-1].shape[0])
        out_specs = [block, whole(count)]
        out_shape = [
            jax.ShapeDtypeStruct((tokens, width), f32),
            jax.ShapeDtypeStruct((count, width), bf16),
        ]
        scratch = [pltpu.VMEM((8, width), f32)]
    else:
        out_specs = [block, block, whole(8)]
        out_shape = [
            jax.ShapeDtypeStruct((tokens, width), f32),
            jax.ShapeDtypeStruct((tokens, width), bf16),
            jax.ShapeDtypeStruct((8, width), f32),
        ]
        scratch = []
    return pl.pallas_call(
        functools.partial(norm_backward_kernel, last),
        grid=(steps,),
        in_specs=[block, block, block, whole(1)] + [whole(row.shape[0]) for row in rows],
        out_specs=out_specs,
        out_shape=out_shape,
        scratch_shapes=scratch,
        compiler_params=pltpu.CompilerParams(vmem_limit_bytes=24 << 20),
        cost_estimate=kernel_cost(3e-6),
        name="norm_backward",
    )(values, grad, kept, gain, *rows)


def unit_results_kernel(own, even, up, down):
    width = down.shape[2]
    for layer, grads in enumerate((own, even)):
        up[layer] = grads[:, :width].astype(f32).T
        down[layer] = grads[:, width:].astype(f32)


def unit_results(own, even):
    units, double = own.shape
    width = double // 2
    steps = 3
    block = pl.BlockSpec((units // steps, double), lambda i: (i, 0))
    return pl.pallas_call(
        unit_results_kernel,
        grid=(steps,),
        in_specs=[block, block],
        out_specs=[
            pl.BlockSpec((2, width, units // steps), lambda i: (0, 0, i)),
            pl.BlockSpec((2, units // steps, width), lambda i: (0, i, 0)),
        ],
        out_shape=[
            jax.ShapeDtypeStruct((2, width, units), f32),
            jax.ShapeDtypeStruct((2, units, width), f32),
        ],
        compiler_params=pltpu.CompilerParams(vmem_limit_bytes=24 << 20),
        cost_estimate=kernel_cost(5e-6),
        name="unit_results",
    )(own, even)


flip_pair = [(0, 1), (1, 0)]


def over(axis, array):
    return lax.ppermute(array, axis, flip_pair)


def z_send(array, pairs):
    return lax.ppermute(array, "z", pairs)


def z_pairs(step):
    return [(z, z ^ step) for z in range(4)]


def z_three(blocks):
    return [lax.ppermute(block, "z", z_pairs(step + 1)) for step, block in enumerate(blocks)]


def yx_three(blocks):
    across = [(place, 3 - place) for place in range(4)]
    return [
        over("x", blocks[0]),
        over("y", blocks[1]),
        lax.ppermute(blocks[2], ("y", "x"), across),
    ]


def add_low(*terms):
    total = terms[0].astype(f32)
    for term in terms[1:]:
        total = total + term.astype(f32)
    return total.astype(bf16)


def together(*arrays):
    return lax.optimization_barrier(arrays)


def tie(array, *after):
    return lax.optimization_barrier((array, after))[0]


def flip_if(bit, array, axis):
    return jnp.where(bit == 1, jnp.flip(array, axis), array)


def paired(bit, own, received, axis):
    return jnp.stack(
        [jnp.where(bit == 0, own, received), jnp.where(bit == 0, received, own)], axis=axis
    )


def local(
    stream_in,
    patch_size,
    norm_gain,
    norm_bias,
    input_weight,
    input_bias,
    output_weight,
    output_bias,
    up_weight,
    up_bias,
    down_weight,
    down_bias,
    cotangent,
):
    half, width_all = stream_in.shape
    layer_count = input_weight.shape[0]
    shard = input_weight.shape[-1]
    unit_shard = up_weight.shape[-1]
    unit_slice = unit_shard // 8
    groups = lax.axis_size("z")
    outer = lax.axis_size("o")
    core, x_bit, y_bit = lax.axis_index("c"), lax.axis_index("x"), lax.axis_index("y")
    z_place = lax.axis_index("z")
    z_low, z_high = z_place % 2, z_place // 2

    swap = []
    for c in range(2):
        for z in range(groups):
            if c != z % 2:
                swap.append((c * groups + z, (z % 2) * groups + (z - z % 2 + c)))

    def swap_rows(array):
        return jnp.where(z_low == core, array, lax.ppermute(array, ("c", "z"), swap))

    other_patch = over("c", patch_size)
    patch = jnp.where(z_low == core, patch_size, other_patch)
    patch = jnp.where(z_high == 0, patch[0], patch[1])
    grid_side = IMAGE // patch
    valid = grid_side * grid_side
    info = jnp.stack([core, valid]).astype(jnp.int32)

    stream_rows = swap_rows(stream_in)

    def z_order(array):
        pairs = array.reshape((2, 2) + array.shape[1:])
        pairs = flip_if(z_high, flip_if(z_low, pairs, 1), 0)
        return pairs.reshape(array.shape)

    def unit_flip(cut):
        cut = flip_if(z_high, flip_if(z_low, cut, 1), 0)
        return flip_if(y_bit, flip_if(x_bit, flip_if(core, cut, 4), 3), 2)

    def own_order(rows):
        cut = unit_flip(rows.reshape(2, 2, 2, 2, 2, unit_slice))
        cut = jnp.stack([cut[0].transpose(3, 1, 2, 0, 4), cut[1].transpose(3, 2, 1, 0, 4)], axis=1)
        return cut[::-1].reshape(8, unit_shard // 2)

    def own_order_back(pieces):
        cut = pieces.reshape(2, 2, 2, 2, 2, unit_slice)[::-1]
        cut = jnp.stack([cut[:, 0].transpose(3, 1, 2, 0, 4), cut[:, 1].transpose(3, 2, 1, 0, 4)])
        return unit_flip(cut).reshape(groups, unit_shard)

    def even_order(rows):
        cut = rows.reshape(groups, 8, unit_slice).transpose(1, 0, 2)
        return cut.reshape(8, unit_shard // 2)

    def even_order_back(pieces):
        cut = pieces.reshape(8, groups, unit_slice).transpose(1, 0, 2)
        return cut.reshape(groups, unit_shard)

    slice_index = (y_bit * 2 + x_bit) * 2 + core

    part = shard // 2

    def attention_slice(layer_idx):
        first = jnp.where(core == 0, input_weight[layer_idx, 1], input_weight[layer_idx, 0]).T
        second = jnp.where(core == 0, input_weight[layer_idx, 2].T, output_weight[layer_idx])
        return jnp.concatenate(
            [
                lax.dynamic_slice_in_dim(first, x_bit * part, part, axis=0),
                lax.dynamic_slice_in_dim(second, y_bit * part, part, axis=0),
            ]
        )

    def attention_halves(blocks):
        return (
            jnp.stack([block[:part] for block in blocks]),
            jnp.stack([block[part : 2 * part] for block in blocks]),
        )

    def attention_own(first, second, received):
        first = paired(x_bit, first, received[0], 1).reshape(groups, shard, width_all)
        second = paired(y_bit, second, received[1], 1).reshape(groups, shard, width_all)
        return jnp.stack([first, second], axis=1)

    def attention_whole(own):
        received = over("c", own)
        kv = jnp.where(core == 0, own, received)
        qo = jnp.where(core == 0, received, own)
        return (
            kv.reshape(2 * groups * shard, width_all),
            qo[:, 0].reshape(groups * shard, width_all),
            qo[:, 1].reshape(groups * shard, width_all),
        )

    def unit_block(layer_idx):
        up = lax.dynamic_slice_in_dim(
            up_weight[layer_idx], slice_index * unit_slice, unit_slice, axis=1
        )
        down = lax.dynamic_slice_in_dim(
            down_weight[layer_idx], slice_index * unit_slice, unit_slice, axis=0
        )
        return jnp.concatenate([up.T, down], axis=1)

    small_bias = input_bias.reshape(-1, unit_shard)
    bias_count = layer_count + small_bias.shape[0]
    bias_rows = jnp.pad(up_bias, ((0, 16 - layer_count), (0, 0))) + jnp.pad(
        small_bias, ((layer_count, 16 - bias_count), (0, 0))
    )
    everyone = ("y", "x", "c", "z")
    block = jnp.concatenate([attention_slice(0), bias_rows])
    first_blocks = z_three([block] * 3)
    blocks = [block] + first_blocks
    biases = jnp.stack([block[2 * part :] for block in blocks]).astype(f32)
    first, second = attention_halves(blocks)
    own_attention = attention_own(first, second, [over("x", first), over("y", second)])
    block = tie(unit_block(0), first, second)
    unit_blocks = z_three([block] * 3)
    first_weights = attention_whole(own_attention)
    one = tie(jnp.concatenate([block, unit_blocks[0]]), first_weights[0])
    two = tie(jnp.concatenate(unit_blocks[1:]), first_weights[0])
    one = jnp.concatenate([one, over("x", one)])
    two = jnp.concatenate([two, over("y", two)])
    near_units = [over("y", one), over("x", two)]
    even_units = lax.all_gather(
        tie(unit_block(1), *first_blocks), everyone, axis=0, tiled=True
    )
    attention_weights = [first_weights, None]
    unit_weights = [None, [even_units]]
    up_bias_all = z_order(biases[:, :layer_count])
    input_bias_all = biases[:, layer_count : layer_count + input_bias.size // unit_shard].reshape(
        groups, layer_count, 2, shard
    )
    gains = norm_gain.astype(f32)
    shifts = norm_bias.astype(f32)

    stream = stream_rows.astype(f32)
    saved = []
    for layer_idx in range(layer_count):
        if layer_idx == 1:
            attention_weights[1] = attention_whole(own_attention)
            cotangent_rows = swap_rows(tie(cotangent, own_attention))
        weight_kv, weight_q, weight_o = attention_weights[layer_idx]
        layer_input = stream
        normed = normalize(stream, gains[layer_idx, 0], shifts[layer_idx, 0]).astype(bf16)
        value_bias = input_bias_all[:, layer_idx, 1]
        kv_bias = jnp.stack([jnp.zeros_like(value_bias), value_bias], axis=1).reshape(-1, 1)
        kv_own = (dot(weight_kv, normed, (1, 1)) + kv_bias).astype(bf16)
        if layer_idx == 0:
            later_block = tie(attention_slice(1), kv_own)
            later_blocks = z_three([later_block] * 3)
        kv_other = over("c", kv_own)
        query_bias = input_bias_all[:, layer_idx, 0].reshape(-1, 1)
        queries = (dot(weight_q, normed, (1, 1)) + query_bias).astype(bf16)
        mixed, log_total = attend_forward(info, queries, kv_own, kv_other, groups)
        if layer_idx == 0:
            mixed, log_total, near_units, later_blocks = together(
                mixed, log_total, near_units, later_blocks
            )
            pieces = [one, near_units[0], two, near_units[1]]
            unit_weights[0] = [over("c", piece) for piece in pieces] + pieces
            first, second = attention_halves([later_block, *later_blocks])
        middle = stream + (
            dot(mixed, weight_o, (0, 0)) + output_bias[layer_idx].astype(f32)
        )
        normed_two = normalize(middle, gains[layer_idx, 1], shifts[layer_idx, 1]).astype(bf16)
        order = own_order if layer_idx == 0 else even_order
        if layer_idx == 0:
            unit_weights[0], normed_two, first, second = together(
                unit_weights[0], normed_two, first, second
            )
            received = [over("x", first), over("y", second)]
        activated, slopes, stream = units_forward(
            normed_two,
            middle,
            order(up_bias_all[:, layer_idx]),
            down_bias[layer_idx].astype(f32)[None, :],
            unit_weights[layer_idx],
        )
        if layer_idx == 0:
            activated, slopes, stream, received = together(activated, slopes, stream, received)
            own_attention = attention_own(first, second, received)
        saved.append(
            (
                layer_input,
                middle,
                normed,
                queries,
                kv_own,
                kv_other,
                log_total,
                mixed,
                normed_two,
                slopes,
                activated,
            )
        )
    layer_rows = stream.astype(bf16)

    row_place = core * half + jnp.arange(half, dtype=jnp.int32)
    row_mask = (row_place < valid).astype(f32)[:, None]
    grad_stream = cotangent_rows.astype(f32) * row_mask

    slab = (4, unit_shard // 2, 2 * width_all)
    strip = unit_shard // 4
    thin = (2, unit_slice, 2 * width_all)

    def own_first(kept, received):
        kept, received = kept.reshape(slab), received.reshape(slab)
        parts = [add_low(kept[k], received[k]) for k in range(4)]
        return [parts[0], parts[2]], [parts[1], parts[3]]

    def even_first(kept, received):
        kept, received = kept.reshape(slab), received.reshape(slab)

        def part(rows, blocks):
            return add_low(
                jnp.concatenate([kept[k, rows] for k in blocks]),
                jnp.concatenate([received[k, rows] for k in blocks]),
            )

        one, two = slice(0, strip), slice(strip, 2 * strip)
        return [part(one, (0, 1)), part(two, (0, 2))], [part(one, (2, 3)), part(two, (1, 3))]

    def unit_second(parts, received):
        kept, sent = [], []
        for part, other in zip(parts, received):
            kept.append(add_low(part[:strip], other[:strip]).reshape(thin))
            sent.append(add_low(part[strip:], other[strip:]).reshape(thin))
        return kept, sent

    def own_third(parts, received):
        one, two = [add_low(*pair) for pair in zip(parts, received)]
        return [one[0], one[1], two[0], two[1]]

    def even_third(parts, received):
        total = jnp.concatenate([add_low(*pair) for pair in zip(parts, received)])
        return [
            lax.dynamic_index_in_dim(total, z_place ^ step, axis=0, keepdims=False)
            for step in range(4)
        ]

    def over_outer(total):
        return lax.psum(total, "o") if outer > 1 else total

    def gather_shard(total):
        return lax.all_gather(total, everyone[:3], axis=0, tiled=True)

    def attention_parts(grad_kv, grad_q, grad_o):
        kv = grad_kv.reshape(groups, 2, shard, width_all)
        qo = jnp.stack(
            [
                grad_q.reshape(groups, shard, width_all),
                grad_o.reshape(groups, shard, width_all),
            ],
            axis=1,
        )
        sent = jnp.where(core == 0, qo, kv)
        kept = jnp.where(core == 0, kv, qo)
        return sent, kept

    quarter = shard // 4
    rest = 2 * quarter

    def attention_first(total):
        cut = total.reshape(groups, 2, 2, 2, quarter, width_all)
        one, two = cut[:, 0], cut[:, 1]

        def pick(array, index, axis):
            return lax.dynamic_index_in_dim(array, index, axis, keepdims=False)

        kept = [pick(one, y_bit, 1), pick(two, x_bit, 2)]
        return kept, [pick(one, 1 - y_bit, 1), pick(two, 1 - x_bit, 2)]

    def attention_second(parts, received):
        kept, sent = [], []
        for part, other, bit in zip(parts, received, (x_bit, y_bit)):
            total = add_low(part, other)
            kept.append(lax.dynamic_index_in_dim(total, bit, 1, keepdims=False))
            sent.append(lax.dynamic_index_in_dim(total, 1 - bit, 1, keepdims=False))
        return kept, sent

    def attention_third(parts, received):
        total = jnp.concatenate([add_low(*pair) for pair in zip(parts, received)], axis=1)
        return [total[step] for step in range(4)]

    def attention_gathered(rows):
        cut = rows.reshape(4, 2, 2, quarter, width_all).transpose(1, 2, 0, 3, 4).astype(f32)
        cut = cut.reshape(2, 2, shard, width_all)
        weight_in = jnp.stack([cut[1, 0], cut[0, 0], cut[0, 1]])
        return jnp.swapaxes(weight_in, 1, 2), cut[1, 1]

    def attention_out(whole, received):
        cut = (2, shard, width_all)
        total = paired(core, whole.reshape(cut), received.reshape(cut), 0).astype(f32)
        weight_in = jnp.stack([total[1, 0], total[0, 0], total[0, 1]])
        return jnp.swapaxes(weight_in, 1, 2), total[1, 1]

    def attention_cuts(kept, received):
        place = y_bit * 2 + x_bit

        def cut(array, step):
            return lax.dynamic_slice_in_dim(array, (place ^ step) * quarter, quarter, axis=2)

        return [add_low(cut(kept, step), cut(received, step)) for step in range(4)]

    def attention_sum(cuts, received):
        return add_low(cuts[0], *received).reshape(4, rest, width_all)

    def attention_join(blocks):
        whole = jnp.stack(blocks).reshape(2, 2, 2, quarter, width_all)
        whole = flip_if(y_bit, flip_if(x_bit, whole, 1), 0)
        return whole.transpose(2, 0, 1, 3, 4).reshape(2 * shard, width_all)

    def pack(rows):
        high = rows.astype(bf16)
        low = (rows - lax.optimization_barrier(high).astype(f32)).astype(bf16)
        return lax.optimization_barrier(jnp.concatenate([high, low]))

    def unpack(rows):
        count = rows.shape[0] // 2
        return rows[:count].astype(f32) + rows[count:].astype(f32)

    def four(own, received):
        one, two, three = received
        return (unpack(own) + unpack(one)) + (unpack(two) + unpack(three))

    grad_down = grad_stream.astype(bf16)
    other_rows = [jnp.sum(grad_down.astype(f32), axis=0, keepdims=True)]
    sum_rows = []
    for layer_idx in reversed(range(layer_count)):
        (
            layer_input,
            middle,
            normed,
            queries,
            kv_own,
            kv_other,
            log_total,
            mixed,
            normed_two,
            slopes,
            activated,
        ) = saved[layer_idx]
        weight_kv, weight_q, weight_o = attention_weights[layer_idx]
        first = layer_idx == 0
        steps = jnp.arange(8, dtype=jnp.int32)
        if first:
            place = steps
            later, later_sent = attention_first(add_low(attention_kept, attention_received))
            even_cuts = even_third(unit_parts, unit_received)
            grad_down, later, later_sent, even_cuts = together(
                grad_down, later, later_sent, even_cuts
            )
            later_received = [over("y", later_sent[0]), over("x", later_sent[1])]
            even_received = z_three(even_cuts[1:])
        else:
            place = slice_index ^ ((steps % 4) * 2 + (1 - steps // 4))
        grads = units_backward(
            place,
            grad_down,
            normed_two,
            activated,
            slopes,
            unit_weights[layer_idx],
            unit_shard // 2,
        )
        if first:
            grads, later_received, even_received = together(grads, later_received, even_received)
            later, later_sent = attention_second(later, later_received)
            even_total = over_outer(add_low(even_cuts[0], *even_received))
            grads, later, later_sent, even_total = together(grads, later, later_sent, even_total)
            later_received = [over("x", later_sent[0]), over("y", later_sent[1])]
            even_grads = gather_shard(even_total)
        unit_sent, unit_kept, grad_normed_two, up_bias_grad = grads
        unit_received = over("c", unit_sent)
        order_back = own_order_back if first else even_order_back
        other_rows.append(order_back(up_bias_grad))
        grad_middle, grad_branch, rows = norm_backward(
            middle, grad_normed_two, grad_stream, gains[layer_idx, 1][None, :]
        )
        sum_rows.append(rows)
        grad_o = dot(mixed, grad_branch, (1, 0)).astype(bf16)
        grad_mixed = dot(weight_o, grad_branch, (1, 1)).astype(bf16)
        grad_mixed, grad_o, unit_received = together(grad_mixed, grad_o, unit_received)
        unit_parts, unit_sent = (own_first if first else even_first)(unit_kept, unit_received)
        if first:
            later_received = tie(later_received, grad_mixed)
            later_cuts = attention_third(later, later_received)
            grad_mixed, unit_parts, unit_sent, later_cuts = together(
                grad_mixed, unit_parts, unit_sent, later_cuts
            )
            later_received = z_three(later_cuts[1:])
        else:
            grad_mixed, unit_parts, unit_sent, layer_rows = together(
                grad_mixed, unit_parts, unit_sent, layer_rows
            )
            layer_out = swap_rows(layer_rows)
        unit_received = [over("y", unit_sent[0]), over("x", unit_sent[1])]
        outs = attend_backward(
            info, queries, kv_own, kv_other, mixed, log_total, grad_mixed, groups
        )
        outs, unit_received = together(outs, unit_received)
        unit_parts, unit_sent = unit_second(unit_parts, unit_received)
        if first:
            later_received = tie(later_received, outs[0])
            later_total = over_outer(add_low(later_cuts[0], *later_received))
            outs, unit_parts, unit_sent, later_total = together(
                outs, unit_parts, unit_sent, later_total
            )
            later_grads = gather_shard(later_total)
        else:
            outs, unit_parts, unit_sent, layer_out = together(
                outs, unit_parts, unit_sent, layer_out
            )
        unit_received = [over("x", unit_sent[0]), over("y", unit_sent[1])]
        grad_queries, grad_kv_own, grad_kv_other = outs
        grad_kv = add_low(grad_kv_own, over("c", grad_kv_other))
        grad_q = dot(grad_queries, normed, (1, 0)).astype(bf16)
        grad_kv_weight = dot(grad_kv, normed, (1, 0)).astype(bf16)
        attention_sent, attention_kept = attention_parts(grad_kv_weight, grad_q, grad_o)
        attention_received = over("c", attention_sent)
        query_bias_grad = jnp.sum(grad_queries.astype(f32), axis=1)
        value_bias_grad = jnp.sum(
            grad_kv.reshape(groups, 2, shard, half)[:, 1].astype(f32), axis=-1
        )
        other_rows.append(z_order(query_bias_grad.reshape(groups, shard)).reshape(1, -1))
        other_rows.append(z_order(value_bias_grad).reshape(1, -1))
        grad_normed = dot(grad_queries, weight_q, (0, 0)) + dot(grad_kv, weight_kv, (0, 0))
        if first:
            other_rows = jnp.concatenate(other_rows)
            grad_normed, attention_received, unit_received, other_rows = together(
                grad_normed, attention_received, unit_received, other_rows
            )
            cuts = attention_cuts(attention_kept, attention_received)
            unit_cuts = own_third(unit_parts, unit_received)
            grad_normed, cuts, unit_cuts = together(grad_normed, cuts, unit_cuts)
            received = yx_three(cuts[1:])
            unit_received = z_three(unit_cuts[1:])
            grad_stream, small = norm_backward(
                layer_input,
                grad_normed,
                grad_middle,
                gains[layer_idx, 0][None, :],
                *sum_rows,
                other_rows,
            )
        else:
            grad_stream, grad_down, rows = norm_backward(
                layer_input, grad_normed, grad_middle, gains[layer_idx, 0][None, :]
            )
            sum_rows.append(rows)
            grad_stream, grad_down, attention_received, unit_received = together(
                grad_stream, grad_down, attention_received, unit_received
            )
    width = width_all
    grad_stream, small, received, unit_received = together(
        grad_stream, small, received, unit_received
    )
    last = attention_sum(cuts, received)
    unit_total = over_outer(add_low(unit_cuts[0], *unit_received))
    sent = [jnp.concatenate([last[k], small]) for k in (1, 2, 3)]
    sent, last, unit_total, grad_stream, even_grads, later_grads = together(
        sent, last, unit_total, grad_stream, even_grads, later_grads
    )
    received = z_three(sent)
    own_grads = gather_shard(unit_total)
    grad_in = swap_rows(grad_stream)
    later_grads = attention_gathered(later_grads)
    received, later_grads = together(received, later_grads)
    last = over_outer(add_low(last[0], *[block[:rest] for block in received]))
    small = pack(over_outer(four(small, [block[rest:] for block in received])))
    sent = jnp.concatenate([last, small])
    received = yx_three([sent] * 3)
    up_grads, down_grads = unit_results(own_grads, even_grads)
    received, up_grads, down_grads, grad_in = together(received, up_grads, down_grads, grad_in)
    small = pack(four(small, [block[rest:] for block in received]))
    last = attention_join([last] + [block[:rest] for block in received])
    received = over("c", jnp.concatenate([last, small]))
    small = unpack(small) + unpack(received[2 * shard :])
    first_grads = attention_out(last, received[: 2 * shard])

    def two_layers(one, two):
        return jnp.stack([one, two])

    gain_grads = two_layers(jnp.stack([small[9], small[6]]), jnp.stack([small[3], small[0]]))
    shift_grads = two_layers(jnp.stack([small[10], small[7]]), jnp.stack([small[4], small[1]]))
    output_bias_grads = two_layers(small[8], small[2])
    down_bias_grads = two_layers(small[5], small[11])
    up_bias_rows = two_layers(small[18:22], small[12:16])
    input_bias_rows = two_layers(small[22:24], small[16:18])

    def z_part(array, size):
        return lax.dynamic_slice_in_dim(array, z_place * size, size, axis=-1)

    return (
        layer_out,
        grad_in,
        gain_grads,
        shift_grads,
        jnp.stack([first_grads[0], later_grads[0]]),
        z_part(input_bias_rows, shard),
        jnp.stack([first_grads[1], later_grads[1]]),
        output_bias_grads,
        up_grads,
        z_part(up_bias_rows.reshape(layer_count, -1), unit_shard),
        down_grads,
        down_bias_grads,
    )


def solution(mesh):
    split = mesh.shape["dp"] // 8
    fine = Mesh(
        mesh.devices.reshape(split, 2, 2, 2, mesh.shape["tensor"]), ("o", "y", "x", "c", "z")
    )
    rows = P(("o", "y", "x", "c", "z"), None)
    placed = (
        rows,
        P(("o", "y", "x", "c")),
        P(),
        P(),
        P(None, None, None, "z"),
        P(None, None, "z"),
        P(None, "z", None),
        P(),
        P(None, None, "z"),
        P(None, "z"),
        P(None, "z", None),
        P(),
        rows,
    )
    return jax.shard_map(
        local,
        mesh=fine,
        in_specs=placed,
        out_specs=(rows, rows) + placed[2:12],
        check_vma=False,
    )
```

time: 827 us -> 546 us (0.66)
  the two profiles are of different devices: /device:TPU:9 before, /device:TPU:3 now
where the time goes in v2:
time: 546 us; the launch traced here: 538 us
  Pallas kernels  151 us (28%)
  waiting for transfers between devices  143 us (26%)
  other arithmetic  77.4 us (14%)
  starting transfers between devices  76.9 us (14%)
  local copies, waits for them, and re-layouts  46.1 us (8%)
  matrix products  25.3 us (5%)
  between operations  18 us (3%)
    ppermute x40, waiting for transfers between devices, over(): return lax.ppermute(array, axis, flip_pair)  81.6 us
    pallas_call x2, Pallas kernels, units_backward(): pl.pallas_call(functools.partial(units_backward_kernel, len(weights), row...  41.2 us
    pallas_call x2, Pallas kernels, attend_backward(): pl.pallas_call(attend_backward_kernel, grid_spec=pltpu.PrefetchScalarGrid...  38.7 us
    ppermute x21, waiting for transfers between devices, z_three(): lax.ppermute(block, 'z', z_pairs(step + 1))  35.4 us
    pallas_call x2, Pallas kernels, units_forward(): pl.pallas_call(functools.partial(units_forward_kernel, len(weights), rows...  33.5 us
    ppermute x40, starting transfers between devices, over(): return lax.ppermute(array, axis, flip_pair)  32.2 us
    ppermute x21, starting transfers between devices, z_three(): lax.ppermute(block, 'z', z_pairs(step + 1))  28.3 us
    convert_element_type x26, other arithmetic, add_low(): return total.astype(bf16)  27.8 us
  transfers between devices with their start and end apart: 71, of which 30 were waited for; matrix products, arithmetic and copies ran while one was open for 18% of the time, Pallas kernels for 21%

profile of v2, /device:TPU:3, one launch (start us, length us, event | category | flops | bytes accessed | tf_op | source)
XLA Modules:
  0.0 537.6 jit_solution(2902773094538406813)
XLA Ops:
  32.6 11.0 %collective-permute-done.2 = bf16[208,768]{1,0:T(8,128)(2,1)} collective-permute-done((bf16[208,768]{1,0:T(8,128)(2,1)}, bf16[208,768]{1,0:T(8,128)(2,1)}, u32[]{:S(2)}, u32[]{:S(2)}) %collective-permute-start.2) | collective-permute-done | bytes 319520 | tf_op jit(solution)/shard_map/ppermute | solution.py:483
  52.6 6.6 %collective-permute-done.6 = bf16[4,96,768]{2,1,0:T(8,128)(2,1)S(1)} collective-permute-done((bf16[4,96,768]{2,1,0:T(8,128)(2,1)S(1)}, bf16[4,96,768]{2,1,0:T(8,128)(2,1)S(1)}, u32[]{:S(2)}, u32[]{:S(2)}) %collective-permute-start.6) | collective-permute-done | bytes 589856 | tf_op jit(solution)/shard_map/ppermute | solution.py:471
  68.5 8.4 %collective-permute-done.13 = bf16[96,1536]{1,0:T(8,128)(2,1)} collective-permute-done((bf16[96,1536]{1,0:T(8,128)(2,1)S(1)}, bf16[96,1536]{1,0:T(8,128)(2,1)}, u32[]{:S(2)}, u32[]{:S(2)}) %collective-permute-start.13) | collective-permute-done | bytes 294944 | tf_op jit(solution)/shard_map/ppermute | solution.py:483
  91.2 7.8 %collective-permute-done.8 = bf16[192,1536]{1,0:T(8,128)(2,1)S(1)} collective-permute-done((bf16[192,1536]{1,0:T(8,128)(2,1)S(1)}, bf16[192,1536]{1,0:T(8,128)(2,1)S(1)}, u32[]{:S(2)}, u32[]{:S(2)}) %collective-permute-start.8) | collective-permute-done | bytes 589856 | tf_op jit(solution)/shard_map/ppermute | solution.py:471
  99.1 7.8 %collective-permute-done.15 = bf16[192,1536]{1,0:T(8,128)(2,1)S(1)} collective-permute-done((bf16[192,1536]{1,0:T(8,128)(2,1)S(1)}, bf16[192,1536]{1,0:T(8,128)(2,1)S(1)}, u32[]{:S(2)}, u32[]{:S(2)}) %collective-permute-start.15) | collective-permute-done | bytes 589856 | tf_op jit(solution)/shard_map/ppermute | solution.py:471
  107.5 12.2 %attend_forward.2 = (bf16[768,512]{1,0:T(8,128)(2,1)S(1)}, f32[4,8,512]{2,1,0:T(8,128)S(1)}) custom-call(s32[2]{0:T(128)S(1)} %pad_add_fusion.1.info, bf16[768,512]{1,0:T(8,128)(2,1)S(1)} %add_convert_fusion.15.queries, bf16[1536,512]{1,0:T(8,128)(2,1)S(1)} %fusion.kv_own, bf16[1536,512]{1,0:T(8,128)(2,1)S(1)} %collective-permute-done.11.kv_other), custom_call_target="tpu_custom_call" | custom-call | flops 16149000192 | bytes 51660000 | tf_op jit(solution)/shard_map/attend_forward/pallas_call | solution.py:142
  121.2 12.5 %collective-permute-done.12.refs_5_ = bf16[384,1536]{1,0:T(8,128)(2,1)S(1)} collective-permute-done((bf16[384,1536]{1,0:T(8,128)(2,1)S(1)}, bf16[384,1536]{1,0:T(8,128)(2,1)S(1)}, u32[]{:S(2)}, u32[]{:S(2)}) %collective-permute-start.12) | collective-permute-done | bytes 1179680 | tf_op jit(solution)/shard_map/ppermute | solution.py:471
  142.3 17.0 %units_forward.2 = (bf16[512,3072]{1,0:T(8,128)(2,1)}, bf16[512,3072]{1,0:T(8,128)(2,1)}, f32[512,768]{1,0:T(8,128)S(1)}) custom-call(bf16[512,768]{1,0:T(8,128)(2,1)S(1)} %add_convert_fusion.14.normed, f32[512,768]{1,0:T(8,128)S(1)} %get-tuple-element.570.middle.values, f32[8,1,384]{2,1,0:T(1,128)S(1)} %broadcast_in_dim_reshape.6.unit_bias, ...), custom_call_target="tpu_custom_call" | custom-call | flops 19609499648 | bytes 62730000 | tf_op jit(solution)/shard_map/units_forward/pallas_call | solution.py:241
  159.3 5.2 collective-permute-done.23
  178.8 5.4 %collective-permute-done.27 = bf16[512,768]{1,0:T(8,128)(2,1)} collective-permute-done((bf16[512,768]{1,0:T(8,128)(2,1)}, bf16[512,768]{1,0:T(8,128)(2,1)}, u32[]{:S(2)}, u32[]{:S(2)}) %collective-permute-start.27) | collective-permute-done | bytes 786464 | tf_op jit(solution)/shard_map/ppermute | solution.py:553
  189.8 13.5 %attend_forward.3 = (bf16[768,512]{1,0:T(8,128)(2,1)S(1)}, f32[4,8,512]{2,1,0:T(8,128)S(1)}) custom-call(s32[2]{0:T(128)S(1)} %pad_add_fusion.1.info, bf16[768,512]{1,0:T(8,128)(2,1)S(1)} %add_convert_fusion.12.queries, bf16[1536,512]{1,0:T(8,128)(2,1)S(1)} %fusion.1.kv_own, bf16[1536,512]{1,0:T(8,128)(2,1)} %collective-permute-done.26.kv_other), custom_call_target="tpu_custom_call" | custom-call | flops 16149000192 | bytes 51660000 | tf_op jit(solution)/shard_map/attend_forward/pallas_call | solution.py:142
  206.9 16.6 %units_forward.3 = (bf16[512,3072]{1,0:T(8,128)(2,1)S(1)}, bf16[512,3072]{1,0:T(8,128)(2,1)S(1)}, f32[512,768]{1,0:T(8,128)S(1)}) custom-call(bf16[512,768]{1,0:T(8,128)(2,1)S(1)} %copy-done.9, f32[512,768]{1,0:T(8,128)S(1)} %get-tuple-element.572.middle.values, f32[8,1,384]{2,1,0:T(1,128)S(1)} %broadcast_in_dim_reshape.7.unit_bias, ...), custom_call_target="tpu_custom_call" | custom-call | flops 19609499648 | bytes 62730000 | tf_op jit(solution)/shard_map/units_forward/pallas_call | solution.py:241
  223.5 19.4 %units_backward.2 = (bf16[1536,1536]{1,0:T(8,128)(2,1)S(1)}, bf16[1536,1536]{1,0:T(8,128)(2,1)}, f32[512,768]{1,0:T(8,128)S(1)}, f32[8,1,384]{2,1,0:T(1,128)S(1)}) custom-call(s32[8]{0:T(128)S(1)} %fusion.29.place, bf16[512,768]{1,0:T(8,128)(2,1)S(1)} %copy-done.8, bf16[512,768]{1,0:T(8,128)(2,1)S(1)} %copy-done.9, ...), custom_call_target="tpu_custom_call" | custom-call | flops 23069999104 | bytes 73800000 | tf_op jit(solution)/shard_map/units_backward/pallas_call | solution.py:328
  256.1 20.0 %attend_backward.2 = (bf16[768,512]{1,0:T(8,128)(2,1)S(1)}, f32[1536,512]{1,0:T(8,128)S(1)}, bf16[1536,512]{1,0:T(8,128)(2,1)S(1)}) custom-call(s32[2]{0:T(128)S(1)} %pad_add_fusion.1.info, bf16[768,512]{1,0:T(8,128)(2,1)S(1)} %copy-done.40, bf16[1536,512]{1,0:T(8,128)(2,1)S(1)} %copy-done.21, bf16[1536,512]{1,0:T(8,128)(2,1)} %collective-permute-done.26.kv_other, ...), custom_call_target="tpu_custom_call" | custom-call | flops 24223500288 | bytes 77490000 | tf_op jit(solution)/shard_map/attend_backward/pallas_call | solution.py:164
  300.8 5.3 collective-permute-done.34
  316.8 21.8 %units_backward.3 = (bf16[1536,1536]{1,0:T(8,128)(2,1)}, bf16[1536,1536]{1,0:T(8,128)(2,1)}, f32[512,768]{1,0:T(8,128)S(1)}, f32[8,1,384]{2,1,0:T(1,128)S(1)}) custom-call(s32[8]{0:T(128)S(1)} %iota.13.place, bf16[512,768]{1,0:T(8,128)(2,1)S(1)} %get-tuple-element.276.grad_down, bf16[512,768]{1,0:T(8,128)(2,1)S(1)} %copy-done.7, ...), custom_call_target="tpu_custom_call" | custom-call | flops 23069999104 | bytes 73800000 | tf_op jit(solution)/shard_map/units_backward/pallas_call | solution.py:328
  357.4 4.7 add_convert_fusion.3
  369.9 18.7 %attend_backward.3 = (bf16[768,512]{1,0:T(8,128)(2,1)S(1)}, f32[1536,512]{1,0:T(8,128)S(1)}, bf16[1536,512]{1,0:T(8,128)(2,1)S(1)}) custom-call(s32[2]{0:T(128)S(1)} %pad_add_fusion.1.info, bf16[768,512]{1,0:T(8,128)(2,1)S(1)} %copy-done.42, bf16[1536,512]{1,0:T(8,128)(2,1)S(1)} %copy-done.17, bf16[1536,512]{1,0:T(8,128)(2,1)S(1)} %copy-done.19, ...), custom_call_target="tpu_custom_call" | custom-call | flops 24223500288 | bytes 77490000 | tf_op jit(solution)/shard_map/attend_backward/pallas_call | solution.py:164
  388.5 11.3 %collective-permute-done.44 = bf16[384,1536]{1,0:T(8,128)(2,1)S(1)} collective-permute-done((bf16[384,1536]{1,0:T(8,128)(2,1)S(1)}, bf16[384,1536]{1,0:T(8,128)(2,1)S(1)}, u32[]{:S(2)}, u32[]{:S(2)}) %collective-permute-start.44) | collective-permute-done | bytes 1179680 | tf_op jit(solution)/shard_map/ppermute | solution.py:471
  421.4 9.5 %collective-permute-done.51 = bf16[2,96,1536]{2,1,0:T(8,128)(2,1)} collective-permute-done((bf16[2,96,1536]{2,1,0:T(8,128)(2,1)}, bf16[2,96,1536]{2,1,0:T(8,128)(2,1)}, u32[]{:S(2)}, u32[]{:S(2)}) %collective-permute-start.51) | collective-permute-done | bytes 589856 | tf_op jit(solution)/shard_map/ppermute | solution.py:471
  443.6 4.5 collective-permute-start.58
  449.8 11.0 %collective-permute-done.57 = bf16[96,1536]{1,0:T(8,128)(2,1)S(1)} collective-permute-done((bf16[96,1536]{1,0:T(8,128)(2,1)S(1)}, bf16[96,1536]{1,0:T(8,128)(2,1)S(1)}, u32[]{:S(2)}, u32[]{:S(2)}) %collective-permute-start.57) | collective-permute-done | bytes 294944 | tf_op jit(solution)/shard_map/ppermute | solution.py:483
  472.6 5.7 %collective-permute-start.65 = (f32[512,768]{1,0:T(8,128)S(1)}, f32[512,768]{1,0:T(8,128)S(1)}, u32[]{:S(2)}, u32[]{:S(2)}) collective-permute-start(f32[512,768]{1,0:T(8,128)S(1)} %get-tuple-element.385), channel_id=1, source_target_pairs={{1,4},{3,6},{4,1},{6,3},{9,12},{11,14},{12,9},{14,11},{17,20},{19,... | collective-permute-start | bytes 4718600 | tf_op jit(solution)/shard_map/ppermute | solution.py:553
  489.8 13.7 %collective-permute-done.65 = f32[512,768]{1,0:T(8,128)S(1)} collective-permute-done((f32[512,768]{1,0:T(8,128)S(1)}, f32[512,768]{1,0:T(8,128)S(1)}, u32[]{:S(2)}, u32[]{:S(2)}) %collective-permute-start.65) | collective-permute-done | bytes 1572896 | tf_op jit(solution)/shard_map/ppermute | solution.py:553
  (619 shorter events, 250.3 us)
Async XLA Ops:
  7.2 198.6 %all-gather.5.cloned.1.call-start = ((), (), s32[]{:S(2)}) async-start(), calls=%async_computation | async-start | bytes 9732096 | tf_op jit(solution)/shard_map/all_gather | solution.py:655
  16.4 27.2 %collective-permute-start.2 = (bf16[208,768]{1,0:T(8,128)(2,1)}, bf16[208,768]{1,0:T(8,128)(2,1)}, u32[]{:S(2)}, u32[]{:S(2)}) collective-permute-start(bf16[208,768]{1,0:T(8,128)(2,1)} %pad_maximum_fusion.18), channel_id=1, source_target_pairs={{0,2},{1,3},{2,0},{3,1},{4,6},{5,7},{6,4},{7,5},{8,10},{9,11},{10,... | collective-permute-start | bytes 958472 | tf_op jit(solution)/shard_map/ppermute | solution.py:483
  16.4 28.2 %collective-permute-start.1 = (bf16[208,768]{1,0:T(8,128)(2,1)}, bf16[208,768]{1,0:T(8,128)(2,1)}, u32[]{:S(2)}, u32[]{:S(2)}) collective-permute-start(bf16[208,768]{1,0:T(8,128)(2,1)} %pad_maximum_fusion.18), channel_id=1, source_target_pairs={{0,1},{1,0},{2,3},{3,2},{4,5},{5,4},{6,7},{7,6},{8,9},{9,8},{10,11... | collective-permute-start | bytes 958472 | tf_op jit(solution)/shard_map/ppermute | solution.py:483
  18.1 59.9 %collective-permute-start.10 = (bf16[512,768]{1,0:T(8,128)(2,1)}, bf16[512,768]{1,0:T(8,128)(2,1)}, u32[]{:S(2)}, u32[]{:S(2)}) collective-permute-start(bf16[512,768]{1,0:T(8,128)(2,1)} %param.13), channel_id=1, source_target_pairs={{1,4},{3,6},{4,1},{6,3},{9,12},{11,14},{12,9},{14,11},{17,20},{19,... | collective-permute-start | bytes 2359304 | tf_op jit(solution)/shard_map/ppermute | solution.py:553
  67.4 399.6 %all-gather.7.cloned.1.call-start = ((), (), s32[]{:S(2)}) async-start(), calls=%async_computation.1 | async-start | bytes 2654208 | tf_op jit(solution)/shard_map/all_gather | solution.py:777
  87.9 31.9 %collective-permute-start.17 = (bf16[192,768]{1,0:T(8,128)(2,1)S(1)}, bf16[192,768]{1,0:T(8,128)(2,1)S(1)}, u32[]{:S(2)}, u32[]{:S(2)}) collective-permute-start(bf16[192,768]{1,0:T(8,128)(2,1)S(1)} %pad_maximum_fusion.23), channel_id=1, source_target_pairs={{0,1},{1,0},{2,3},{3,2},{4,5},{5,4},{6,7},{7,6},{8,9},{9,8},{10,11... | collective-permute-start | bytes 884744 | tf_op jit(solution)/shard_map/ppermute | solution.py:483
  87.9 33.2 %collective-permute-start.18 = (bf16[192,768]{1,0:T(8,128)(2,1)S(1)}, bf16[192,768]{1,0:T(8,128)(2,1)S(1)}, u32[]{:S(2)}, u32[]{:S(2)}) collective-permute-start(bf16[192,768]{1,0:T(8,128)(2,1)S(1)} %pad_maximum_fusion.23), channel_id=1, source_target_pairs={{0,2},{1,3},{2,0},{3,1},{4,6},{5,7},{6,4},{7,5},{8,10},{9,11},{10,... | collective-permute-start | bytes 884744 | tf_op jit(solution)/shard_map/ppermute | solution.py:483
  106.9 26.8 %collective-permute-start.12 = (bf16[384,1536]{1,0:T(8,128)(2,1)S(1)}, bf16[384,1536]{1,0:T(8,128)(2,1)S(1)}, u32[]{:S(2)}, u32[]{:S(2)}) collective-permute-start(bf16[384,1536]{1,0:T(8,128)(2,1)S(1)} %constant_dynamic-update-slice_fusion.refs_4_), channel_id=1, source_target_pairs={{0,16},{16,0},{1,17},{17,1},{2,18},{18,2},{3,19},{19,3},{4,20},{20... | collective-permute-start | bytes 3538952 | tf_op jit(solution)/shard_map/ppermute | solution.py:471
  107.2 26.6 %collective-permute-start.16 = (bf16[384,1536]{1,0:T(8,128)(2,1)S(1)}, bf16[384,1536]{1,0:T(8,128)(2,1)S(1)}, u32[]{:S(2)}, u32[]{:S(2)}) collective-permute-start(bf16[384,1536]{1,0:T(8,128)(2,1)S(1)} %constant_dynamic-update-slice_fusion.2.refs_6_), channel_id=1, source_target_pairs={{0,8},{8,0},{1,9},{9,1},{2,10},{10,2},{3,11},{11,3},{4,12},{12,4},... | collective-permute-start | bytes 3538952 | tf_op jit(solution)/shard_map/ppermute | solution.py:471
  252.6 27.5 %collective-permute-start.29 = (bf16[384,1536]{1,0:T(8,128)(2,1)S(1)}, bf16[384,1536]{1,0:T(8,128)(2,1)S(1)}, u32[]{:S(2)}, u32[]{:S(2)}) collective-permute-start(bf16[384,1536]{1,0:T(8,128)(2,1)S(1)} %add_convert_fusion.8), channel_id=1, source_target_pairs={{0,16},{16,0},{1,17},{17,1},{2,18},{18,2},{3,19},{19,3},{4,20},{20... | collective-permute-start | bytes 3538952 | tf_op jit(solution)/shard_map/ppermute | solution.py:471
  252.6 27.5 %collective-permute-start.30 = (bf16[384,1536]{1,0:T(8,128)(2,1)S(1)}, bf16[384,1536]{1,0:T(8,128)(2,1)S(1)}, u32[]{:S(2)}, u32[]{:S(2)}) collective-permute-start(bf16[384,1536]{1,0:T(8,128)(2,1)S(1)} %add_convert_fusion.7), channel_id=1, source_target_pairs={{0,8},{8,0},{1,9},{9,1},{2,10},{10,2},{3,11},{11,3},{4,12},{12,4},... | collective-permute-start | bytes 3538952 | tf_op jit(solution)/shard_map/ppermute | solution.py:471
  311.4 27.3 %collective-permute-start.36 = (bf16[4,2,48,768]{3,2,1,0:T(8,128)(2,1)S(1)}, bf16[4,2,48,768]{3,2,1,0:T(8,128)(2,1)S(1)}, u32[]{:S(2)}, u32[]{:S(2)}) collective-permute-start(bf16[4,2,48,768]{3,2,1,0:T(8,128)(2,1)S(1)} %get-tuple-element.283), channel_id=1, source_target_pairs={{0,16},{16,0},{1,17},{17,1},{2,18},{18,2},{3,19},{19,3},{4,20},{20... | collective-permute-start | bytes 1769480 | tf_op jit(solution)/shard_map/ppermute | solution.py:471
  312.0 26.6 %collective-permute-start.37 = (bf16[4,2,48,768]{3,2,1,0:T(8,128)(2,1)S(1)}, bf16[4,2,48,768]{3,2,1,0:T(8,128)(2,1)S(1)}, u32[]{:S(2)}, u32[]{:S(2)}) collective-permute-start(bf16[4,2,48,768]{3,2,1,0:T(8,128)(2,1)S(1)} %get-tuple-element.284), channel_id=1, source_target_pairs={{0,8},{8,0},{1,9},{9,1},{2,10},{10,2},{3,11},{11,3},{4,12},{12,4},... | collective-permute-start | bytes 1769480 | tf_op jit(solution)/shard_map/ppermute | solution.py:471
  355.6 111.5 %all-gather.9.cloned.1.call-start = ((), (), s32[]{:S(2)}) async-start(), calls=%async_computation.2 | async-start | bytes 1327104 | tf_op jit(solution)/shard_map/all_gather | solution.py:777
  364.5 35.3 %collective-permute-start.44 = (bf16[384,1536]{1,0:T(8,128)(2,1)S(1)}, bf16[384,1536]{1,0:T(8,128)(2,1)S(1)}, u32[]{:S(2)}, u32[]{:S(2)}) collective-permute-start(bf16[384,1536]{1,0:T(8,128)(2,1)S(1)} %get-tuple-element.317), channel_id=1, source_target_pairs={{0,16},{16,0},{1,17},{17,1},{2,18},{18,2},{3,19},{19,3},{4,20},{20... | collective-permute-start | bytes 3538952 | tf_op jit(solution)/shard_map/ppermute | solution.py:471
  364.9 34.9 %collective-permute-start.45 = (bf16[384,1536]{1,0:T(8,128)(2,1)S(1)}, bf16[384,1536]{1,0:T(8,128)(2,1)S(1)}, u32[]{:S(2)}, u32[]{:S(2)}) collective-permute-start(bf16[384,1536]{1,0:T(8,128)(2,1)S(1)} %get-tuple-element.318), channel_id=1, source_target_pairs={{0,8},{8,0},{1,9},{9,1},{2,10},{10,2},{3,11},{11,3},{4,12},{12,4},... | collective-permute-start | bytes 3538952 | tf_op jit(solution)/shard_map/ppermute | solution.py:471
  366.3 33.5 %collective-permute-start.46 = (bf16[96,768]{1,0:T(8,128)(2,1)S(1)}, bf16[96,768]{1,0:T(8,128)(2,1)S(1)}, u32[]{:S(2)}, u32[]{:S(2)}) collective-permute-start(bf16[96,768]{1,0:T(8,128)(2,1)S(1)} %get-tuple-element.327), channel_id=1, source_target_pairs={{0,1},{1,0},{2,3},{3,2},{4,5},{5,4},{6,7},{7,6},{8,9},{9,8},{10,11... | collective-permute-start | bytes 442376 | tf_op jit(solution)/shard_map/ppermute | solution.py:483
  367.5 32.3 %collective-permute-start.47 = (bf16[96,768]{1,0:T(8,128)(2,1)S(1)}, bf16[96,768]{1,0:T(8,128)(2,1)S(1)}, u32[]{:S(2)}, u32[]{:S(2)}) collective-permute-start(bf16[96,768]{1,0:T(8,128)(2,1)S(1)} %get-tuple-element.328), channel_id=1, source_target_pairs={{0,2},{1,3},{2,0},{3,1},{4,6},{5,7},{6,4},{7,5},{8,10},{9,11},{10,... | collective-permute-start | bytes 442376 | tf_op jit(solution)/shard_map/ppermute | solution.py:483
  368.5 31.3 %collective-permute-start.48 = (bf16[96,768]{1,0:T(8,128)(2,1)S(1)}, bf16[96,768]{1,0:T(8,128)(2,1)S(1)}, u32[]{:S(2)}, u32[]{:S(2)}) collective-permute-start(bf16[96,768]{1,0:T(8,128)(2,1)S(1)} %get-tuple-element.329), channel_id=1, source_target_pairs={{0,3},{1,2},{2,1},{3,0},{4,7},{5,6},{6,5},{7,4},{8,11},{9,10},{10,... | collective-permute-start | bytes 442376 | tf_op jit(solution)/shard_map/ppermute | solution.py:483
  415.9 92.5 %all-gather.11.cloned.1.call-start = ((), (), s32[]{:S(2)}) async-start(), calls=%async_computation.3 | async-start | bytes 2654208 | tf_op jit(solution)/shard_map/all_gather | solution.py:777
  472.6 30.8 %collective-permute-start.65 = (f32[512,768]{1,0:T(8,128)S(1)}, f32[512,768]{1,0:T(8,128)S(1)}, u32[]{:S(2)}, u32[]{:S(2)}) collective-permute-start(f32[512,768]{1,0:T(8,128)S(1)} %get-tuple-element.385), channel_id=1, source_target_pairs={{1,4},{3,6},{4,1},{6,3},{9,12},{11,14},{12,9},{14,11},{17,20},{19,... | collective-permute-start | bytes 4718600 | tf_op jit(solution)/shard_map/ppermute | solution.py:553
  486.9 28.8 %collective-permute-start.62 = (bf16[144,768]{1,0:T(8,128)(2,1)}, bf16[144,768]{1,0:T(8,128)(2,1)}, u32[]{:S(2)}, u32[]{:S(2)}) collective-permute-start(bf16[144,768]{1,0:T(8,128)(2,1)} %pad_maximum_fusion.25), channel_id=1, source_target_pairs={{0,8},{8,0},{1,9},{9,1},{2,10},{10,2},{3,11},{11,3},{4,12},{12,4},... | collective-permute-start | bytes 663560 | tf_op jit(solution)/shard_map/ppermute | solution.py:471
  488.6 27.1 %collective-permute-start.63 = (bf16[144,768]{1,0:T(8,128)(2,1)}, bf16[144,768]{1,0:T(8,128)(2,1)}, u32[]{:S(2)}, u32[]{:S(2)}) collective-permute-start(bf16[144,768]{1,0:T(8,128)(2,1)} %pad_maximum_fusion.25), channel_id=1, source_target_pairs={{0,16},{16,0},{1,17},{17,1},{2,18},{18,2},{3,19},{19,3},{4,20},{20... | collective-permute-start | bytes 663560 | tf_op jit(solution)/shard_map/ppermute | solution.py:471
  488.6 27.1 %collective-permute-start.64 = (bf16[144,768]{1,0:T(8,128)(2,1)}, bf16[144,768]{1,0:T(8,128)(2,1)}, u32[]{:S(2)}, u32[]{:S(2)}) collective-permute-start(bf16[144,768]{1,0:T(8,128)(2,1)} %pad_maximum_fusion.25), channel_id=1, source_target_pairs={{0,24},{8,16},{16,8},{24,0},{1,25},{9,17},{17,9},{25,1},{2,26},{10... | collective-permute-start | bytes 663560 | tf_op jit(solution)/shard_map/ppermute | solution.py:491
  (154 other events, 1725.9 us)
Sparse Core Ops, SparseCore 0:
  67.5 110.8 all-gather.4
  355.7 37.1 all-gather.6
  416.0 26.3 all-gather.8
  467.2 41.1 all-gather.10

commit v3 on v2

--- a/solution.py
+++ b/solution.py
@@ -218,17 +218,20 @@
     activated, slopes, result, buffer, arrived = refs[count:]
     slot = stream_pieces(list_pieces(weights, rows), buffer, arrived)
     width = normed.shape[1]
-    pre = dot(normed[...], buffer[slot, :, :width], (1, 1)) + unit_bias[0]
-    act, slope = gelu_pair(pre)
-    act = act.astype(bf16)
-    activated[...] = act
-    slopes[...] = slope.astype(bf16)
 
     @pl.when(pl.program_id(0) == 0)
     def _():
         result[...] = middle[...] + down_bias[...]
 
-    result[...] += dot(act, buffer[slot, :, width:], (1, 0))
+    size = normed.shape[0] // 2
+    for start in range(0, 2 * size, size):
+        part = slice(start, start + size)
+        pre = dot(normed[part, :], buffer[slot, :, :width], (1, 1)) + unit_bias[0]
+        act, slope = gelu_pair(pre)
+        act = act.astype(bf16)
+        activated[part, :] = act
+        slopes[part, :] = slope.astype(bf16)
+        result[part, :] += dot(act, buffer[slot, :, width:], (1, 0))
 
 
 def units_forward(normed, middle, unit_bias, down_bias, weights):
@@ -388,9 +391,11 @@
 
         @pl.when(step == pl.num_programs(0) - 1)
         def _():
-            rows = jnp.concatenate(
-                [ref[0:3, :] for ref in earlier] + [sums[0:2, :], others[...]]
-            )
+            rows = [sums[0:1, :], earlier[2][0:1, :], earlier[1][0:1, :], earlier[0][0:1, :]]
+            rows += [sums[1:2, :], earlier[2][1:2, :], earlier[1][1:2, :], earlier[0][1:2, :]]
+            rows += [earlier[2][2:3, :], earlier[0][2:3, :], earlier[1][2:3, :]]
+            rows += [others[0:1, :], others[7:11, :], others[1:5, :]]
+            rows = jnp.concatenate(rows + [others[11:13, :], others[5:7, :]])
             high = rows.astype(bf16)
             packed[0 : rows.shape[0], :] = high
             packed[rows.shape[0] :, :] = (rows - high.astype(f32)).astype(bf16)
@@ -930,7 +935,8 @@
         outs = attend_backward(
             info, queries, kv_own, kv_other, mixed, log_total, grad_mixed, groups
         )
-        outs, unit_received = together(outs, unit_received)
+        kv_received = over("c", outs[2])
+        outs, unit_received = together(outs[:2], unit_received)
         unit_parts, unit_sent = unit_second(unit_parts, unit_received)
         if first:
             later_received = tie(later_received, outs[0])
@@ -944,8 +950,8 @@
                 outs, unit_parts, unit_sent, layer_out
             )
         unit_received = [over("x", unit_sent[0]), over("y", unit_sent[1])]
-        grad_queries, grad_kv_own, grad_kv_other = outs
-        grad_kv = add_low(grad_kv_own, over("c", grad_kv_other))
+        grad_queries, grad_kv_own = outs
+        grad_kv = add_low(grad_kv_own, kv_received)
         grad_q = dot(grad_queries, normed, (1, 0)).astype(bf16)
         grad_kv_weight = dot(grad_kv, normed, (1, 0)).astype(bf16)
         attention_sent, attention_kept = attention_parts(grad_kv_weight, grad_q, grad_o)
@@ -1002,23 +1008,22 @@
     small = pack(over_outer(four(small, [block[rest:] for block in received])))
     sent = jnp.concatenate([last, small])
     received = yx_three([sent] * 3)
-    up_grads, down_grads = unit_results(own_grads, even_grads)
-    received, up_grads, down_grads, grad_in = together(received, up_grads, down_grads, grad_in)
+    received, grad_in = together(received, grad_in)
     small = pack(four(small, [block[rest:] for block in received]))
     last = attention_join([last] + [block[:rest] for block in received])
-    received = over("c", jnp.concatenate([last, small]))
+    sent = jnp.concatenate([last, small])
+    sent, own_grads, even_grads = together(sent, own_grads, even_grads)
+    received = over("c", sent)
+    up_grads, down_grads = unit_results(own_grads, even_grads)
+    received, up_grads, down_grads = together(received, up_grads, down_grads)
     small = unpack(small) + unpack(received[2 * shard :])
     first_grads = attention_out(last, received[: 2 * shard])
 
-    def two_layers(one, two):
-        return jnp.stack([one, two])
-
-    gain_grads = two_layers(jnp.stack([small[9], small[6]]), jnp.stack([small[3], small[0]]))
-    shift_grads = two_layers(jnp.stack([small[10], small[7]]), jnp.stack([small[4], small[1]]))
-    output_bias_grads = two_layers(small[8], small[2])
-    down_bias_grads = two_layers(small[5], small[11])
-    up_bias_rows = two_layers(small[18:22], small[12:16])
-    input_bias_rows = two_layers(small[22:24], small[16:18])
+    gain_grads = small[0:4].reshape(layer_count, 2, width)
+    shift_grads = small[4:8].reshape(layer_count, 2, width)
+    output_bias_grads, down_bias_grads = small[8:10], small[10:12]
+    up_bias_rows = small[12:20].reshape(layer_count, -1)
+    input_bias_rows = small[20:24].reshape(layer_count, 2, width)
 
     def z_part(array, size):
         return lax.dynamic_slice_in_dim(array, z_place * size, size, axis=-1)
@@ -1033,7 +1038,7 @@
         jnp.stack([first_grads[1], later_grads[1]]),
         output_bias_grads,
         up_grads,
-        z_part(up_bias_rows.reshape(layer_count, -1), unit_shard),
+        z_part(up_bias_rows, unit_shard),
         down_grads,
         down_bias_grads,
     )

time: 546 us -> 542 us (level)
  the two profiles are of different devices: /device:TPU:3 before, /device:TPU:9 now
where the time goes in v3:
time: 542 us; the launch traced here: 532 us
  Pallas kernels  147 us (27%)
  waiting for transfers between devices  137 us (25%)
  starting transfers between devices  80.2 us (15%)
  other arithmetic  76.8 us (14%)
  local copies, waits for them, and re-layouts  47.4 us (9%)
  matrix products  25.3 us (5%)
  between operations  17.9 us (3%)
    ppermute x40, waiting for transfers between devices, over(): return lax.ppermute(array, axis, flip_pair)  69.4 us
    ppermute x21, waiting for transfers between devices, z_three(): lax.ppermute(block, 'z', z_pairs(step + 1))  61.4 us
    ppermute x40, starting transfers between devices, over(): return lax.ppermute(array, axis, flip_pair)  44.1 us
    pallas_call x2, Pallas kernels, units_backward(): pl.pallas_call(functools.partial(units_backward_kernel, len(weights), row...  41.2 us
    pallas_call x2, Pallas kernels, attend_backward(): pl.pallas_call(attend_backward_kernel, grid_spec=pltpu.PrefetchScalarGrid...  38.5 us
    convert_element_type x26, other arithmetic, add_low(): return total.astype(bf16)  30.8 us
    pallas_call x2, Pallas kernels, units_forward(): pl.pallas_call(functools.partial(units_forward_kernel, len(weights), rows...  30.7 us
    ppermute x21, starting transfers between devices, z_three(): lax.ppermute(block, 'z', z_pairs(step + 1))  27.6 us
  transfers between devices with their start and end apart: 71, of which 27 were waited for; matrix products, arithmetic and copies ran while one was open for 19% of the time, Pallas kernels for 21%

profile of v3, /device:TPU:9, one launch (start us, length us, event | category | flops | bytes accessed | tf_op | source)
XLA Modules:
  0.0 531.6 jit_solution(13153073377427782482)
XLA Ops:
  30.0 5.7 %collective-permute-done.3 = bf16[208,768]{1,0:T(8,128)(2,1)} collective-permute-done((bf16[208,768]{1,0:T(8,128)(2,1)}, bf16[208,768]{1,0:T(8,128)(2,1)}, u32[]{:S(2)}, u32[]{:S(2)}) %collective-permute-start.3) | collective-permute-done | bytes 319520 | tf_op jit(solution)/shard_map/ppermute | solution.py:488
  36.6 4.8 collective-permute-done.2
  70.1 4.8 collective-permute-done.13
  90.0 4.5 collective-permute-done.8
  96.5 7.7 %collective-permute-done.15 = bf16[192,1536]{1,0:T(8,128)(2,1)S(1)} collective-permute-done((bf16[192,1536]{1,0:T(8,128)(2,1)S(1)}, bf16[192,1536]{1,0:T(8,128)(2,1)S(1)}, u32[]{:S(2)}, u32[]{:S(2)}) %collective-permute-start.15) | collective-permute-done | bytes 589856 | tf_op jit(solution)/shard_map/ppermute | solution.py:476
  105.8 12.0 %attend_forward.2 = (bf16[768,512]{1,0:T(8,128)(2,1)S(1)}, f32[4,8,512]{2,1,0:T(8,128)S(1)}) custom-call(s32[2]{0:T(128)S(1)} %pad_add_fusion.1.info, bf16[768,512]{1,0:T(8,128)(2,1)S(1)} %add_convert_fusion.15.queries, bf16[1536,512]{1,0:T(8,128)(2,1)S(1)} %fusion.kv_own, bf16[1536,512]{1,0:T(8,128)(2,1)S(1)} %collective-permute-done.11.kv_other), custom_call_target="tpu_custom_call" | custom-call | flops 16149000192 | bytes 51660000 | tf_op jit(solution)/shard_map/attend_forward/pallas_call | solution.py:142
  119.8 8.2 %collective-permute-done.19 = bf16[192,768]{1,0:T(8,128)(2,1)S(1)} collective-permute-done((bf16[192,768]{1,0:T(8,128)(2,1)S(1)}, bf16[192,768]{1,0:T(8,128)(2,1)S(1)}, u32[]{:S(2)}, u32[]{:S(2)}) %collective-permute-start.19) | collective-permute-done | bytes 294944 | tf_op jit(solution)/shard_map/ppermute | solution.py:488
  141.3 15.6 %units_forward.2 = (bf16[512,3072]{1,0:T(8,128)(2,1)}, bf16[512,3072]{1,0:T(8,128)(2,1)}, f32[512,768]{1,0:T(8,128)S(1)}) custom-call(bf16[512,768]{1,0:T(8,128)(2,1)S(1)} %add_convert_fusion.14.normed, f32[512,768]{1,0:T(8,128)S(1)} %get-tuple-element.559.middle.values, f32[8,1,384]{2,1,0:T(1,128)S(1)} %broadcast_in_dim_reshape.6.unit_bias, ...), custom_call_target="tpu_custom_call" | custom-call | flops 19609499648 | bytes 62730000 | tf_op jit(solution)/shard_map/units_forward/pallas_call | solution.py:244
  157.0 8.3 %collective-permute-done.23 = bf16[4,96,768]{2,1,0:T(8,128)(2,1)S(1)} collective-permute-done((bf16[4,96,768]{2,1,0:T(8,128)(2,1)S(1)}, bf16[4,96,768]{2,1,0:T(8,128)(2,1)S(1)}, u32[]{:S(2)}, u32[]{:S(2)}) %collective-permute-start.23) | collective-permute-done | bytes 589856 | tf_op jit(solution)/shard_map/ppermute | solution.py:476
  185.5 13.3 %attend_forward.3 = (bf16[768,512]{1,0:T(8,128)(2,1)S(1)}, f32[4,8,512]{2,1,0:T(8,128)S(1)}) custom-call(s32[2]{0:T(128)S(1)} %pad_add_fusion.1.info, bf16[768,512]{1,0:T(8,128)(2,1)S(1)} %add_convert_fusion.12.queries, bf16[1536,512]{1,0:T(8,128)(2,1)S(1)} %fusion.1.kv_own, bf16[1536,512]{1,0:T(8,128)(2,1)} %collective-permute-done.26.kv_other), custom_call_target="tpu_custom_call" | custom-call | flops 16149000192 | bytes 51660000 | tf_op jit(solution)/shard_map/attend_forward/pallas_call | solution.py:142
  202.4 15.0 %units_forward.3 = (bf16[512,3072]{1,0:T(8,128)(2,1)S(1)}, bf16[512,3072]{1,0:T(8,128)(2,1)S(1)}, f32[512,768]{1,0:T(8,128)S(1)}) custom-call(bf16[512,768]{1,0:T(8,128)(2,1)S(1)} %copy-done.9, f32[512,768]{1,0:T(8,128)S(1)} %get-tuple-element.561.middle.values, f32[8,1,384]{2,1,0:T(1,128)S(1)} %broadcast_in_dim_reshape.7.unit_bias, ...), custom_call_target="tpu_custom_call" | custom-call | flops 19609499648 | bytes 62730000 | tf_op jit(solution)/shard_map/units_forward/pallas_call | solution.py:244
  217.4 19.4 %units_backward.2 = (bf16[1536,1536]{1,0:T(8,128)(2,1)S(1)}, bf16[1536,1536]{1,0:T(8,128)(2,1)}, f32[512,768]{1,0:T(8,128)S(1)}, f32[8,1,384]{2,1,0:T(1,128)S(1)}) custom-call(s32[8]{0:T(128)S(1)} %fusion.27.place, bf16[512,768]{1,0:T(8,128)(2,1)S(1)} %copy-done.8, bf16[512,768]{1,0:T(8,128)(2,1)S(1)} %copy-done.9, ...), custom_call_target="tpu_custom_call" | custom-call | flops 23069999104 | bytes 73800000 | tf_op jit(solution)/shard_map/units_backward/pallas_call | solution.py:331
  252.0 19.9 %attend_backward.2 = (bf16[768,512]{1,0:T(8,128)(2,1)S(1)}, f32[1536,512]{1,0:T(8,128)S(1)}, bf16[1536,512]{1,0:T(8,128)(2,1)S(1)}) custom-call(s32[2]{0:T(128)S(1)} %pad_add_fusion.1.info, bf16[768,512]{1,0:T(8,128)(2,1)S(1)} %copy-done.40, bf16[1536,512]{1,0:T(8,128)(2,1)S(1)} %copy-done.21, bf16[1536,512]{1,0:T(8,128)(2,1)} %collective-permute-done.26.kv_other, ...), custom_call_target="tpu_custom_call" | custom-call | flops 24223500288 | bytes 77490000 | tf_op jit(solution)/shard_map/attend_backward/pallas_call | solution.py:164
  297.4 5.1 collective-permute-done.34
  311.7 21.8 %units_backward.3 = (bf16[1536,1536]{1,0:T(8,128)(2,1)}, bf16[1536,1536]{1,0:T(8,128)(2,1)}, f32[512,768]{1,0:T(8,128)S(1)}, f32[8,1,384]{2,1,0:T(1,128)S(1)}) custom-call(s32[8]{0:T(128)S(1)} %iota.13.place, bf16[512,768]{1,0:T(8,128)(2,1)S(1)} %get-tuple-element.274.grad_down, bf16[512,768]{1,0:T(8,128)(2,1)S(1)} %copy-done.7, ...), custom_call_target="tpu_custom_call" | custom-call | flops 23069999104 | bytes 73800000 | tf_op jit(solution)/shard_map/units_backward/pallas_call | solution.py:331
  354.0 5.6 %add_convert_fusion.3 = (bf16[384,1536]{1,0:T(8,128)(2,1)S(1)}, bf16[384,1536]{1,0:T(8,128)(2,1)S(1)}, bf16[384,1536]{1,0:T(8,128)(2,1)}, bf16[384,1536]{1,0:T(8,128)(2,1)}) fusion(bf16[1536,1536]{1,0:T(8,128)(2,1)} %collective-permute-done.41, bf16[1536,1536]{1,0:T(8,128)(2,1)} %get-tuple-element.303), kind=kLoop, calls=%fused_computation.15 | loop fusion | flops 9437184 | bytes 14155776 | tf_op jit(solution)/shard_map/convert_element_type | solution.py:504
  366.2 18.6 %attend_backward.3 = (bf16[768,512]{1,0:T(8,128)(2,1)S(1)}, f32[1536,512]{1,0:T(8,128)S(1)}, bf16[1536,512]{1,0:T(8,128)(2,1)S(1)}) custom-call(s32[2]{0:T(128)S(1)} %pad_add_fusion.1.info, bf16[768,512]{1,0:T(8,128)(2,1)S(1)} %copy-done.42, bf16[1536,512]{1,0:T(8,128)(2,1)S(1)} %copy-done.17, bf16[1536,512]{1,0:T(8,128)(2,1)S(1)} %copy-done.19, ...), custom_call_target="tpu_custom_call" | custom-call | flops 24223500288 | bytes 77490000 | tf_op jit(solution)/shard_map/attend_backward/pallas_call | solution.py:164
  386.5 8.7 %collective-permute-done.44 = bf16[384,1536]{1,0:T(8,128)(2,1)S(1)} collective-permute-done((bf16[384,1536]{1,0:T(8,128)(2,1)S(1)}, bf16[384,1536]{1,0:T(8,128)(2,1)S(1)}, u32[]{:S(2)}, u32[]{:S(2)}) %collective-permute-start.44) | collective-permute-done | bytes 1179680 | tf_op jit(solution)/shard_map/ppermute | solution.py:476
  419.8 9.6 %collective-permute-done.51 = bf16[2,96,1536]{2,1,0:T(8,128)(2,1)} collective-permute-done((bf16[2,96,1536]{2,1,0:T(8,128)(2,1)}, bf16[2,96,1536]{2,1,0:T(8,128)(2,1)}, u32[]{:S(2)}, u32[]{:S(2)}) %collective-permute-start.51) | collective-permute-done | bytes 589856 | tf_op jit(solution)/shard_map/ppermute | solution.py:476
  446.0 11.9 %collective-permute-done.57 = bf16[96,1536]{1,0:T(8,128)(2,1)S(1)} collective-permute-done((bf16[96,1536]{1,0:T(8,128)(2,1)S(1)}, bf16[96,1536]{1,0:T(8,128)(2,1)S(1)}, u32[]{:S(2)}, u32[]{:S(2)}) %collective-permute-start.57) | collective-permute-done | bytes 294944 | tf_op jit(solution)/shard_map/ppermute | solution.py:488
  457.9 6.9 %collective-permute-done.58 = bf16[96,1536]{1,0:T(8,128)(2,1)S(1)} collective-permute-done((bf16[96,1536]{1,0:T(8,128)(2,1)S(1)}, bf16[96,1536]{1,0:T(8,128)(2,1)S(1)}, u32[]{:S(2)}, u32[]{:S(2)}) %collective-permute-start.58) | collective-permute-done | bytes 294944 | tf_op jit(solution)/shard_map/ppermute | solution.py:488
  477.6 10.0 %collective-permute-done.61 = bf16[144,768]{1,0:T(8,128)(2,1)S(1)} collective-permute-done((bf16[144,768]{1,0:T(8,128)(2,1)S(1)}, bf16[144,768]{1,0:T(8,128)(2,1)S(1)}, u32[]{:S(2)}, u32[]{:S(2)}) %collective-permute-start.61) | collective-permute-done | bytes 221216 | tf_op jit(solution)/shard_map/ppermute | solution.py:488
  491.9 7.0 %collective-permute-done.62 = bf16[144,768]{1,0:T(8,128)(2,1)S(1)} collective-permute-done((bf16[144,768]{1,0:T(8,128)(2,1)S(1)}, bf16[144,768]{1,0:T(8,128)(2,1)S(1)}, u32[]{:S(2)}, u32[]{:S(2)}) %collective-permute-start.62) | collective-permute-done | bytes 221216 | tf_op jit(solution)/shard_map/ppermute | solution.py:476
  499.2 5.7 %collective-permute-done.64 = bf16[144,768]{1,0:T(8,128)(2,1)S(1)} collective-permute-done((bf16[144,768]{1,0:T(8,128)(2,1)S(1)}, bf16[144,768]{1,0:T(8,128)(2,1)S(1)}, u32[]{:S(2)}, u32[]{:S(2)}) %collective-permute-start.64) | collective-permute-done | bytes 221216 | tf_op jit(solution)/shard_map/ppermute | solution.py:496
  (623 shorter events, 263.5 us)
Async XLA Ops:
  7.2 194.1 %all-gather.5.cloned.1.call-start = ((), (), s32[]{:S(2)}) async-start(), calls=%async_computation | async-start | bytes 9732096 | tf_op jit(solution)/shard_map/all_gather | solution.py:660
  14.3 27.1 %collective-permute-start.2 = (bf16[208,768]{1,0:T(8,128)(2,1)}, bf16[208,768]{1,0:T(8,128)(2,1)}, u32[]{:S(2)}, u32[]{:S(2)}) collective-permute-start(bf16[208,768]{1,0:T(8,128)(2,1)} %pad_maximum_fusion.18), channel_id=1, source_target_pairs={{0,2},{1,3},{2,0},{3,1},{4,6},{5,7},{6,4},{7,5},{8,10},{9,11},{10,... | collective-permute-start | bytes 958472 | tf_op jit(solution)/shard_map/ppermute | solution.py:488
  15.4 27.1 %collective-permute-start.1 = (bf16[208,768]{1,0:T(8,128)(2,1)}, bf16[208,768]{1,0:T(8,128)(2,1)}, u32[]{:S(2)}, u32[]{:S(2)}) collective-permute-start(bf16[208,768]{1,0:T(8,128)(2,1)} %pad_maximum_fusion.18), channel_id=1, source_target_pairs={{0,1},{1,0},{2,3},{3,2},{4,5},{5,4},{6,7},{7,6},{8,9},{9,8},{10,11... | collective-permute-start | bytes 958472 | tf_op jit(solution)/shard_map/ppermute | solution.py:488
  17.8 58.2 %collective-permute-start.10 = (bf16[512,768]{1,0:T(8,128)(2,1)}, bf16[512,768]{1,0:T(8,128)(2,1)}, u32[]{:S(2)}, u32[]{:S(2)}) collective-permute-start(bf16[512,768]{1,0:T(8,128)(2,1)} %param.13), channel_id=1, source_target_pairs={{1,4},{3,6},{4,1},{6,3},{9,12},{11,14},{12,9},{14,11},{17,20},{19,... | collective-permute-start | bytes 2359304 | tf_op jit(solution)/shard_map/ppermute | solution.py:558
  68.5 398.4 %all-gather.7.cloned.1.call-start = ((), (), s32[]{:S(2)}) async-start(), calls=%async_computation.1 | async-start | bytes 2654208 | tf_op jit(solution)/shard_map/all_gather | solution.py:782
  85.7 32.2 %collective-permute-start.17 = (bf16[192,768]{1,0:T(8,128)(2,1)S(1)}, bf16[192,768]{1,0:T(8,128)(2,1)S(1)}, u32[]{:S(2)}, u32[]{:S(2)}) collective-permute-start(bf16[192,768]{1,0:T(8,128)(2,1)S(1)} %pad_maximum_fusion.23), channel_id=1, source_target_pairs={{0,1},{1,0},{2,3},{3,2},{4,5},{5,4},{6,7},{7,6},{8,9},{9,8},{10,11... | collective-permute-start | bytes 884744 | tf_op jit(solution)/shard_map/ppermute | solution.py:488
  88.0 31.7 %collective-permute-start.18 = (bf16[192,768]{1,0:T(8,128)(2,1)S(1)}, bf16[192,768]{1,0:T(8,128)(2,1)S(1)}, u32[]{:S(2)}, u32[]{:S(2)}) collective-permute-start(bf16[192,768]{1,0:T(8,128)(2,1)S(1)} %pad_maximum_fusion.23), channel_id=1, source_target_pairs={{0,2},{1,3},{2,0},{3,1},{4,6},{5,7},{6,4},{7,5},{8,10},{9,11},{10,... | collective-permute-start | bytes 884744 | tf_op jit(solution)/shard_map/ppermute | solution.py:488
  94.5 33.5 %collective-permute-start.19 = (bf16[192,768]{1,0:T(8,128)(2,1)S(1)}, bf16[192,768]{1,0:T(8,128)(2,1)S(1)}, u32[]{:S(2)}, u32[]{:S(2)}) collective-permute-start(bf16[192,768]{1,0:T(8,128)(2,1)S(1)} %pad_maximum_fusion.23), channel_id=1, source_target_pairs={{0,3},{1,2},{2,1},{3,0},{4,7},{5,6},{6,5},{7,4},{8,11},{9,10},{10,... | collective-permute-start | bytes 884744 | tf_op jit(solution)/shard_map/ppermute | solution.py:488
  104.2 26.3 %collective-permute-start.12 = (bf16[384,1536]{1,0:T(8,128)(2,1)S(1)}, bf16[384,1536]{1,0:T(8,128)(2,1)S(1)}, u32[]{:S(2)}, u32[]{:S(2)}) collective-permute-start(bf16[384,1536]{1,0:T(8,128)(2,1)S(1)} %constant_dynamic-update-slice_fusion.refs_4_), channel_id=1, source_target_pairs={{0,16},{16,0},{1,17},{17,1},{2,18},{18,2},{3,19},{19,3},{4,20},{20... | collective-permute-start | bytes 3538952 | tf_op jit(solution)/shard_map/ppermute | solution.py:476
  138.8 26.5 %collective-permute-start.23 = (bf16[4,96,768]{2,1,0:T(8,128)(2,1)S(1)}, bf16[4,96,768]{2,1,0:T(8,128)(2,1)S(1)}, u32[]{:S(2)}, u32[]{:S(2)}) collective-permute-start(bf16[4,96,768]{2,1,0:T(8,128)(2,1)S(1)} %pad_maximum_fusion.15), channel_id=1, source_target_pairs={{0,8},{8,0},{1,9},{9,1},{2,10},{10,2},{3,11},{11,3},{4,12},{12,4},... | collective-permute-start | bytes 1769480 | tf_op jit(solution)/shard_map/ppermute | solution.py:476
  250.0 27.2 %collective-permute-start.29 = (bf16[384,1536]{1,0:T(8,128)(2,1)S(1)}, bf16[384,1536]{1,0:T(8,128)(2,1)S(1)}, u32[]{:S(2)}, u32[]{:S(2)}) collective-permute-start(bf16[384,1536]{1,0:T(8,128)(2,1)S(1)} %add_convert_fusion.8), channel_id=1, source_target_pairs={{0,16},{16,0},{1,17},{17,1},{2,18},{18,2},{3,19},{19,3},{4,20},{20... | collective-permute-start | bytes 3538952 | tf_op jit(solution)/shard_map/ppermute | solution.py:476
  251.2 27.1 %collective-permute-start.30 = (bf16[384,1536]{1,0:T(8,128)(2,1)}, bf16[384,1536]{1,0:T(8,128)(2,1)S(1)}, u32[]{:S(2)}, u32[]{:S(2)}) collective-permute-start(bf16[384,1536]{1,0:T(8,128)(2,1)} %add_convert_fusion.7), channel_id=1, source_target_pairs={{0,8},{8,0},{1,9},{9,1},{2,10},{10,2},{3,11},{11,3},{4,12},{12,4},... | collective-permute-start | bytes 3538952 | tf_op jit(solution)/shard_map/ppermute | solution.py:476
  306.9 29.3 %collective-permute-start.36 = (bf16[4,2,48,768]{3,2,1,0:T(8,128)(2,1)S(1)}, bf16[4,2,48,768]{3,2,1,0:T(8,128)(2,1)S(1)}, u32[]{:S(2)}, u32[]{:S(2)}) collective-permute-start(bf16[4,2,48,768]{3,2,1,0:T(8,128)(2,1)S(1)} %get-tuple-element.281), channel_id=1, source_target_pairs={{0,16},{16,0},{1,17},{17,1},{2,18},{18,2},{3,19},{19,3},{4,20},{20... | collective-permute-start | bytes 1769480 | tf_op jit(solution)/shard_map/ppermute | solution.py:476
  308.3 28.0 %collective-permute-start.37 = (bf16[4,2,48,768]{3,2,1,0:T(8,128)(2,1)S(1)}, bf16[4,2,48,768]{3,2,1,0:T(8,128)(2,1)S(1)}, u32[]{:S(2)}, u32[]{:S(2)}) collective-permute-start(bf16[4,2,48,768]{3,2,1,0:T(8,128)(2,1)S(1)} %get-tuple-element.282), channel_id=1, source_target_pairs={{0,8},{8,0},{1,9},{9,1},{2,10},{10,2},{3,11},{11,3},{4,12},{12,4},... | collective-permute-start | bytes 1769480 | tf_op jit(solution)/shard_map/ppermute | solution.py:476
  352.1 114.8 %all-gather.9.cloned.1.call-start = ((), (), s32[]{:S(2)}) async-start(), calls=%async_computation.2 | async-start | bytes 1327104 | tf_op jit(solution)/shard_map/all_gather | solution.py:782
  361.9 33.3 %collective-permute-start.44 = (bf16[384,1536]{1,0:T(8,128)(2,1)S(1)}, bf16[384,1536]{1,0:T(8,128)(2,1)S(1)}, u32[]{:S(2)}, u32[]{:S(2)}) collective-permute-start(bf16[384,1536]{1,0:T(8,128)(2,1)S(1)} %get-tuple-element.314), channel_id=1, source_target_pairs={{0,16},{16,0},{1,17},{17,1},{2,18},{18,2},{3,19},{19,3},{4,20},{20... | collective-permute-start | bytes 3538952 | tf_op jit(solution)/shard_map/ppermute | solution.py:476
  363.2 33.6 %collective-permute-start.45 = (bf16[384,1536]{1,0:T(8,128)(2,1)S(1)}, bf16[384,1536]{1,0:T(8,128)(2,1)S(1)}, u32[]{:S(2)}, u32[]{:S(2)}) collective-permute-start(bf16[384,1536]{1,0:T(8,128)(2,1)S(1)} %get-tuple-element.315), channel_id=1, source_target_pairs={{0,8},{8,0},{1,9},{9,1},{2,10},{10,2},{3,11},{11,3},{4,12},{12,4},... | collective-permute-start | bytes 3538952 | tf_op jit(solution)/shard_map/ppermute | solution.py:476
  363.5 34.3 %collective-permute-start.46 = (bf16[96,768]{1,0:T(8,128)(2,1)S(1)}, bf16[96,768]{1,0:T(8,128)(2,1)S(1)}, u32[]{:S(2)}, u32[]{:S(2)}) collective-permute-start(bf16[96,768]{1,0:T(8,128)(2,1)S(1)} %get-tuple-element.323), channel_id=1, source_target_pairs={{0,1},{1,0},{2,3},{3,2},{4,5},{5,4},{6,7},{7,6},{8,9},{9,8},{10,11... | collective-permute-start | bytes 442376 | tf_op jit(solution)/shard_map/ppermute | solution.py:488
  363.5 34.3 %collective-permute-start.47 = (bf16[96,768]{1,0:T(8,128)(2,1)S(1)}, bf16[96,768]{1,0:T(8,128)(2,1)S(1)}, u32[]{:S(2)}, u32[]{:S(2)}) collective-permute-start(bf16[96,768]{1,0:T(8,128)(2,1)S(1)} %get-tuple-element.324), channel_id=1, source_target_pairs={{0,2},{1,3},{2,0},{3,1},{4,6},{5,7},{6,4},{7,5},{8,10},{9,11},{10,... | collective-permute-start | bytes 442376 | tf_op jit(solution)/shard_map/ppermute | solution.py:488
  365.8 32.1 %collective-permute-start.48 = (bf16[96,768]{1,0:T(8,128)(2,1)S(1)}, bf16[96,768]{1,0:T(8,128)(2,1)S(1)}, u32[]{:S(2)}, u32[]{:S(2)}) collective-permute-start(bf16[96,768]{1,0:T(8,128)(2,1)S(1)} %get-tuple-element.325), channel_id=1, source_target_pairs={{0,3},{1,2},{2,1},{3,0},{4,7},{5,6},{6,5},{7,4},{8,11},{9,10},{10,... | collective-permute-start | bytes 442376 | tf_op jit(solution)/shard_map/ppermute | solution.py:488
  414.4 92.1 %all-gather.11.cloned.1.call-start = ((), (), s32[]{:S(2)}) async-start(), calls=%async_computation.3 | async-start | bytes 2654208 | tf_op jit(solution)/shard_map/all_gather | solution.py:782
  435.5 29.4 %collective-permute-start.53 = (bf16[4,2,48,768]{3,2,0,1:T(8,128)(2,1)S(1)}, bf16[4,2,48,768]{3,2,0,1:T(8,128)(2,1)S(1)}, u32[]{:S(2)}, u32[]{:S(2)}) collective-permute-start(bf16[4,2,48,768]{3,2,0,1:T(8,128)(2,1)S(1)} %get-tuple-element.352), channel_id=1, source_target_pairs={{0,8},{8,0},{1,9},{9,1},{2,10},{10,2},{3,11},{11,3},{4,12},{12,4},... | collective-permute-start | bytes 1769480 | tf_op jit(solution)/shard_map/ppermute | solution.py:476
  436.5 28.4 %collective-permute-start.54 = (bf16[4,2,48,768]{3,2,0,1:T(8,128)(2,1)S(1)}, bf16[4,2,48,768]{3,2,0,1:T(8,128)(2,1)S(1)}, u32[]{:S(2)}, u32[]{:S(2)}) collective-permute-start(bf16[4,2,48,768]{3,2,0,1:T(8,128)(2,1)S(1)} %get-tuple-element.353), channel_id=1, source_target_pairs={{0,16},{16,0},{1,17},{17,1},{2,18},{18,2},{3,19},{19,3},{4,20},{20... | collective-permute-start | bytes 1769480 | tf_op jit(solution)/shard_map/ppermute | solution.py:476
  436.5 28.4 %collective-permute-start.55 = (bf16[4,2,48,768]{3,2,0,1:T(8,128)(2,1)S(1)}, bf16[4,2,48,768]{3,2,0,1:T(8,128)(2,1)S(1)}, u32[]{:S(2)}, u32[]{:S(2)}) collective-permute-start(bf16[4,2,48,768]{3,2,0,1:T(8,128)(2,1)S(1)} %get-tuple-element.354), channel_id=1, source_target_pairs={{0,24},{8,16},{16,8},{24,0},{1,25},{9,17},{17,9},{25,1},{2,26},{10... | collective-permute-start | bytes 1769480 | tf_op jit(solution)/shard_map/ppermute | solution.py:496
  (159 other events, 1684.6 us)
Sparse Core Ops, SparseCore 0:
  68.6 107.1 all-gather.4
  352.2 36.0 all-gather.6
  414.5 25.7 all-gather.8
  467.0 34.5 all-gather.10

commit v4 on v3

--- a/solution.py
+++ b/solution.py
@@ -674,7 +674,6 @@
     for layer_idx in range(layer_count):
         if layer_idx == 1:
             attention_weights[1] = attention_whole(own_attention)
-            cotangent_rows = swap_rows(tie(cotangent, own_attention))
         weight_kv, weight_q, weight_o = attention_weights[layer_idx]
         layer_input = stream
         normed = normalize(stream, gains[layer_idx, 0], shifts[layer_idx, 0]).astype(bf16)
@@ -705,6 +704,7 @@
                 unit_weights[0], normed_two, first, second
             )
             received = [over("x", first), over("y", second)]
+            cotangent_rows = swap_rows(tie(cotangent, first, second))
         activated, slopes, stream = units_forward(
             normed_two,
             middle,
@@ -713,7 +713,9 @@
             unit_weights[layer_idx],
         )
         if layer_idx == 0:
-            activated, slopes, stream, received = together(activated, slopes, stream, received)
+            activated, slopes, stream, received, cotangent_rows = together(
+                activated, slopes, stream, received, cotangent_rows
+            )
             own_attention = attention_own(first, second, received)
         saved.append(
             (

time: 542 us -> 534 us (0.985)
  starting transfers between devices: 80.2 us -> 72.8 us
    unnamed x231 -> x233, local copies, waits for them, and re-layouts: 17.9 us -> 18.9 us
  transfers between devices with their start and end apart: 71 -> 71, of which waited for: 27 -> 28; matrix products, arithmetic and copies ran while one was open for 19% -> 20% of each run, Pallas kernels for 21% -> 21%
where the time goes in v4:
time: 534 us; the launch traced here: 528 us
  Pallas kernels  147 us (28%)
  waiting for transfers between devices  139 us (26%)
  other arithmetic  77.9 us (15%)
  starting transfers between devices  72.8 us (14%)
  local copies, waits for them, and re-layouts  48.4 us (9%)
  matrix products  25.4 us (5%)
  between operations  17.9 us (3%)
    ppermute x40, waiting for transfers between devices, over(): return lax.ppermute(array, axis, flip_pair)  71.1 us
    ppermute x21, waiting for transfers between devices, z_three(): lax.ppermute(block, 'z', z_pairs(step + 1))  62.2 us
    pallas_call x2, Pallas kernels, units_backward(): pl.pallas_call(functools.partial(units_backward_kernel, len(weights), row...  41.4 us
    ppermute x40, starting transfers between devices, over(): return lax.ppermute(array, axis, flip_pair)  40.8 us
    pallas_call x2, Pallas kernels, attend_backward(): pl.pallas_call(attend_backward_kernel, grid_spec=pltpu.PrefetchScalarGrid...  38.3 us
    convert_element_type x26, other arithmetic, add_low(): return total.astype(bf16)  31.1 us
    pallas_call x2, Pallas kernels, units_forward(): pl.pallas_call(functools.partial(units_forward_kernel, len(weights), rows...  30.6 us
    ppermute x21, starting transfers between devices, z_three(): lax.ppermute(block, 'z', z_pairs(step + 1))  26.3 us
  transfers between devices with their start and end apart: 71, of which 28 were waited for; matrix products, arithmetic and copies ran while one was open for 20% of the time, Pallas kernels for 21%

profile of v4, /device:TPU:9, one launch (start us, length us, event | category | flops | bytes accessed | tf_op | source)
XLA Modules:
  0.0 528.4 jit_solution(8790470398560219442)
XLA Ops:
  30.0 5.7 %collective-permute-done.3 = bf16[208,768]{1,0:T(8,128)(2,1)} collective-permute-done((bf16[208,768]{1,0:T(8,128)(2,1)}, bf16[208,768]{1,0:T(8,128)(2,1)}, u32[]{:S(2)}, u32[]{:S(2)}) %collective-permute-start.3) | collective-permute-done | bytes 319520 | tf_op jit(solution)/shard_map/ppermute | solution.py:488
  36.7 4.8 collective-permute-done.2
  69.8 5.1 collective-permute-done.13
  96.5 7.7 %collective-permute-done.15 = bf16[192,1536]{1,0:T(8,128)(2,1)S(1)} collective-permute-done((bf16[192,1536]{1,0:T(8,128)(2,1)S(1)}, bf16[192,1536]{1,0:T(8,128)(2,1)S(1)}, u32[]{:S(2)}, u32[]{:S(2)}) %collective-permute-start.15) | collective-permute-done | bytes 589856 | tf_op jit(solution)/shard_map/ppermute | solution.py:476
  105.8 12.0 %attend_forward.2 = (bf16[768,512]{1,0:T(8,128)(2,1)S(1)}, f32[4,8,512]{2,1,0:T(8,128)S(1)}) custom-call(s32[2]{0:T(128)S(1)} %pad_add_fusion.1.info, bf16[768,512]{1,0:T(8,128)(2,1)S(1)} %add_convert_fusion.15.queries, bf16[1536,512]{1,0:T(8,128)(2,1)S(1)} %fusion.kv_own, bf16[1536,512]{1,0:T(8,128)(2,1)S(1)} %collective-permute-done.11.kv_other), custom_call_target="tpu_custom_call" | custom-call | flops 16149000192 | bytes 51660000 | tf_op jit(solution)/shard_map/attend_forward/pallas_call | solution.py:142
  119.8 8.2 %collective-permute-done.19 = bf16[192,768]{1,0:T(8,128)(2,1)S(1)} collective-permute-done((bf16[192,768]{1,0:T(8,128)(2,1)S(1)}, bf16[192,768]{1,0:T(8,128)(2,1)S(1)}, u32[]{:S(2)}, u32[]{:S(2)}) %collective-permute-start.19) | collective-permute-done | bytes 294944 | tf_op jit(solution)/shard_map/ppermute | solution.py:488
  142.6 15.6 %units_forward.2 = (bf16[512,3072]{1,0:T(8,128)(2,1)}, bf16[512,3072]{1,0:T(8,128)(2,1)}, f32[512,768]{1,0:T(8,128)S(1)}) custom-call(bf16[512,768]{1,0:T(8,128)(2,1)S(1)} %add_convert_fusion.14.normed, f32[512,768]{1,0:T(8,128)S(1)} %get-tuple-element.561.middle.values, f32[8,1,384]{2,1,0:T(1,128)S(1)} %broadcast_in_dim_reshape.6.unit_bias, ...), custom_call_target="tpu_custom_call" | custom-call | flops 19609499648 | bytes 62730000 | tf_op jit(solution)/shard_map/units_forward/pallas_call | solution.py:244
  159.3 6.0 %collective-permute-done.23 = bf16[4,96,768]{2,1,0:T(8,128)(2,1)S(1)} collective-permute-done((bf16[4,96,768]{2,1,0:T(8,128)(2,1)S(1)}, bf16[4,96,768]{2,1,0:T(8,128)(2,1)S(1)}, u32[]{:S(2)}, u32[]{:S(2)}) %collective-permute-start.23) | collective-permute-done | bytes 589856 | tf_op jit(solution)/shard_map/ppermute | solution.py:476
  169.2 4.9 collective-permute-done.26
  185.5 13.3 %attend_forward.3 = (bf16[768,512]{1,0:T(8,128)(2,1)S(1)}, f32[4,8,512]{2,1,0:T(8,128)S(1)}) custom-call(s32[2]{0:T(128)S(1)} %pad_add_fusion.1.info, bf16[768,512]{1,0:T(8,128)(2,1)S(1)} %add_convert_fusion.12.queries, bf16[1536,512]{1,0:T(8,128)(2,1)S(1)} %fusion.1.kv_own, bf16[1536,512]{1,0:T(8,128)(2,1)} %collective-permute-done.27.kv_other), custom_call_target="tpu_custom_call" | custom-call | flops 16149000192 | bytes 51660000 | tf_op jit(solution)/shard_map/attend_forward/pallas_call | solution.py:142
  202.4 15.0 %units_forward.3 = (bf16[512,3072]{1,0:T(8,128)(2,1)S(1)}, bf16[512,3072]{1,0:T(8,128)(2,1)S(1)}, f32[512,768]{1,0:T(8,128)S(1)}) custom-call(bf16[512,768]{1,0:T(8,128)(2,1)S(1)} %copy-done.9, f32[512,768]{1,0:T(8,128)S(1)} %get-tuple-element.563.middle.values, f32[8,1,384]{2,1,0:T(1,128)S(1)} %broadcast_in_dim_reshape.7.unit_bias, ...), custom_call_target="tpu_custom_call" | custom-call | flops 19609499648 | bytes 62730000 | tf_op jit(solution)/shard_map/units_forward/pallas_call | solution.py:244
  217.4 19.6 %units_backward.2 = (bf16[1536,1536]{1,0:T(8,128)(2,1)S(1)}, bf16[1536,1536]{1,0:T(8,128)(2,1)}, f32[512,768]{1,0:T(8,128)S(1)}, f32[8,1,384]{2,1,0:T(1,128)S(1)}) custom-call(s32[8]{0:T(128)S(1)} %fusion.27.place, bf16[512,768]{1,0:T(8,128)(2,1)S(1)} %copy-done.8, bf16[512,768]{1,0:T(8,128)(2,1)S(1)} %copy-done.9, ...), custom_call_target="tpu_custom_call" | custom-call | flops 23069999104 | bytes 73800000 | tf_op jit(solution)/shard_map/units_backward/pallas_call | solution.py:331
  249.5 19.6 %attend_backward.2 = (bf16[768,512]{1,0:T(8,128)(2,1)S(1)}, f32[1536,512]{1,0:T(8,128)S(1)}, bf16[1536,512]{1,0:T(8,128)(2,1)S(1)}) custom-call(s32[2]{0:T(128)S(1)} %pad_add_fusion.1.info, bf16[768,512]{1,0:T(8,128)(2,1)S(1)} %copy-done.40, bf16[1536,512]{1,0:T(8,128)(2,1)S(1)} %copy-done.21, bf16[1536,512]{1,0:T(8,128)(2,1)} %collective-permute-done.27.kv_other, ...), custom_call_target="tpu_custom_call" | custom-call | flops 24223500288 | bytes 77490000 | tf_op jit(solution)/shard_map/attend_backward/pallas_call | solution.py:164
  293.6 6.5 %collective-permute-done.34 = bf16[2,96,1536]{2,1,0:T(8,128)(2,1)S(1)} collective-permute-done((bf16[2,96,1536]{2,1,0:T(8,128)(2,1)}, bf16[2,96,1536]{2,1,0:T(8,128)(2,1)S(1)}, u32[]{:S(2)}, u32[]{:S(2)}) %collective-permute-start.34) | collective-permute-done | bytes 589856 | tf_op jit(solution)/shard_map/ppermute | solution.py:476
  308.8 21.8 %units_backward.3 = (bf16[1536,1536]{1,0:T(8,128)(2,1)}, bf16[1536,1536]{1,0:T(8,128)(2,1)}, f32[512,768]{1,0:T(8,128)S(1)}, f32[8,1,384]{2,1,0:T(1,128)S(1)}) custom-call(s32[8]{0:T(128)S(1)} %iota.13.place, bf16[512,768]{1,0:T(8,128)(2,1)S(1)} %get-tuple-element.276.grad_down, bf16[512,768]{1,0:T(8,128)(2,1)S(1)} %copy-done.7, ...), custom_call_target="tpu_custom_call" | custom-call | flops 23069999104 | bytes 73800000 | tf_op jit(solution)/shard_map/units_backward/pallas_call | solution.py:331
  351.2 6.0 %add_convert_fusion.3 = (bf16[384,1536]{1,0:T(8,128)(2,1)S(1)}, bf16[384,1536]{1,0:T(8,128)(2,1)S(1)}, bf16[384,1536]{1,0:T(8,128)(2,1)}, bf16[384,1536]{1,0:T(8,128)(2,1)}) fusion(bf16[1536,1536]{1,0:T(8,128)(2,1)} %collective-permute-done.41, bf16[1536,1536]{1,0:T(8,128)(2,1)} %get-tuple-element.305), kind=kLoop, calls=%fused_computation.15 | loop fusion | flops 9437184 | bytes 14155776 | tf_op jit(solution)/shard_map/convert_element_type | solution.py:504
  363.6 18.6 %attend_backward.3 = (bf16[768,512]{1,0:T(8,128)(2,1)S(1)}, f32[1536,512]{1,0:T(8,128)S(1)}, bf16[1536,512]{1,0:T(8,128)(2,1)S(1)}) custom-call(s32[2]{0:T(128)S(1)} %pad_add_fusion.1.info, bf16[768,512]{1,0:T(8,128)(2,1)S(1)} %copy-done.42, bf16[1536,512]{1,0:T(8,128)(2,1)S(1)} %copy-done.17, bf16[1536,512]{1,0:T(8,128)(2,1)S(1)} %copy-done.19, ...), custom_call_target="tpu_custom_call" | custom-call | flops 24223500288 | bytes 77490000 | tf_op jit(solution)/shard_map/attend_backward/pallas_call | solution.py:164
  383.9 8.9 %collective-permute-done.44 = bf16[384,1536]{1,0:T(8,128)(2,1)S(1)} collective-permute-done((bf16[384,1536]{1,0:T(8,128)(2,1)S(1)}, bf16[384,1536]{1,0:T(8,128)(2,1)S(1)}, u32[]{:S(2)}, u32[]{:S(2)}) %collective-permute-start.44) | collective-permute-done | bytes 1179680 | tf_op jit(solution)/shard_map/ppermute | solution.py:476
  417.4 8.6 %collective-permute-done.51 = bf16[2,96,1536]{2,1,0:T(8,128)(2,1)} collective-permute-done((bf16[2,96,1536]{2,1,0:T(8,128)(2,1)}, bf16[2,96,1536]{2,1,0:T(8,128)(2,1)}, u32[]{:S(2)}, u32[]{:S(2)}) %collective-permute-start.51) | collective-permute-done | bytes 589856 | tf_op jit(solution)/shard_map/ppermute | solution.py:476
  443.0 11.5 %collective-permute-done.57 = bf16[96,1536]{1,0:T(8,128)(2,1)S(1)} collective-permute-done((bf16[96,1536]{1,0:T(8,128)(2,1)S(1)}, bf16[96,1536]{1,0:T(8,128)(2,1)S(1)}, u32[]{:S(2)}, u32[]{:S(2)}) %collective-permute-start.57) | collective-permute-done | bytes 294944 | tf_op jit(solution)/shard_map/ppermute | solution.py:488
  454.5 7.9 %collective-permute-done.58 = bf16[96,1536]{1,0:T(8,128)(2,1)S(1)} collective-permute-done((bf16[96,1536]{1,0:T(8,128)(2,1)S(1)}, bf16[96,1536]{1,0:T(8,128)(2,1)S(1)}, u32[]{:S(2)}, u32[]{:S(2)}) %collective-permute-start.58) | collective-permute-done | bytes 294944 | tf_op jit(solution)/shard_map/ppermute | solution.py:488
  474.1 11.1 %collective-permute-done.61 = bf16[144,768]{1,0:T(8,128)(2,1)S(1)} collective-permute-done((bf16[144,768]{1,0:T(8,128)(2,1)S(1)}, bf16[144,768]{1,0:T(8,128)(2,1)S(1)}, u32[]{:S(2)}, u32[]{:S(2)}) %collective-permute-start.61) | collective-permute-done | bytes 221216 | tf_op jit(solution)/shard_map/ppermute | solution.py:488
  490.1 6.1 %collective-permute-done.62 = bf16[144,768]{1,0:T(8,128)(2,1)S(1)} collective-permute-done((bf16[144,768]{1,0:T(8,128)(2,1)S(1)}, bf16[144,768]{1,0:T(8,128)(2,1)S(1)}, u32[]{:S(2)}, u32[]{:S(2)}) %collective-permute-start.62) | collective-permute-done | bytes 221216 | tf_op jit(solution)/shard_map/ppermute | solution.py:476
  496.5 5.5 %collective-permute-done.64 = bf16[144,768]{1,0:T(8,128)(2,1)S(1)} collective-permute-done((bf16[144,768]{1,0:T(8,128)(2,1)S(1)}, bf16[144,768]{1,0:T(8,128)(2,1)S(1)}, u32[]{:S(2)}, u32[]{:S(2)}) %collective-permute-start.64) | collective-permute-done | bytes 221216 | tf_op jit(solution)/shard_map/ppermute | solution.py:496
  (626 shorter events, 260.5 us)
Async XLA Ops:
  7.2 194.0 %all-gather.5.cloned.1.call-start = ((), (), s32[]{:S(2)}) async-start(), calls=%async_computation | async-start | bytes 9732096 | tf_op jit(solution)/shard_map/all_gather | solution.py:660
  14.3 27.1 %collective-permute-start.2 = (bf16[208,768]{1,0:T(8,128)(2,1)}, bf16[208,768]{1,0:T(8,128)(2,1)}, u32[]{:S(2)}, u32[]{:S(2)}) collective-permute-start(bf16[208,768]{1,0:T(8,128)(2,1)} %pad_maximum_fusion.18), channel_id=1, source_target_pairs={{0,2},{1,3},{2,0},{3,1},{4,6},{5,7},{6,4},{7,5},{8,10},{9,11},{10,... | collective-permute-start | bytes 958472 | tf_op jit(solution)/shard_map/ppermute | solution.py:488
  15.4 27.1 %collective-permute-start.1 = (bf16[208,768]{1,0:T(8,128)(2,1)}, bf16[208,768]{1,0:T(8,128)(2,1)}, u32[]{:S(2)}, u32[]{:S(2)}) collective-permute-start(bf16[208,768]{1,0:T(8,128)(2,1)} %pad_maximum_fusion.18), channel_id=1, source_target_pairs={{0,1},{1,0},{2,3},{3,2},{4,5},{5,4},{6,7},{7,6},{8,9},{9,8},{10,11... | collective-permute-start | bytes 958472 | tf_op jit(solution)/shard_map/ppermute | solution.py:488
  17.8 58.2 %collective-permute-start.10 = (bf16[512,768]{1,0:T(8,128)(2,1)}, bf16[512,768]{1,0:T(8,128)(2,1)}, u32[]{:S(2)}, u32[]{:S(2)}) collective-permute-start(bf16[512,768]{1,0:T(8,128)(2,1)} %param.13), channel_id=1, source_target_pairs={{1,4},{3,6},{4,1},{6,3},{9,12},{11,14},{12,9},{14,11},{17,20},{19,... | collective-permute-start | bytes 2359304 | tf_op jit(solution)/shard_map/ppermute | solution.py:558
  68.5 395.9 %all-gather.7.cloned.1.call-start = ((), (), s32[]{:S(2)}) async-start(), calls=%async_computation.1 | async-start | bytes 2654208 | tf_op jit(solution)/shard_map/all_gather | solution.py:784
  85.7 32.2 %collective-permute-start.17 = (bf16[192,768]{1,0:T(8,128)(2,1)S(1)}, bf16[192,768]{1,0:T(8,128)(2,1)S(1)}, u32[]{:S(2)}, u32[]{:S(2)}) collective-permute-start(bf16[192,768]{1,0:T(8,128)(2,1)S(1)} %pad_maximum_fusion.23), channel_id=1, source_target_pairs={{0,1},{1,0},{2,3},{3,2},{4,5},{5,4},{6,7},{7,6},{8,9},{9,8},{10,11... | collective-permute-start | bytes 884744 | tf_op jit(solution)/shard_map/ppermute | solution.py:488
  88.1 31.6 %collective-permute-start.18 = (bf16[192,768]{1,0:T(8,128)(2,1)S(1)}, bf16[192,768]{1,0:T(8,128)(2,1)S(1)}, u32[]{:S(2)}, u32[]{:S(2)}) collective-permute-start(bf16[192,768]{1,0:T(8,128)(2,1)S(1)} %pad_maximum_fusion.23), channel_id=1, source_target_pairs={{0,2},{1,3},{2,0},{3,1},{4,6},{5,7},{6,4},{7,5},{8,10},{9,11},{10,... | collective-permute-start | bytes 884744 | tf_op jit(solution)/shard_map/ppermute | solution.py:488
  94.5 33.5 %collective-permute-start.19 = (bf16[192,768]{1,0:T(8,128)(2,1)S(1)}, bf16[192,768]{1,0:T(8,128)(2,1)S(1)}, u32[]{:S(2)}, u32[]{:S(2)}) collective-permute-start(bf16[192,768]{1,0:T(8,128)(2,1)S(1)} %pad_maximum_fusion.23), channel_id=1, source_target_pairs={{0,3},{1,2},{2,1},{3,0},{4,7},{5,6},{6,5},{7,4},{8,11},{9,10},{10,... | collective-permute-start | bytes 884744 | tf_op jit(solution)/shard_map/ppermute | solution.py:488
  104.2 26.3 %collective-permute-start.12 = (bf16[384,1536]{1,0:T(8,128)(2,1)S(1)}, bf16[384,1536]{1,0:T(8,128)(2,1)S(1)}, u32[]{:S(2)}, u32[]{:S(2)}) collective-permute-start(bf16[384,1536]{1,0:T(8,128)(2,1)S(1)} %constant_dynamic-update-slice_fusion.refs_4_), channel_id=1, source_target_pairs={{0,16},{16,0},{1,17},{17,1},{2,18},{18,2},{3,19},{19,3},{4,20},{20... | collective-permute-start | bytes 3538952 | tf_op jit(solution)/shard_map/ppermute | solution.py:476
  138.8 26.5 %collective-permute-start.23 = (bf16[4,96,768]{2,1,0:T(8,128)(2,1)S(1)}, bf16[4,96,768]{2,1,0:T(8,128)(2,1)S(1)}, u32[]{:S(2)}, u32[]{:S(2)}) collective-permute-start(bf16[4,96,768]{2,1,0:T(8,128)(2,1)S(1)} %pad_maximum_fusion.15), channel_id=1, source_target_pairs={{0,8},{8,0},{1,9},{9,1},{2,10},{10,2},{3,11},{11,3},{4,12},{12,4},... | collective-permute-start | bytes 1769480 | tf_op jit(solution)/shard_map/ppermute | solution.py:476
  247.6 27.4 %collective-permute-start.29 = (bf16[384,1536]{1,0:T(8,128)(2,1)S(1)}, bf16[384,1536]{1,0:T(8,128)(2,1)S(1)}, u32[]{:S(2)}, u32[]{:S(2)}) collective-permute-start(bf16[384,1536]{1,0:T(8,128)(2,1)S(1)} %add_convert_fusion.8), channel_id=1, source_target_pairs={{0,16},{16,0},{1,17},{17,1},{2,18},{18,2},{3,19},{19,3},{4,20},{20... | collective-permute-start | bytes 3538952 | tf_op jit(solution)/shard_map/ppermute | solution.py:476
  248.8 27.2 %collective-permute-start.30 = (bf16[384,1536]{1,0:T(8,128)(2,1)}, bf16[384,1536]{1,0:T(8,128)(2,1)S(1)}, u32[]{:S(2)}, u32[]{:S(2)}) collective-permute-start(bf16[384,1536]{1,0:T(8,128)(2,1)} %add_convert_fusion.7), channel_id=1, source_target_pairs={{0,8},{8,0},{1,9},{9,1},{2,10},{10,2},{3,11},{11,3},{4,12},{12,4},... | collective-permute-start | bytes 3538952 | tf_op jit(solution)/shard_map/ppermute | solution.py:476
  304.6 28.3 %collective-permute-start.36 = (bf16[4,2,48,768]{3,2,1,0:T(8,128)(2,1)S(1)}, bf16[4,2,48,768]{3,2,1,0:T(8,128)(2,1)S(1)}, u32[]{:S(2)}, u32[]{:S(2)}) collective-permute-start(bf16[4,2,48,768]{3,2,1,0:T(8,128)(2,1)S(1)} %get-tuple-element.283), channel_id=1, source_target_pairs={{0,16},{16,0},{1,17},{17,1},{2,18},{18,2},{3,19},{19,3},{4,20},{20... | collective-permute-start | bytes 1769480 | tf_op jit(solution)/shard_map/ppermute | solution.py:476
  305.0 27.9 %collective-permute-start.37 = (bf16[4,2,48,768]{3,2,1,0:T(8,128)(2,1)S(1)}, bf16[4,2,48,768]{3,2,1,0:T(8,128)(2,1)S(1)}, u32[]{:S(2)}, u32[]{:S(2)}) collective-permute-start(bf16[4,2,48,768]{3,2,1,0:T(8,128)(2,1)S(1)} %get-tuple-element.284), channel_id=1, source_target_pairs={{0,8},{8,0},{1,9},{9,1},{2,10},{10,2},{3,11},{11,3},{4,12},{12,4},... | collective-permute-start | bytes 1769480 | tf_op jit(solution)/shard_map/ppermute | solution.py:476
  349.3 115.1 %all-gather.9.cloned.1.call-start = ((), (), s32[]{:S(2)}) async-start(), calls=%async_computation.2 | async-start | bytes 1327104 | tf_op jit(solution)/shard_map/all_gather | solution.py:784
  359.5 33.3 %collective-permute-start.44 = (bf16[384,1536]{1,0:T(8,128)(2,1)S(1)}, bf16[384,1536]{1,0:T(8,128)(2,1)S(1)}, u32[]{:S(2)}, u32[]{:S(2)}) collective-permute-start(bf16[384,1536]{1,0:T(8,128)(2,1)S(1)} %get-tuple-element.316), channel_id=1, source_target_pairs={{0,16},{16,0},{1,17},{17,1},{2,18},{18,2},{3,19},{19,3},{4,20},{20... | collective-permute-start | bytes 3538952 | tf_op jit(solution)/shard_map/ppermute | solution.py:476
  359.9 34.4 %collective-permute-start.45 = (bf16[384,1536]{1,0:T(8,128)(2,1)S(1)}, bf16[384,1536]{1,0:T(8,128)(2,1)S(1)}, u32[]{:S(2)}, u32[]{:S(2)}) collective-permute-start(bf16[384,1536]{1,0:T(8,128)(2,1)S(1)} %get-tuple-element.317), channel_id=1, source_target_pairs={{0,8},{8,0},{1,9},{9,1},{2,10},{10,2},{3,11},{11,3},{4,12},{12,4},... | collective-permute-start | bytes 3538952 | tf_op jit(solution)/shard_map/ppermute | solution.py:476
  360.9 34.4 %collective-permute-start.46 = (bf16[96,768]{1,0:T(8,128)(2,1)S(1)}, bf16[96,768]{1,0:T(8,128)(2,1)S(1)}, u32[]{:S(2)}, u32[]{:S(2)}) collective-permute-start(bf16[96,768]{1,0:T(8,128)(2,1)S(1)} %get-tuple-element.325), channel_id=1, source_target_pairs={{0,1},{1,0},{2,3},{3,2},{4,5},{5,4},{6,7},{7,6},{8,9},{9,8},{10,11... | collective-permute-start | bytes 442376 | tf_op jit(solution)/shard_map/ppermute | solution.py:488
  360.9 34.4 %collective-permute-start.47 = (bf16[96,768]{1,0:T(8,128)(2,1)S(1)}, bf16[96,768]{1,0:T(8,128)(2,1)S(1)}, u32[]{:S(2)}, u32[]{:S(2)}) collective-permute-start(bf16[96,768]{1,0:T(8,128)(2,1)S(1)} %get-tuple-element.326), channel_id=1, source_target_pairs={{0,2},{1,3},{2,0},{3,1},{4,6},{5,7},{6,4},{7,5},{8,10},{9,11},{10,... | collective-permute-start | bytes 442376 | tf_op jit(solution)/shard_map/ppermute | solution.py:488
  362.6 32.7 %collective-permute-start.48 = (bf16[96,768]{1,0:T(8,128)(2,1)S(1)}, bf16[96,768]{1,0:T(8,128)(2,1)S(1)}, u32[]{:S(2)}, u32[]{:S(2)}) collective-permute-start(bf16[96,768]{1,0:T(8,128)(2,1)S(1)} %get-tuple-element.327), channel_id=1, source_target_pairs={{0,3},{1,2},{2,1},{3,0},{4,7},{5,6},{6,5},{7,4},{8,11},{9,10},{10,... | collective-permute-start | bytes 442376 | tf_op jit(solution)/shard_map/ppermute | solution.py:488
  412.0 91.6 %all-gather.11.cloned.1.call-start = ((), (), s32[]{:S(2)}) async-start(), calls=%async_computation.3 | async-start | bytes 2654208 | tf_op jit(solution)/shard_map/all_gather | solution.py:784
  432.6 29.8 %collective-permute-start.53 = (bf16[4,2,48,768]{3,2,0,1:T(8,128)(2,1)S(1)}, bf16[4,2,48,768]{3,2,0,1:T(8,128)(2,1)S(1)}, u32[]{:S(2)}, u32[]{:S(2)}) collective-permute-start(bf16[4,2,48,768]{3,2,0,1:T(8,128)(2,1)S(1)} %get-tuple-element.354), channel_id=1, source_target_pairs={{0,8},{8,0},{1,9},{9,1},{2,10},{10,2},{3,11},{11,3},{4,12},{12,4},... | collective-permute-start | bytes 1769480 | tf_op jit(solution)/shard_map/ppermute | solution.py:476
  433.2 29.2 %collective-permute-start.54 = (bf16[4,2,48,768]{3,2,0,1:T(8,128)(2,1)S(1)}, bf16[4,2,48,768]{3,2,0,1:T(8,128)(2,1)S(1)}, u32[]{:S(2)}, u32[]{:S(2)}) collective-permute-start(bf16[4,2,48,768]{3,2,0,1:T(8,128)(2,1)S(1)} %get-tuple-element.355), channel_id=1, source_target_pairs={{0,16},{16,0},{1,17},{17,1},{2,18},{18,2},{3,19},{19,3},{4,20},{20... | collective-permute-start | bytes 1769480 | tf_op jit(solution)/shard_map/ppermute | solution.py:476
  434.3 28.1 %collective-permute-start.55 = (bf16[4,2,48,768]{3,2,0,1:T(8,128)(2,1)S(1)}, bf16[4,2,48,768]{3,2,0,1:T(8,128)(2,1)S(1)}, u32[]{:S(2)}, u32[]{:S(2)}) collective-permute-start(bf16[4,2,48,768]{3,2,0,1:T(8,128)(2,1)S(1)} %get-tuple-element.356), channel_id=1, source_target_pairs={{0,24},{8,16},{16,8},{24,0},{1,25},{9,17},{17,9},{25,1},{2,26},{10... | collective-permute-start | bytes 1769480 | tf_op jit(solution)/shard_map/ppermute | solution.py:496
  (160 other events, 1704.8 us)
Sparse Core Ops, SparseCore 0:
  68.6 107.1 all-gather.4
  349.4 35.0 all-gather.6
  412.2 24.4 all-gather.8
  464.5 33.0 all-gather.10

commit v5 on v4

--- a/solution.py
+++ b/solution.py
@@ -439,34 +439,36 @@
     )(values, grad, kept, gain, *rows)
 
 
-def unit_results_kernel(own, even, up, down):
+def unit_results_kernel(grads, *refs):
+    up, down = refs[-2:]
     width = down.shape[2]
-    for layer, grads in enumerate((own, even)):
-        up[layer] = grads[:, :width].astype(f32).T
-        down[layer] = grads[:, width:].astype(f32)
-
-
-def unit_results(own, even):
-    units, double = own.shape
+    up[0] = grads[:, :width].astype(f32).T
+    down[0] = grads[:, width:].astype(f32)
+
+
+def unit_results(layer, grads, *started):
+    units, double = grads.shape
     width = double // 2
     steps = 3
-    block = pl.BlockSpec((units // steps, double), lambda i: (i, 0))
+    rows = units // steps
     return pl.pallas_call(
         unit_results_kernel,
         grid=(steps,),
-        in_specs=[block, block],
+        in_specs=[pl.BlockSpec((rows, double), lambda i: (i, 0))]
+        + [pl.BlockSpec(memory_space=pl.ANY)] * len(started),
         out_specs=[
-            pl.BlockSpec((2, width, units // steps), lambda i: (0, 0, i)),
-            pl.BlockSpec((2, units // steps, width), lambda i: (0, i, 0)),
+            pl.BlockSpec((1, width, rows), lambda i: (layer, 0, i)),
+            pl.BlockSpec((1, rows, width), lambda i: (layer, i, 0)),
         ],
         out_shape=[
             jax.ShapeDtypeStruct((2, width, units), f32),
             jax.ShapeDtypeStruct((2, units, width), f32),
         ],
+        input_output_aliases={1 + k: k for k in range(len(started))},
         compiler_params=pltpu.CompilerParams(vmem_limit_bytes=24 << 20),
-        cost_estimate=kernel_cost(5e-6),
+        cost_estimate=kernel_cost(3e-6),
         name="unit_results",
-    )(own, even)
+    )(grads, *started)
 
 
 flip_pair = [(0, 1), (1, 0)]
@@ -992,6 +994,7 @@
                 grad_stream, grad_down, attention_received, unit_received
             )
     width = width_all
+    small = pack(unpack(small) + unpack(over("c", small)))
     grad_stream, small, received, unit_received = together(
         grad_stream, small, received, unit_received
     )
@@ -1009,17 +1012,18 @@
     last = over_outer(add_low(last[0], *[block[:rest] for block in received]))
     small = pack(over_outer(four(small, [block[rest:] for block in received])))
     sent = jnp.concatenate([last, small])
+    sent, even_grads = together(sent, even_grads)
     received = yx_three([sent] * 3)
-    received, grad_in = together(received, grad_in)
-    small = pack(four(small, [block[rest:] for block in received]))
+    results = unit_results(1, even_grads)
+    received, grad_in, results = together(received, grad_in, results)
     last = attention_join([last] + [block[:rest] for block in received])
-    sent = jnp.concatenate([last, small])
-    sent, own_grads, even_grads = together(sent, own_grads, even_grads)
-    received = over("c", sent)
-    up_grads, down_grads = unit_results(own_grads, even_grads)
-    received, up_grads, down_grads = together(received, up_grads, down_grads)
-    small = unpack(small) + unpack(received[2 * shard :])
-    first_grads = attention_out(last, received[: 2 * shard])
+    small_received = [block[rest:] for block in received]
+    last, own_grads, small_received, results = together(last, own_grads, small_received, results)
+    received = over("c", last)
+    up_grads, down_grads = unit_results(0, own_grads, *results)
+    small = four(small, small_received)
+    received, up_grads, down_grads, small = together(received, up_grads, down_grads, small)
+    first_grads = attention_out(last, received)
 
     gain_grads = small[0:4].reshape(layer_count, 2, width)
     shift_grads = small[4:8].reshape(layer_count, 2, width)

time: 534 us -> 533 us (level)
    ppermute x40 -> x41, waiting for transfers between devices: 71.1 us -> 66.7 us  [over(): return lax.ppermute(array, axis, flip_pair)]
    unnamed x233 -> x229, local copies, waits for them, and re-layouts: 18.9 us -> 17 us
    ppermute x40 -> x41, starting transfers between devices: 40.8 us -> 40 us  [over(): return lax.ppermute(array, axis, flip_pair)]
  transfers between devices with their start and end apart: 71 -> 72, of which waited for: 28 -> 27; matrix products, arithmetic and copies ran while one was open for 20% -> 20% of each run, Pallas kernels for 21% -> 22%
where the time goes in v5:
time: 533 us; the launch traced here: 528 us
  Pallas kernels  148 us (28%)
  waiting for transfers between devices  137 us (26%)
  other arithmetic  77.1 us (14%)
  starting transfers between devices  74.3 us (14%)
  local copies, waits for them, and re-layouts  47.4 us (9%)
  matrix products  25.4 us (5%)
  between operations  17.9 us (3%)
    ppermute x41, waiting for transfers between devices, over(): return lax.ppermute(array, axis, flip_pair)  66.7 us
    ppermute x21, waiting for transfers between devices, z_three(): lax.ppermute(block, 'z', z_pairs(step + 1))  64.7 us
    pallas_call x2, Pallas kernels, units_backward(): pl.pallas_call(functools.partial(units_backward_kernel, len(weights), row...  41.4 us
    ppermute x41, starting transfers between devices, over(): return lax.ppermute(array, axis, flip_pair)  40 us
    pallas_call x2, Pallas kernels, attend_backward(): pl.pallas_call(attend_backward_kernel, grid_spec=pltpu.PrefetchScalarGrid...  38.3 us
    convert_element_type x26, other arithmetic, add_low(): return total.astype(bf16)  31.9 us
    pallas_call x2, Pallas kernels, units_forward(): pl.pallas_call(functools.partial(units_forward_kernel, len(weights), rows...  30.7 us
    ppermute x21, starting transfers between devices, z_three(): lax.ppermute(block, 'z', z_pairs(step + 1))  26.8 us
  transfers between devices with their start and end apart: 72, of which 27 were waited for; matrix products, arithmetic and copies ran while one was open for 20% of the time, Pallas kernels for 22%

profile of v5, /device:TPU:9, one launch (start us, length us, event | category | flops | bytes accessed | tf_op | source)
XLA Modules:
  0.0 527.7 jit_solution(11533633336978803882)
XLA Ops:
  30.0 5.7 %collective-permute-done.3 = bf16[208,768]{1,0:T(8,128)(2,1)} collective-permute-done((bf16[208,768]{1,0:T(8,128)(2,1)}, bf16[208,768]{1,0:T(8,128)(2,1)}, u32[]{:S(2)}, u32[]{:S(2)}) %collective-permute-start.3) | collective-permute-done | bytes 319520 | tf_op jit(solution)/shard_map/ppermute | solution.py:490
  36.6 4.8 collective-permute-done.2
  69.8 5.1 collective-permute-done.13
  96.5 7.7 %collective-permute-done.15 = bf16[192,1536]{1,0:T(8,128)(2,1)S(1)} collective-permute-done((bf16[192,1536]{1,0:T(8,128)(2,1)S(1)}, bf16[192,1536]{1,0:T(8,128)(2,1)S(1)}, u32[]{:S(2)}, u32[]{:S(2)}) %collective-permute-start.15) | collective-permute-done | bytes 589856 | tf_op jit(solution)/shard_map/ppermute | solution.py:478
  105.8 12.0 %attend_forward.2 = (bf16[768,512]{1,0:T(8,128)(2,1)S(1)}, f32[4,8,512]{2,1,0:T(8,128)S(1)}) custom-call(s32[2]{0:T(128)S(1)} %pad_add_fusion.1.info, bf16[768,512]{1,0:T(8,128)(2,1)S(1)} %add_convert_fusion.15.queries, bf16[1536,512]{1,0:T(8,128)(2,1)S(1)} %fusion.kv_own, bf16[1536,512]{1,0:T(8,128)(2,1)S(1)} %collective-permute-done.11.kv_other), custom_call_target="tpu_custom_call" | custom-call | flops 16149000192 | bytes 51660000 | tf_op jit(solution)/shard_map/attend_forward/pallas_call | solution.py:142
  119.8 8.2 %collective-permute-done.19 = bf16[192,768]{1,0:T(8,128)(2,1)S(1)} collective-permute-done((bf16[192,768]{1,0:T(8,128)(2,1)S(1)}, bf16[192,768]{1,0:T(8,128)(2,1)S(1)}, u32[]{:S(2)}, u32[]{:S(2)}) %collective-permute-start.19) | collective-permute-done | bytes 294944 | tf_op jit(solution)/shard_map/ppermute | solution.py:490
  142.6 15.6 %units_forward.2 = (bf16[512,3072]{1,0:T(8,128)(2,1)}, bf16[512,3072]{1,0:T(8,128)(2,1)}, f32[512,768]{1,0:T(8,128)S(1)}) custom-call(bf16[512,768]{1,0:T(8,128)(2,1)S(1)} %add_convert_fusion.14.normed, f32[512,768]{1,0:T(8,128)S(1)} %get-tuple-element.581.middle.values, f32[8,1,384]{2,1,0:T(1,128)S(1)} %broadcast_in_dim_reshape.6.unit_bias, ...), custom_call_target="tpu_custom_call" | custom-call | flops 19609499648 | bytes 62730000 | tf_op jit(solution)/shard_map/units_forward/pallas_call | solution.py:244
  159.3 5.9 %collective-permute-done.23 = bf16[4,96,768]{2,1,0:T(8,128)(2,1)S(1)} collective-permute-done((bf16[4,96,768]{2,1,0:T(8,128)(2,1)S(1)}, bf16[4,96,768]{2,1,0:T(8,128)(2,1)S(1)}, u32[]{:S(2)}, u32[]{:S(2)}) %collective-permute-start.23) | collective-permute-done | bytes 589856 | tf_op jit(solution)/shard_map/ppermute | solution.py:478
  169.2 4.9 collective-permute-done.26
  185.5 13.3 %attend_forward.3 = (bf16[768,512]{1,0:T(8,128)(2,1)S(1)}, f32[4,8,512]{2,1,0:T(8,128)S(1)}) custom-call(s32[2]{0:T(128)S(1)} %pad_add_fusion.1.info, bf16[768,512]{1,0:T(8,128)(2,1)S(1)} %add_convert_fusion.12.queries, bf16[1536,512]{1,0:T(8,128)(2,1)S(1)} %fusion.1.kv_own, bf16[1536,512]{1,0:T(8,128)(2,1)} %collective-permute-done.27.kv_other), custom_call_target="tpu_custom_call" | custom-call | flops 16149000192 | bytes 51660000 | tf_op jit(solution)/shard_map/attend_forward/pallas_call | solution.py:142
  202.3 15.0 %units_forward.3 = (bf16[512,3072]{1,0:T(8,128)(2,1)S(1)}, bf16[512,3072]{1,0:T(8,128)(2,1)S(1)}, f32[512,768]{1,0:T(8,128)S(1)}) custom-call(bf16[512,768]{1,0:T(8,128)(2,1)S(1)} %copy-done.9, f32[512,768]{1,0:T(8,128)S(1)} %get-tuple-element.583.middle.values, f32[8,1,384]{2,1,0:T(1,128)S(1)} %broadcast_in_dim_reshape.7.unit_bias, ...), custom_call_target="tpu_custom_call" | custom-call | flops 19609499648 | bytes 62730000 | tf_op jit(solution)/shard_map/units_forward/pallas_call | solution.py:244
  217.4 19.6 %units_backward.2 = (bf16[1536,1536]{1,0:T(8,128)(2,1)S(1)}, bf16[1536,1536]{1,0:T(8,128)(2,1)}, f32[512,768]{1,0:T(8,128)S(1)}, f32[8,1,384]{2,1,0:T(1,128)S(1)}) custom-call(s32[8]{0:T(128)S(1)} %fusion.28.place, bf16[512,768]{1,0:T(8,128)(2,1)S(1)} %copy-done.8, bf16[512,768]{1,0:T(8,128)(2,1)S(1)} %copy-done.9, ...), custom_call_target="tpu_custom_call" | custom-call | flops 23069999104 | bytes 73800000 | tf_op jit(solution)/shard_map/units_backward/pallas_call | solution.py:331
  249.5 19.6 %attend_backward.2 = (bf16[768,512]{1,0:T(8,128)(2,1)S(1)}, f32[1536,512]{1,0:T(8,128)S(1)}, bf16[1536,512]{1,0:T(8,128)(2,1)S(1)}) custom-call(s32[2]{0:T(128)S(1)} %pad_add_fusion.1.info, bf16[768,512]{1,0:T(8,128)(2,1)S(1)} %copy-done.40, bf16[1536,512]{1,0:T(8,128)(2,1)S(1)} %copy-done.21, bf16[1536,512]{1,0:T(8,128)(2,1)} %collective-permute-done.27.kv_other, ...), custom_call_target="tpu_custom_call" | custom-call | flops 24223500288 | bytes 77490000 | tf_op jit(solution)/shard_map/attend_backward/pallas_call | solution.py:164
  293.6 6.5 %collective-permute-done.34 = bf16[2,96,1536]{2,1,0:T(8,128)(2,1)S(1)} collective-permute-done((bf16[2,96,1536]{2,1,0:T(8,128)(2,1)}, bf16[2,96,1536]{2,1,0:T(8,128)(2,1)S(1)}, u32[]{:S(2)}, u32[]{:S(2)}) %collective-permute-start.34) | collective-permute-done | bytes 589856 | tf_op jit(solution)/shard_map/ppermute | solution.py:478
  308.8 21.8 %units_backward.3 = (bf16[1536,1536]{1,0:T(8,128)(2,1)}, bf16[1536,1536]{1,0:T(8,128)(2,1)}, f32[512,768]{1,0:T(8,128)S(1)}, f32[8,1,384]{2,1,0:T(1,128)S(1)}) custom-call(s32[8]{0:T(128)S(1)} %iota.13.place, bf16[512,768]{1,0:T(8,128)(2,1)S(1)} %get-tuple-element.287.grad_down, bf16[512,768]{1,0:T(8,128)(2,1)S(1)} %copy-done.7, ...), custom_call_target="tpu_custom_call" | custom-call | flops 23069999104 | bytes 73800000 | tf_op jit(solution)/shard_map/units_backward/pallas_call | solution.py:331
  351.1 6.0 %add_convert_fusion.3 = (bf16[384,1536]{1,0:T(8,128)(2,1)S(1)}, bf16[384,1536]{1,0:T(8,128)(2,1)S(1)}, bf16[384,1536]{1,0:T(8,128)(2,1)}, bf16[384,1536]{1,0:T(8,128)(2,1)}) fusion(bf16[1536,1536]{1,0:T(8,128)(2,1)} %collective-permute-done.41, bf16[1536,1536]{1,0:T(8,128)(2,1)} %get-tuple-element.316), kind=kLoop, calls=%fused_computation.15 | loop fusion | flops 9437184 | bytes 14155776 | tf_op jit(solution)/shard_map/convert_element_type | solution.py:506
  363.6 18.6 %attend_backward.3 = (bf16[768,512]{1,0:T(8,128)(2,1)S(1)}, f32[1536,512]{1,0:T(8,128)S(1)}, bf16[1536,512]{1,0:T(8,128)(2,1)S(1)}) custom-call(s32[2]{0:T(128)S(1)} %pad_add_fusion.1.info, bf16[768,512]{1,0:T(8,128)(2,1)S(1)} %copy-done.42, bf16[1536,512]{1,0:T(8,128)(2,1)S(1)} %copy-done.17, bf16[1536,512]{1,0:T(8,128)(2,1)S(1)} %copy-done.19, ...), custom_call_target="tpu_custom_call" | custom-call | flops 24223500288 | bytes 77490000 | tf_op jit(solution)/shard_map/attend_backward/pallas_call | solution.py:164
  383.9 8.9 %collective-permute-done.44 = bf16[384,1536]{1,0:T(8,128)(2,1)S(1)} collective-permute-done((bf16[384,1536]{1,0:T(8,128)(2,1)S(1)}, bf16[384,1536]{1,0:T(8,128)(2,1)S(1)}, u32[]{:S(2)}, u32[]{:S(2)}) %collective-permute-start.44) | collective-permute-done | bytes 1179680 | tf_op jit(solution)/shard_map/ppermute | solution.py:478
  417.4 8.6 %collective-permute-done.51 = bf16[2,96,1536]{2,1,0:T(8,128)(2,1)} collective-permute-done((bf16[2,96,1536]{2,1,0:T(8,128)(2,1)}, bf16[2,96,1536]{2,1,0:T(8,128)(2,1)}, u32[]{:S(2)}, u32[]{:S(2)}) %collective-permute-start.51) | collective-permute-done | bytes 589856 | tf_op jit(solution)/shard_map/ppermute | solution.py:478
  439.9 4.8 collective-permute-done.57
  447.1 10.6 %collective-permute-done.58 = bf16[96,1536]{1,0:T(8,128)(2,1)S(1)} collective-permute-done((bf16[96,1536]{1,0:T(8,128)(2,1)S(1)}, bf16[96,1536]{1,0:T(8,128)(2,1)S(1)}, u32[]{:S(2)}, u32[]{:S(2)}) %collective-permute-start.58) | collective-permute-done | bytes 294944 | tf_op jit(solution)/shard_map/ppermute | solution.py:490
  457.7 8.3 %collective-permute-done.59 = bf16[96,1536]{1,0:T(8,128)(2,1)S(1)} collective-permute-done((bf16[96,1536]{1,0:T(8,128)(2,1)S(1)}, bf16[96,1536]{1,0:T(8,128)(2,1)S(1)}, u32[]{:S(2)}, u32[]{:S(2)}) %collective-permute-start.59) | collective-permute-done | bytes 294944 | tf_op jit(solution)/shard_map/ppermute | solution.py:490
  478.5 11.8 %collective-permute-done.62 = bf16[144,768]{1,0:T(8,128)(2,1)S(1)} collective-permute-done((bf16[144,768]{1,0:T(8,128)(2,1)}, bf16[144,768]{1,0:T(8,128)(2,1)S(1)}, u32[]{:S(2)}, u32[]{:S(2)}) %collective-permute-start.62) | collective-permute-done | bytes 221216 | tf_op jit(solution)/shard_map/ppermute | solution.py:490
  500.3 5.7 %collective-permute-done.65 = bf16[144,768]{1,0:T(8,128)(2,1)S(1)} collective-permute-done((bf16[144,768]{1,0:T(8,128)(2,1)S(1)}, bf16[144,768]{1,0:T(8,128)(2,1)S(1)}, u32[]{:S(2)}, u32[]{:S(2)}) %collective-permute-start.65) | collective-permute-done | bytes 221216 | tf_op jit(solution)/shard_map/ppermute | solution.py:498
  (626 shorter events, 260.6 us)
Async XLA Ops:
  7.2 194.0 %all-gather.5.cloned.1.call-start = ((), (), s32[]{:S(2)}) async-start(), calls=%async_computation | async-start | bytes 9732096 | tf_op jit(solution)/shard_map/all_gather | solution.py:662
  14.3 27.1 %collective-permute-start.2 = (bf16[208,768]{1,0:T(8,128)(2,1)}, bf16[208,768]{1,0:T(8,128)(2,1)}, u32[]{:S(2)}, u32[]{:S(2)}) collective-permute-start(bf16[208,768]{1,0:T(8,128)(2,1)} %pad_maximum_fusion.17), channel_id=1, source_target_pairs={{0,2},{1,3},{2,0},{3,1},{4,6},{5,7},{6,4},{7,5},{8,10},{9,11},{10,... | collective-permute-start | bytes 958472 | tf_op jit(solution)/shard_map/ppermute | solution.py:490
  15.4 27.1 %collective-permute-start.1 = (bf16[208,768]{1,0:T(8,128)(2,1)}, bf16[208,768]{1,0:T(8,128)(2,1)}, u32[]{:S(2)}, u32[]{:S(2)}) collective-permute-start(bf16[208,768]{1,0:T(8,128)(2,1)} %pad_maximum_fusion.17), channel_id=1, source_target_pairs={{0,1},{1,0},{2,3},{3,2},{4,5},{5,4},{6,7},{7,6},{8,9},{9,8},{10,11... | collective-permute-start | bytes 958472 | tf_op jit(solution)/shard_map/ppermute | solution.py:490
  17.8 58.2 %collective-permute-start.10 = (bf16[512,768]{1,0:T(8,128)(2,1)}, bf16[512,768]{1,0:T(8,128)(2,1)}, u32[]{:S(2)}, u32[]{:S(2)}) collective-permute-start(bf16[512,768]{1,0:T(8,128)(2,1)} %param.13), channel_id=1, source_target_pairs={{1,4},{3,6},{4,1},{6,3},{9,12},{11,14},{12,9},{14,11},{17,20},{19,... | collective-permute-start | bytes 2359304 | tf_op jit(solution)/shard_map/ppermute | solution.py:560
  68.5 400.5 %all-gather.7.cloned.1.call-start = ((), (), s32[]{:S(2)}) async-start(), calls=%async_computation.1 | async-start | bytes 2654208 | tf_op jit(solution)/shard_map/all_gather | solution.py:786
  85.7 32.2 %collective-permute-start.17 = (bf16[192,768]{1,0:T(8,128)(2,1)S(1)}, bf16[192,768]{1,0:T(8,128)(2,1)S(1)}, u32[]{:S(2)}, u32[]{:S(2)}) collective-permute-start(bf16[192,768]{1,0:T(8,128)(2,1)S(1)} %pad_maximum_fusion.22), channel_id=1, source_target_pairs={{0,1},{1,0},{2,3},{3,2},{4,5},{5,4},{6,7},{7,6},{8,9},{9,8},{10,11... | collective-permute-start | bytes 884744 | tf_op jit(solution)/shard_map/ppermute | solution.py:490
  88.0 31.6 %collective-permute-start.18 = (bf16[192,768]{1,0:T(8,128)(2,1)S(1)}, bf16[192,768]{1,0:T(8,128)(2,1)S(1)}, u32[]{:S(2)}, u32[]{:S(2)}) collective-permute-start(bf16[192,768]{1,0:T(8,128)(2,1)S(1)} %pad_maximum_fusion.22), channel_id=1, source_target_pairs={{0,2},{1,3},{2,0},{3,1},{4,6},{5,7},{6,4},{7,5},{8,10},{9,11},{10,... | collective-permute-start | bytes 884744 | tf_op jit(solution)/shard_map/ppermute | solution.py:490
  94.5 33.5 %collective-permute-start.19 = (bf16[192,768]{1,0:T(8,128)(2,1)S(1)}, bf16[192,768]{1,0:T(8,128)(2,1)S(1)}, u32[]{:S(2)}, u32[]{:S(2)}) collective-permute-start(bf16[192,768]{1,0:T(8,128)(2,1)S(1)} %pad_maximum_fusion.22), channel_id=1, source_target_pairs={{0,3},{1,2},{2,1},{3,0},{4,7},{5,6},{6,5},{7,4},{8,11},{9,10},{10,... | collective-permute-start | bytes 884744 | tf_op jit(solution)/shard_map/ppermute | solution.py:490
  104.2 26.3 %collective-permute-start.12 = (bf16[384,1536]{1,0:T(8,128)(2,1)S(1)}, bf16[384,1536]{1,0:T(8,128)(2,1)S(1)}, u32[]{:S(2)}, u32[]{:S(2)}) collective-permute-start(bf16[384,1536]{1,0:T(8,128)(2,1)S(1)} %constant_dynamic-update-slice_fusion.refs_4_), channel_id=1, source_target_pairs={{0,16},{16,0},{1,17},{17,1},{2,18},{18,2},{3,19},{19,3},{4,20},{20... | collective-permute-start | bytes 3538952 | tf_op jit(solution)/shard_map/ppermute | solution.py:478
  138.8 26.5 %collective-permute-start.23 = (bf16[4,96,768]{2,1,0:T(8,128)(2,1)S(1)}, bf16[4,96,768]{2,1,0:T(8,128)(2,1)S(1)}, u32[]{:S(2)}, u32[]{:S(2)}) collective-permute-start(bf16[4,96,768]{2,1,0:T(8,128)(2,1)S(1)} %pad_maximum_fusion.14), channel_id=1, source_target_pairs={{0,8},{8,0},{1,9},{9,1},{2,10},{10,2},{3,11},{11,3},{4,12},{12,4},... | collective-permute-start | bytes 1769480 | tf_op jit(solution)/shard_map/ppermute | solution.py:478
  247.6 27.4 %collective-permute-start.29 = (bf16[384,1536]{1,0:T(8,128)(2,1)S(1)}, bf16[384,1536]{1,0:T(8,128)(2,1)S(1)}, u32[]{:S(2)}, u32[]{:S(2)}) collective-permute-start(bf16[384,1536]{1,0:T(8,128)(2,1)S(1)} %add_convert_fusion.8), channel_id=1, source_target_pairs={{0,16},{16,0},{1,17},{17,1},{2,18},{18,2},{3,19},{19,3},{4,20},{20... | collective-permute-start | bytes 3538952 | tf_op jit(solution)/shard_map/ppermute | solution.py:478
  248.8 27.3 %collective-permute-start.30 = (bf16[384,1536]{1,0:T(8,128)(2,1)}, bf16[384,1536]{1,0:T(8,128)(2,1)S(1)}, u32[]{:S(2)}, u32[]{:S(2)}) collective-permute-start(bf16[384,1536]{1,0:T(8,128)(2,1)} %add_convert_fusion.7), channel_id=1, source_target_pairs={{0,8},{8,0},{1,9},{9,1},{2,10},{10,2},{3,11},{11,3},{4,12},{12,4},... | collective-permute-start | bytes 3538952 | tf_op jit(solution)/shard_map/ppermute | solution.py:478
  304.6 28.3 %collective-permute-start.36 = (bf16[4,2,48,768]{3,2,1,0:T(8,128)(2,1)S(1)}, bf16[4,2,48,768]{3,2,1,0:T(8,128)(2,1)S(1)}, u32[]{:S(2)}, u32[]{:S(2)}) collective-permute-start(bf16[4,2,48,768]{3,2,1,0:T(8,128)(2,1)S(1)} %get-tuple-element.294), channel_id=1, source_target_pairs={{0,16},{16,0},{1,17},{17,1},{2,18},{18,2},{3,19},{19,3},{4,20},{20... | collective-permute-start | bytes 1769480 | tf_op jit(solution)/shard_map/ppermute | solution.py:478
  304.9 27.9 %collective-permute-start.37 = (bf16[4,2,48,768]{3,2,1,0:T(8,128)(2,1)S(1)}, bf16[4,2,48,768]{3,2,1,0:T(8,128)(2,1)S(1)}, u32[]{:S(2)}, u32[]{:S(2)}) collective-permute-start(bf16[4,2,48,768]{3,2,1,0:T(8,128)(2,1)S(1)} %get-tuple-element.295), channel_id=1, source_target_pairs={{0,8},{8,0},{1,9},{9,1},{2,10},{10,2},{3,11},{11,3},{4,12},{12,4},... | collective-permute-start | bytes 1769480 | tf_op jit(solution)/shard_map/ppermute | solution.py:478
  349.2 119.7 %all-gather.9.cloned.1.call-start = ((), (), s32[]{:S(2)}) async-start(), calls=%async_computation.2 | async-start | bytes 1327104 | tf_op jit(solution)/shard_map/all_gather | solution.py:786
  359.5 33.3 %collective-permute-start.44 = (bf16[384,1536]{1,0:T(8,128)(2,1)S(1)}, bf16[384,1536]{1,0:T(8,128)(2,1)S(1)}, u32[]{:S(2)}, u32[]{:S(2)}) collective-permute-start(bf16[384,1536]{1,0:T(8,128)(2,1)S(1)} %get-tuple-element.327), channel_id=1, source_target_pairs={{0,16},{16,0},{1,17},{17,1},{2,18},{18,2},{3,19},{19,3},{4,20},{20... | collective-permute-start | bytes 3538952 | tf_op jit(solution)/shard_map/ppermute | solution.py:478
  359.8 34.4 %collective-permute-start.45 = (bf16[384,1536]{1,0:T(8,128)(2,1)S(1)}, bf16[384,1536]{1,0:T(8,128)(2,1)S(1)}, u32[]{:S(2)}, u32[]{:S(2)}) collective-permute-start(bf16[384,1536]{1,0:T(8,128)(2,1)S(1)} %get-tuple-element.328), channel_id=1, source_target_pairs={{0,8},{8,0},{1,9},{9,1},{2,10},{10,2},{3,11},{11,3},{4,12},{12,4},... | collective-permute-start | bytes 3538952 | tf_op jit(solution)/shard_map/ppermute | solution.py:478
  360.9 34.4 %collective-permute-start.46 = (bf16[96,768]{1,0:T(8,128)(2,1)S(1)}, bf16[96,768]{1,0:T(8,128)(2,1)S(1)}, u32[]{:S(2)}, u32[]{:S(2)}) collective-permute-start(bf16[96,768]{1,0:T(8,128)(2,1)S(1)} %get-tuple-element.336), channel_id=1, source_target_pairs={{0,1},{1,0},{2,3},{3,2},{4,5},{5,4},{6,7},{7,6},{8,9},{9,8},{10,11... | collective-permute-start | bytes 442376 | tf_op jit(solution)/shard_map/ppermute | solution.py:490
  360.9 34.4 %collective-permute-start.47 = (bf16[96,768]{1,0:T(8,128)(2,1)S(1)}, bf16[96,768]{1,0:T(8,128)(2,1)S(1)}, u32[]{:S(2)}, u32[]{:S(2)}) collective-permute-start(bf16[96,768]{1,0:T(8,128)(2,1)S(1)} %get-tuple-element.337), channel_id=1, source_target_pairs={{0,2},{1,3},{2,0},{3,1},{4,6},{5,7},{6,4},{7,5},{8,10},{9,11},{10,... | collective-permute-start | bytes 442376 | tf_op jit(solution)/shard_map/ppermute | solution.py:490
  362.6 32.7 %collective-permute-start.48 = (bf16[96,768]{1,0:T(8,128)(2,1)S(1)}, bf16[96,768]{1,0:T(8,128)(2,1)S(1)}, u32[]{:S(2)}, u32[]{:S(2)}) collective-permute-start(bf16[96,768]{1,0:T(8,128)(2,1)S(1)} %get-tuple-element.338), channel_id=1, source_target_pairs={{0,3},{1,2},{2,1},{3,0},{4,7},{5,6},{6,5},{7,4},{8,11},{9,10},{10,... | collective-permute-start | bytes 442376 | tf_op jit(solution)/shard_map/ppermute | solution.py:490
  412.0 94.4 %all-gather.11.cloned.1.call-start = ((), (), s32[]{:S(2)}) async-start(), calls=%async_computation.3 | async-start | bytes 2654208 | tf_op jit(solution)/shard_map/all_gather | solution.py:786
  435.8 30.2 %collective-permute-start.54 = (bf16[4,2,48,768]{3,2,0,1:T(8,128)(2,1)S(1)}, bf16[4,2,48,768]{3,2,0,1:T(8,128)(2,1)S(1)}, u32[]{:S(2)}, u32[]{:S(2)}) collective-permute-start(bf16[4,2,48,768]{3,2,0,1:T(8,128)(2,1)S(1)} %get-tuple-element.365), channel_id=1, source_target_pairs={{0,8},{8,0},{1,9},{9,1},{2,10},{10,2},{3,11},{11,3},{4,12},{12,4},... | collective-permute-start | bytes 1769480 | tf_op jit(solution)/shard_map/ppermute | solution.py:478
  436.0 30.1 %collective-permute-start.55 = (bf16[4,2,48,768]{3,2,0,1:T(8,128)(2,1)S(1)}, bf16[4,2,48,768]{3,2,0,1:T(8,128)(2,1)S(1)}, u32[]{:S(2)}, u32[]{:S(2)}) collective-permute-start(bf16[4,2,48,768]{3,2,0,1:T(8,128)(2,1)S(1)} %get-tuple-element.366), channel_id=1, source_target_pairs={{0,16},{16,0},{1,17},{17,1},{2,18},{18,2},{3,19},{19,3},{4,20},{20... | collective-permute-start | bytes 1769480 | tf_op jit(solution)/shard_map/ppermute | solution.py:478
  437.0 29.0 %collective-permute-start.56 = (bf16[4,2,48,768]{3,2,0,1:T(8,128)(2,1)S(1)}, bf16[4,2,48,768]{3,2,0,1:T(8,128)(2,1)S(1)}, u32[]{:S(2)}, u32[]{:S(2)}) collective-permute-start(bf16[4,2,48,768]{3,2,0,1:T(8,128)(2,1)S(1)} %get-tuple-element.367), channel_id=1, source_target_pairs={{0,24},{8,16},{16,8},{24,0},{1,25},{9,17},{17,9},{25,1},{2,26},{10... | collective-permute-start | bytes 1769480 | tf_op jit(solution)/shard_map/ppermute | solution.py:498
  (159 other events, 1703.9 us)
Sparse Core Ops, SparseCore 0:
  68.6 107.1 all-gather.4
  349.4 35.0 all-gather.6
  412.1 24.5 all-gather.8
  469.1 30.5 all-gather.10

commit v6 on v5

--- a/solution.py
+++ b/solution.py
@@ -710,7 +710,7 @@
         activated, slopes, stream = units_forward(
             normed_two,
             middle,
-            order(up_bias_all[:, layer_idx]),
+            order(up_bias_all[:, layer_idx]).reshape(8 if layer_idx == 0 else 4, -1),
             down_bias[layer_idx].astype(f32)[None, :],
             unit_weights[layer_idx],
         )

time: 533 us -> 530 us (level)
  no operation moved by 1% of the time
where the time goes in v6:
time: 530 us; the launch traced here: 525 us
  Pallas kernels  146 us (28%)
  waiting for transfers between devices  137 us (26%)
  other arithmetic  77.2 us (15%)
  starting transfers between devices  74.1 us (14%)
  local copies, waits for them, and re-layouts  47.4 us (9%)
  matrix products  25.4 us (5%)
  between operations  17.9 us (3%)
    ppermute x41, waiting for transfers between devices, over(): return lax.ppermute(array, axis, flip_pair)  66.5 us
    ppermute x21, waiting for transfers between devices, z_three(): lax.ppermute(block, 'z', z_pairs(step + 1))  64.8 us
    pallas_call x2, Pallas kernels, units_backward(): pl.pallas_call(functools.partial(units_backward_kernel, len(weights), row...  41.2 us
    ppermute x41, starting transfers between devices, over(): return lax.ppermute(array, axis, flip_pair)  40 us
    pallas_call x2, Pallas kernels, attend_backward(): pl.pallas_call(attend_backward_kernel, grid_spec=pltpu.PrefetchScalarGrid...  38.5 us
    convert_element_type x26, other arithmetic, add_low(): return total.astype(bf16)  32 us
    pallas_call x2, Pallas kernels, units_forward(): pl.pallas_call(functools.partial(units_forward_kernel, len(weights), rows...  27.8 us
    ppermute x21, starting transfers between devices, z_three(): lax.ppermute(block, 'z', z_pairs(step + 1))  26.7 us
  transfers between devices with their start and end apart: 72, of which 27 were waited for; matrix products, arithmetic and copies ran while one was open for 20% of the time, Pallas kernels for 22%

profile of v6, /device:TPU:9, one launch (start us, length us, event | category | flops | bytes accessed | tf_op | source)
XLA Modules:
  0.0 524.8 jit_solution(3078073124946932205)
XLA Ops:
  30.0 5.7 %collective-permute-done.3 = bf16[208,768]{1,0:T(8,128)(2,1)} collective-permute-done((bf16[208,768]{1,0:T(8,128)(2,1)}, bf16[208,768]{1,0:T(8,128)(2,1)}, u32[]{:S(2)}, u32[]{:S(2)}) %collective-permute-start.3) | collective-permute-done | bytes 319520 | tf_op jit(solution)/shard_map/ppermute | solution.py:490
  36.6 4.8 collective-permute-done.2
  69.8 5.1 collective-permute-done.13
  96.5 7.7 %collective-permute-done.15 = bf16[192,1536]{1,0:T(8,128)(2,1)S(1)} collective-permute-done((bf16[192,1536]{1,0:T(8,128)(2,1)S(1)}, bf16[192,1536]{1,0:T(8,128)(2,1)S(1)}, u32[]{:S(2)}, u32[]{:S(2)}) %collective-permute-start.15) | collective-permute-done | bytes 589856 | tf_op jit(solution)/shard_map/ppermute | solution.py:478
  105.8 12.0 %attend_forward.2 = (bf16[768,512]{1,0:T(8,128)(2,1)S(1)}, f32[4,8,512]{2,1,0:T(8,128)S(1)}) custom-call(s32[2]{0:T(128)S(1)} %pad_add_fusion.1.info, bf16[768,512]{1,0:T(8,128)(2,1)S(1)} %add_convert_fusion.15.queries, bf16[1536,512]{1,0:T(8,128)(2,1)S(1)} %fusion.kv_own, bf16[1536,512]{1,0:T(8,128)(2,1)S(1)} %collective-permute-done.11.kv_other), custom_call_target="tpu_custom_call" | custom-call | flops 16149000192 | bytes 51660000 | tf_op jit(solution)/shard_map/attend_forward/pallas_call | solution.py:142
  119.8 8.2 %collective-permute-done.19 = bf16[192,768]{1,0:T(8,128)(2,1)S(1)} collective-permute-done((bf16[192,768]{1,0:T(8,128)(2,1)S(1)}, bf16[192,768]{1,0:T(8,128)(2,1)S(1)}, u32[]{:S(2)}, u32[]{:S(2)}) %collective-permute-start.19) | collective-permute-done | bytes 294944 | tf_op jit(solution)/shard_map/ppermute | solution.py:490
  142.5 15.6 %units_forward.2 = (bf16[512,3072]{1,0:T(8,128)(2,1)}, bf16[512,3072]{1,0:T(8,128)(2,1)}, f32[512,768]{1,0:T(8,128)S(1)}) custom-call(bf16[512,768]{1,0:T(8,128)(2,1)S(1)} %add_convert_fusion.14.normed, f32[512,768]{1,0:T(8,128)S(1)} %get-tuple-element.581.middle.values, f32[8,1,384]{2,1,0:T(1,128)S(1)} %broadcast_in_dim_reshape.3.unit_bias, ...), custom_call_target="tpu_custom_call" | custom-call | flops 19609499648 | bytes 62730000 | tf_op jit(solution)/shard_map/units_forward/pallas_call | solution.py:244
  159.2 6.0 %collective-permute-done.23 = bf16[4,96,768]{2,1,0:T(8,128)(2,1)S(1)} collective-permute-done((bf16[4,96,768]{2,1,0:T(8,128)(2,1)S(1)}, bf16[4,96,768]{2,1,0:T(8,128)(2,1)S(1)}, u32[]{:S(2)}, u32[]{:S(2)}) %collective-permute-start.23) | collective-permute-done | bytes 589856 | tf_op jit(solution)/shard_map/ppermute | solution.py:478
  169.2 4.9 collective-permute-done.26
  185.5 13.3 %attend_forward.3 = (bf16[768,512]{1,0:T(8,128)(2,1)S(1)}, f32[4,8,512]{2,1,0:T(8,128)S(1)}) custom-call(s32[2]{0:T(128)S(1)} %pad_add_fusion.1.info, bf16[768,512]{1,0:T(8,128)(2,1)S(1)} %add_convert_fusion.12.queries, bf16[1536,512]{1,0:T(8,128)(2,1)S(1)} %fusion.1.kv_own, bf16[1536,512]{1,0:T(8,128)(2,1)} %collective-permute-done.27.kv_other), custom_call_target="tpu_custom_call" | custom-call | flops 16149000192 | bytes 51660000 | tf_op jit(solution)/shard_map/attend_forward/pallas_call | solution.py:142
  202.3 12.2 %units_forward.3 = (bf16[512,3072]{1,0:T(8,128)(2,1)S(1)}, bf16[512,3072]{1,0:T(8,128)(2,1)S(1)}, f32[512,768]{1,0:T(8,128)S(1)}) custom-call(bf16[512,768]{1,0:T(8,128)(2,1)S(1)} %copy-done.9, f32[512,768]{1,0:T(8,128)S(1)} %get-tuple-element.583.middle.values, f32[4,1,768]{2,1,0:T(1,128)S(1)} %broadcast_in_dim_reshape_reshape.3.unit_bias, ...), custom_call_target="tpu_custom_call" | custom-call | flops 19609499648 | bytes 62730000 | tf_op jit(solution)/shard_map/units_forward/pallas_call | solution.py:244
  214.6 19.4 %units_backward.2 = (bf16[1536,1536]{1,0:T(8,128)(2,1)S(1)}, bf16[1536,1536]{1,0:T(8,128)(2,1)}, f32[512,768]{1,0:T(8,128)S(1)}, f32[8,1,384]{2,1,0:T(1,128)S(1)}) custom-call(s32[8]{0:T(128)S(1)} %fusion.28.place, bf16[512,768]{1,0:T(8,128)(2,1)S(1)} %copy-done.8, bf16[512,768]{1,0:T(8,128)(2,1)S(1)} %copy-done.9, ...), custom_call_target="tpu_custom_call" | custom-call | flops 23069999104 | bytes 73800000 | tf_op jit(solution)/shard_map/units_backward/pallas_call | solution.py:331
  246.5 19.8 %attend_backward.2 = (bf16[768,512]{1,0:T(8,128)(2,1)S(1)}, f32[1536,512]{1,0:T(8,128)S(1)}, bf16[1536,512]{1,0:T(8,128)(2,1)S(1)}) custom-call(s32[2]{0:T(128)S(1)} %pad_add_fusion.1.info, bf16[768,512]{1,0:T(8,128)(2,1)S(1)} %copy-done.40, bf16[1536,512]{1,0:T(8,128)(2,1)S(1)} %copy-done.21, bf16[1536,512]{1,0:T(8,128)(2,1)} %collective-permute-done.27.kv_other, ...), custom_call_target="tpu_custom_call" | custom-call | flops 24223500288 | bytes 77490000 | tf_op jit(solution)/shard_map/attend_backward/pallas_call | solution.py:164
  290.6 6.5 %collective-permute-done.34 = bf16[2,96,1536]{2,1,0:T(8,128)(2,1)S(1)} collective-permute-done((bf16[2,96,1536]{2,1,0:T(8,128)(2,1)}, bf16[2,96,1536]{2,1,0:T(8,128)(2,1)S(1)}, u32[]{:S(2)}, u32[]{:S(2)}) %collective-permute-start.34) | collective-permute-done | bytes 589856 | tf_op jit(solution)/shard_map/ppermute | solution.py:478
  305.8 21.8 %units_backward.3 = (bf16[1536,1536]{1,0:T(8,128)(2,1)}, bf16[1536,1536]{1,0:T(8,128)(2,1)}, f32[512,768]{1,0:T(8,128)S(1)}, f32[8,1,384]{2,1,0:T(1,128)S(1)}) custom-call(s32[8]{0:T(128)S(1)} %iota.13.place, bf16[512,768]{1,0:T(8,128)(2,1)S(1)} %get-tuple-element.287.grad_down, bf16[512,768]{1,0:T(8,128)(2,1)S(1)} %copy-done.7, ...), custom_call_target="tpu_custom_call" | custom-call | flops 23069999104 | bytes 73800000 | tf_op jit(solution)/shard_map/units_backward/pallas_call | solution.py:331
  348.1 6.1 %add_convert_fusion.3 = (bf16[384,1536]{1,0:T(8,128)(2,1)S(1)}, bf16[384,1536]{1,0:T(8,128)(2,1)S(1)}, bf16[384,1536]{1,0:T(8,128)(2,1)}, bf16[384,1536]{1,0:T(8,128)(2,1)}) fusion(bf16[1536,1536]{1,0:T(8,128)(2,1)} %collective-permute-done.41, bf16[1536,1536]{1,0:T(8,128)(2,1)} %get-tuple-element.316), kind=kLoop, calls=%fused_computation.15 | loop fusion | flops 9437184 | bytes 14155776 | tf_op jit(solution)/shard_map/convert_element_type | solution.py:506
  360.6 18.6 %attend_backward.3 = (bf16[768,512]{1,0:T(8,128)(2,1)S(1)}, f32[1536,512]{1,0:T(8,128)S(1)}, bf16[1536,512]{1,0:T(8,128)(2,1)S(1)}) custom-call(s32[2]{0:T(128)S(1)} %pad_add_fusion.1.info, bf16[768,512]{1,0:T(8,128)(2,1)S(1)} %copy-done.42, bf16[1536,512]{1,0:T(8,128)(2,1)S(1)} %copy-done.17, bf16[1536,512]{1,0:T(8,128)(2,1)S(1)} %copy-done.19, ...), custom_call_target="tpu_custom_call" | custom-call | flops 24223500288 | bytes 77490000 | tf_op jit(solution)/shard_map/attend_backward/pallas_call | solution.py:164
  381.0 8.9 %collective-permute-done.44 = bf16[384,1536]{1,0:T(8,128)(2,1)S(1)} collective-permute-done((bf16[384,1536]{1,0:T(8,128)(2,1)S(1)}, bf16[384,1536]{1,0:T(8,128)(2,1)S(1)}, u32[]{:S(2)}, u32[]{:S(2)}) %collective-permute-start.44) | collective-permute-done | bytes 1179680 | tf_op jit(solution)/shard_map/ppermute | solution.py:478
  414.5 8.6 %collective-permute-done.51 = bf16[2,96,1536]{2,1,0:T(8,128)(2,1)} collective-permute-done((bf16[2,96,1536]{2,1,0:T(8,128)(2,1)}, bf16[2,96,1536]{2,1,0:T(8,128)(2,1)}, u32[]{:S(2)}, u32[]{:S(2)}) %collective-permute-start.51) | collective-permute-done | bytes 589856 | tf_op jit(solution)/shard_map/ppermute | solution.py:478
  437.0 4.8 collective-permute-done.57
  444.1 10.7 %collective-permute-done.58 = bf16[96,1536]{1,0:T(8,128)(2,1)S(1)} collective-permute-done((bf16[96,1536]{1,0:T(8,128)(2,1)S(1)}, bf16[96,1536]{1,0:T(8,128)(2,1)S(1)}, u32[]{:S(2)}, u32[]{:S(2)}) %collective-permute-start.58) | collective-permute-done | bytes 294944 | tf_op jit(solution)/shard_map/ppermute | solution.py:490
  454.8 8.3 %collective-permute-done.59 = bf16[96,1536]{1,0:T(8,128)(2,1)S(1)} collective-permute-done((bf16[96,1536]{1,0:T(8,128)(2,1)S(1)}, bf16[96,1536]{1,0:T(8,128)(2,1)S(1)}, u32[]{:S(2)}, u32[]{:S(2)}) %collective-permute-start.59) | collective-permute-done | bytes 294944 | tf_op jit(solution)/shard_map/ppermute | solution.py:490
  475.6 11.8 %collective-permute-done.62 = bf16[144,768]{1,0:T(8,128)(2,1)S(1)} collective-permute-done((bf16[144,768]{1,0:T(8,128)(2,1)}, bf16[144,768]{1,0:T(8,128)(2,1)S(1)}, u32[]{:S(2)}, u32[]{:S(2)}) %collective-permute-start.62) | collective-permute-done | bytes 221216 | tf_op jit(solution)/shard_map/ppermute | solution.py:490
  497.4 5.7 %collective-permute-done.65 = bf16[144,768]{1,0:T(8,128)(2,1)S(1)} collective-permute-done((bf16[144,768]{1,0:T(8,128)(2,1)S(1)}, bf16[144,768]{1,0:T(8,128)(2,1)S(1)}, u32[]{:S(2)}, u32[]{:S(2)}) %collective-permute-start.65) | collective-permute-done | bytes 221216 | tf_op jit(solution)/shard_map/ppermute | solution.py:498
  (626 shorter events, 260.2 us)
Async XLA Ops:
  7.2 194.0 %all-gather.5.cloned.1.call-start = ((), (), s32[]{:S(2)}) async-start(), calls=%async_computation | async-start | bytes 9732096 | tf_op jit(solution)/shard_map/all_gather | solution.py:662
  14.3 27.1 %collective-permute-start.2 = (bf16[208,768]{1,0:T(8,128)(2,1)}, bf16[208,768]{1,0:T(8,128)(2,1)}, u32[]{:S(2)}, u32[]{:S(2)}) collective-permute-start(bf16[208,768]{1,0:T(8,128)(2,1)} %pad_maximum_fusion.17), channel_id=1, source_target_pairs={{0,2},{1,3},{2,0},{3,1},{4,6},{5,7},{6,4},{7,5},{8,10},{9,11},{10,... | collective-permute-start | bytes 958472 | tf_op jit(solution)/shard_map/ppermute | solution.py:490
  15.4 27.1 %collective-permute-start.1 = (bf16[208,768]{1,0:T(8,128)(2,1)}, bf16[208,768]{1,0:T(8,128)(2,1)}, u32[]{:S(2)}, u32[]{:S(2)}) collective-permute-start(bf16[208,768]{1,0:T(8,128)(2,1)} %pad_maximum_fusion.17), channel_id=1, source_target_pairs={{0,1},{1,0},{2,3},{3,2},{4,5},{5,4},{6,7},{7,6},{8,9},{9,8},{10,11... | collective-permute-start | bytes 958472 | tf_op jit(solution)/shard_map/ppermute | solution.py:490
  17.8 58.2 %collective-permute-start.10 = (bf16[512,768]{1,0:T(8,128)(2,1)}, bf16[512,768]{1,0:T(8,128)(2,1)}, u32[]{:S(2)}, u32[]{:S(2)}) collective-permute-start(bf16[512,768]{1,0:T(8,128)(2,1)} %param.13), channel_id=1, source_target_pairs={{1,4},{3,6},{4,1},{6,3},{9,12},{11,14},{12,9},{14,11},{17,20},{19,... | collective-permute-start | bytes 2359304 | tf_op jit(solution)/shard_map/ppermute | solution.py:560
  68.5 397.6 %all-gather.7.cloned.1.call-start = ((), (), s32[]{:S(2)}) async-start(), calls=%async_computation.1 | async-start | bytes 2654208 | tf_op jit(solution)/shard_map/all_gather | solution.py:786
  85.7 32.2 %collective-permute-start.17 = (bf16[192,768]{1,0:T(8,128)(2,1)S(1)}, bf16[192,768]{1,0:T(8,128)(2,1)S(1)}, u32[]{:S(2)}, u32[]{:S(2)}) collective-permute-start(bf16[192,768]{1,0:T(8,128)(2,1)S(1)} %pad_maximum_fusion.22), channel_id=1, source_target_pairs={{0,1},{1,0},{2,3},{3,2},{4,5},{5,4},{6,7},{7,6},{8,9},{9,8},{10,11... | collective-permute-start | bytes 884744 | tf_op jit(solution)/shard_map/ppermute | solution.py:490
  88.0 31.6 %collective-permute-start.18 = (bf16[192,768]{1,0:T(8,128)(2,1)S(1)}, bf16[192,768]{1,0:T(8,128)(2,1)S(1)}, u32[]{:S(2)}, u32[]{:S(2)}) collective-permute-start(bf16[192,768]{1,0:T(8,128)(2,1)S(1)} %pad_maximum_fusion.22), channel_id=1, source_target_pairs={{0,2},{1,3},{2,0},{3,1},{4,6},{5,7},{6,4},{7,5},{8,10},{9,11},{10,... | collective-permute-start | bytes 884744 | tf_op jit(solution)/shard_map/ppermute | solution.py:490
  94.5 33.5 %collective-permute-start.19 = (bf16[192,768]{1,0:T(8,128)(2,1)S(1)}, bf16[192,768]{1,0:T(8,128)(2,1)S(1)}, u32[]{:S(2)}, u32[]{:S(2)}) collective-permute-start(bf16[192,768]{1,0:T(8,128)(2,1)S(1)} %pad_maximum_fusion.22), channel_id=1, source_target_pairs={{0,3},{1,2},{2,1},{3,0},{4,7},{5,6},{6,5},{7,4},{8,11},{9,10},{10,... | collective-permute-start | bytes 884744 | tf_op jit(solution)/shard_map/ppermute | solution.py:490
  104.2 26.3 %collective-permute-start.12 = (bf16[384,1536]{1,0:T(8,128)(2,1)S(1)}, bf16[384,1536]{1,0:T(8,128)(2,1)S(1)}, u32[]{:S(2)}, u32[]{:S(2)}) collective-permute-start(bf16[384,1536]{1,0:T(8,128)(2,1)S(1)} %constant_dynamic-update-slice_fusion.refs_4_), channel_id=1, source_target_pairs={{0,16},{16,0},{1,17},{17,1},{2,18},{18,2},{3,19},{19,3},{4,20},{20... | collective-permute-start | bytes 3538952 | tf_op jit(solution)/shard_map/ppermute | solution.py:478
  138.8 26.5 %collective-permute-start.23 = (bf16[4,96,768]{2,1,0:T(8,128)(2,1)S(1)}, bf16[4,96,768]{2,1,0:T(8,128)(2,1)S(1)}, u32[]{:S(2)}, u32[]{:S(2)}) collective-permute-start(bf16[4,96,768]{2,1,0:T(8,128)(2,1)S(1)} %pad_maximum_fusion.14), channel_id=1, source_target_pairs={{0,8},{8,0},{1,9},{9,1},{2,10},{10,2},{3,11},{11,3},{4,12},{12,4},... | collective-permute-start | bytes 1769480 | tf_op jit(solution)/shard_map/ppermute | solution.py:478
  244.6 27.4 %collective-permute-start.29 = (bf16[384,1536]{1,0:T(8,128)(2,1)S(1)}, bf16[384,1536]{1,0:T(8,128)(2,1)S(1)}, u32[]{:S(2)}, u32[]{:S(2)}) collective-permute-start(bf16[384,1536]{1,0:T(8,128)(2,1)S(1)} %add_convert_fusion.8), channel_id=1, source_target_pairs={{0,16},{16,0},{1,17},{17,1},{2,18},{18,2},{3,19},{19,3},{4,20},{20... | collective-permute-start | bytes 3538952 | tf_op jit(solution)/shard_map/ppermute | solution.py:478
  245.8 27.3 %collective-permute-start.30 = (bf16[384,1536]{1,0:T(8,128)(2,1)}, bf16[384,1536]{1,0:T(8,128)(2,1)S(1)}, u32[]{:S(2)}, u32[]{:S(2)}) collective-permute-start(bf16[384,1536]{1,0:T(8,128)(2,1)} %add_convert_fusion.7), channel_id=1, source_target_pairs={{0,8},{8,0},{1,9},{9,1},{2,10},{10,2},{3,11},{11,3},{4,12},{12,4},... | collective-permute-start | bytes 3538952 | tf_op jit(solution)/shard_map/ppermute | solution.py:478
  301.6 28.3 %collective-permute-start.36 = (bf16[4,2,48,768]{3,2,1,0:T(8,128)(2,1)S(1)}, bf16[4,2,48,768]{3,2,1,0:T(8,128)(2,1)S(1)}, u32[]{:S(2)}, u32[]{:S(2)}) collective-permute-start(bf16[4,2,48,768]{3,2,1,0:T(8,128)(2,1)S(1)} %get-tuple-element.294), channel_id=1, source_target_pairs={{0,16},{16,0},{1,17},{17,1},{2,18},{18,2},{3,19},{19,3},{4,20},{20... | collective-permute-start | bytes 1769480 | tf_op jit(solution)/shard_map/ppermute | solution.py:478
  301.9 27.9 %collective-permute-start.37 = (bf16[4,2,48,768]{3,2,1,0:T(8,128)(2,1)S(1)}, bf16[4,2,48,768]{3,2,1,0:T(8,128)(2,1)S(1)}, u32[]{:S(2)}, u32[]{:S(2)}) collective-permute-start(bf16[4,2,48,768]{3,2,1,0:T(8,128)(2,1)S(1)} %get-tuple-element.295), channel_id=1, source_target_pairs={{0,8},{8,0},{1,9},{9,1},{2,10},{10,2},{3,11},{11,3},{4,12},{12,4},... | collective-permute-start | bytes 1769480 | tf_op jit(solution)/shard_map/ppermute | solution.py:478
  346.2 119.8 %all-gather.9.cloned.1.call-start = ((), (), s32[]{:S(2)}) async-start(), calls=%async_computation.2 | async-start | bytes 1327104 | tf_op jit(solution)/shard_map/all_gather | solution.py:786
  356.6 33.3 %collective-permute-start.44 = (bf16[384,1536]{1,0:T(8,128)(2,1)S(1)}, bf16[384,1536]{1,0:T(8,128)(2,1)S(1)}, u32[]{:S(2)}, u32[]{:S(2)}) collective-permute-start(bf16[384,1536]{1,0:T(8,128)(2,1)S(1)} %get-tuple-element.327), channel_id=1, source_target_pairs={{0,16},{16,0},{1,17},{17,1},{2,18},{18,2},{3,19},{19,3},{4,20},{20... | collective-permute-start | bytes 3538952 | tf_op jit(solution)/shard_map/ppermute | solution.py:478
  356.9 34.4 %collective-permute-start.45 = (bf16[384,1536]{1,0:T(8,128)(2,1)S(1)}, bf16[384,1536]{1,0:T(8,128)(2,1)S(1)}, u32[]{:S(2)}, u32[]{:S(2)}) collective-permute-start(bf16[384,1536]{1,0:T(8,128)(2,1)S(1)} %get-tuple-element.328), channel_id=1, source_target_pairs={{0,8},{8,0},{1,9},{9,1},{2,10},{10,2},{3,11},{11,3},{4,12},{12,4},... | collective-permute-start | bytes 3538952 | tf_op jit(solution)/shard_map/ppermute | solution.py:478
  358.0 34.4 %collective-permute-start.46 = (bf16[96,768]{1,0:T(8,128)(2,1)S(1)}, bf16[96,768]{1,0:T(8,128)(2,1)S(1)}, u32[]{:S(2)}, u32[]{:S(2)}) collective-permute-start(bf16[96,768]{1,0:T(8,128)(2,1)S(1)} %get-tuple-element.336), channel_id=1, source_target_pairs={{0,1},{1,0},{2,3},{3,2},{4,5},{5,4},{6,7},{7,6},{8,9},{9,8},{10,11... | collective-permute-start | bytes 442376 | tf_op jit(solution)/shard_map/ppermute | solution.py:490
  358.0 34.4 %collective-permute-start.47 = (bf16[96,768]{1,0:T(8,128)(2,1)S(1)}, bf16[96,768]{1,0:T(8,128)(2,1)S(1)}, u32[]{:S(2)}, u32[]{:S(2)}) collective-permute-start(bf16[96,768]{1,0:T(8,128)(2,1)S(1)} %get-tuple-element.337), channel_id=1, source_target_pairs={{0,2},{1,3},{2,0},{3,1},{4,6},{5,7},{6,4},{7,5},{8,10},{9,11},{10,... | collective-permute-start | bytes 442376 | tf_op jit(solution)/shard_map/ppermute | solution.py:490
  359.6 32.8 %collective-permute-start.48 = (bf16[96,768]{1,0:T(8,128)(2,1)S(1)}, bf16[96,768]{1,0:T(8,128)(2,1)S(1)}, u32[]{:S(2)}, u32[]{:S(2)}) collective-permute-start(bf16[96,768]{1,0:T(8,128)(2,1)S(1)} %get-tuple-element.338), channel_id=1, source_target_pairs={{0,3},{1,2},{2,1},{3,0},{4,7},{5,6},{6,5},{7,4},{8,11},{9,10},{10,... | collective-permute-start | bytes 442376 | tf_op jit(solution)/shard_map/ppermute | solution.py:490
  409.1 94.4 %all-gather.11.cloned.1.call-start = ((), (), s32[]{:S(2)}) async-start(), calls=%async_computation.3 | async-start | bytes 2654208 | tf_op jit(solution)/shard_map/all_gather | solution.py:786
  432.9 30.2 %collective-permute-start.54 = (bf16[4,2,48,768]{3,2,0,1:T(8,128)(2,1)S(1)}, bf16[4,2,48,768]{3,2,0,1:T(8,128)(2,1)S(1)}, u32[]{:S(2)}, u32[]{:S(2)}) collective-permute-start(bf16[4,2,48,768]{3,2,0,1:T(8,128)(2,1)S(1)} %get-tuple-element.365), channel_id=1, source_target_pairs={{0,8},{8,0},{1,9},{9,1},{2,10},{10,2},{3,11},{11,3},{4,12},{12,4},... | collective-permute-start | bytes 1769480 | tf_op jit(solution)/shard_map/ppermute | solution.py:478
  433.1 30.1 %collective-permute-start.55 = (bf16[4,2,48,768]{3,2,0,1:T(8,128)(2,1)S(1)}, bf16[4,2,48,768]{3,2,0,1:T(8,128)(2,1)S(1)}, u32[]{:S(2)}, u32[]{:S(2)}) collective-permute-start(bf16[4,2,48,768]{3,2,0,1:T(8,128)(2,1)S(1)} %get-tuple-element.366), channel_id=1, source_target_pairs={{0,16},{16,0},{1,17},{17,1},{2,18},{18,2},{3,19},{19,3},{4,20},{20... | collective-permute-start | bytes 1769480 | tf_op jit(solution)/shard_map/ppermute | solution.py:478
  434.1 29.0 %collective-permute-start.56 = (bf16[4,2,48,768]{3,2,0,1:T(8,128)(2,1)S(1)}, bf16[4,2,48,768]{3,2,0,1:T(8,128)(2,1)S(1)}, u32[]{:S(2)}, u32[]{:S(2)}) collective-permute-start(bf16[4,2,48,768]{3,2,0,1:T(8,128)(2,1)S(1)} %get-tuple-element.367), channel_id=1, source_target_pairs={{0,24},{8,16},{16,8},{24,0},{1,25},{9,17},{17,9},{25,1},{2,26},{10... | collective-permute-start | bytes 1769480 | tf_op jit(solution)/shard_map/ppermute | solution.py:498
  (159 other events, 1700.8 us)
Sparse Core Ops, SparseCore 0:
  68.6 107.1 all-gather.4
  346.4 34.9 all-gather.6
  409.2 24.3 all-gather.8
  466.2 30.5 all-gather.10
